TPU v7x, 128 devices: a whole 4x4x4 slice. The times are simulated.
128 devices in a mesh: replica: 16 (over z_lo, y, core), shard: 8 (over z_hi, x).
Axes of the slice: x: 4, y: 4, z: 4 (z_hi: 2, z_lo: 2; z = z_hi * 2 + z_lo), core: 2. Of those that a mesh axis runs over, the one named last changes fastest.
Arguments:
- tokens: bfloat16 [32, 576, 1024], P('replica', 'shard'), may hold values from -6 to 6
- cotangent: bfloat16 [32, 576, 1024], P('replica', 'shard'), may hold values from -6 to 6
- attn_gain: bfloat16 [1024], P('shard'), may hold values from 0.099609375 to 1.8984375
- attn_shift: bfloat16 [1024], P('shard'), may hold values from -1.5 to 1.5
- qkv_weight: bfloat16 [1024, 3072], P('shard'), may hold values from -0.1875 to 0.1875
- query_bias: bfloat16 [1024], P('shard'), may hold values from -2.5 to 2.5
- value_bias: bfloat16 [1024], P('shard'), may hold values from -2.5 to 2.5
- out_weight: bfloat16 [1024, 1024], P('shard'), may hold values from -1.5 to 1.5
- out_bias: bfloat16 [1024], P('shard'), may hold values from -1.5 to 1.5
- mlp_gain: bfloat16 [1024], P('shard'), may hold values from 0.099609375 to 1.8984375
- mlp_shift: bfloat16 [1024], P('shard'), may hold values from -1.5 to 1.5
- up_weight: bfloat16 [1024, 4096], P('shard'), may hold values from -0.1875 to 0.1875
- up_bias: bfloat16 [4096], P('shard'), may hold values from -2.5 to 2.5
- down_weight: bfloat16 [4096, 1024], P('shard'), may hold values from -0.09375 to 0.09375
- down_bias: bfloat16 [1024], P('shard'), may hold values from -1.5 to 1.5
Outputs:
- block_out: bfloat16 [32, 576, 1024], P('replica', 'shard')
- input_grad: bfloat16 [32, 576, 1024], P('replica', 'shard')
- attn_gain_grad: float32 [1024], P('shard')
- attn_shift_grad: float32 [1024], P('shard')
- qkv_weight_grad: float32 [1024, 3072], P('shard')
- query_bias_grad: float32 [1024], P('shard')
- value_bias_grad: float32 [1024], P('shard')
- out_weight_grad: float32 [1024, 1024], P('shard')
- out_bias_grad: float32 [1024], P('shard')
- mlp_gain_grad: float32 [1024], P('shard')
- mlp_shift_grad: float32 [1024], P('shard')
- up_weight_grad: float32 [1024, 4096], P('shard')
- up_bias_grad: float32 [4096], P('shard')
- down_weight_grad: float32 [4096, 1024], P('shard')
- down_bias_grad: float32 [1024], P('shard')
All inputs are finite; a program needn't handle non-finite values.
Results may differ from a plain program's by a relative error of at most 0.024.
Values may be sent and summed in bfloat16 or wider, within the bound.
A program may use at most 192 MiB of HBM per device.

v0:
```python
import math

import jax
import jax.numpy as jnp
from jax import lax
from jax.sharding import Mesh
from jax.sharding import PartitionSpec as P

HEAD_DIM = 64
SHARD = ("shard_0", "shard_1")


epsilon = 1e-06


def gather_turned(arrays, axis, dims):
    turned = [jnp.moveaxis(a, dim, 0) for a, dim in zip(arrays, dims)]
    widths = [t[0].size for t in turned]
    both = jnp.concatenate([t.reshape(-1, w) for t, w in zip(turned, widths)], axis=1)
    whole = lax.all_gather(both, axis, axis=0, tiled=True)
    tiles = jnp.split(whole, [sum(widths[:k]) for k in range(1, len(widths))], axis=1)
    return tuple(
        (
            jnp.moveaxis(b.reshape(-1, *t.shape[1:]), 0, dim)
            for b, t, dim in zip(tiles, turned, dims)
        )
    )


def in_one_piece(arrays, axis, dim, along):
    both = jnp.concatenate(arrays, axis=along)
    whole, at, done = (lax.all_gather(both, axis, axis=dim, tiled=True), 0, [])
    for a in arrays:
        done.append(lax.slice_in_dim(whole, at, at + a.shape[along], axis=along))
        at += a.shape[along]
    return tuple(done)


def side_by_side(arrays, axis, dim, along):
    widths = [math.prod(a.shape[along:]) for a in arrays]
    both = jnp.concatenate(
        [a.reshape(*a.shape[:along], w) for a, w in zip(arrays, widths)], axis=along
    )
    whole = lax.all_gather(both, axis, axis=dim, tiled=True)
    tiles = jnp.split(whole, [sum(widths[:k]) for k in range(1, len(widths))], axis=along)
    return tuple((b.reshape(*whole.shape[:along], *a.shape[along:]) for a, b in zip(arrays, tiles)))


def reduced_to_own(tiles, axes, turns):
    inside = tiles.shape[1:]
    tiles = tiles.reshape(*(lax.axis_size(a) for a in axes), *inside)
    tiles = jnp.moveaxis(tiles, turns, range(len(axes))).reshape(-1, *inside)
    for k in turns:
        tiles = lax.psum_scatter(tiles, axes[k], scatter_dimension=0, tiled=True)
    return tiles[0]


def in_blocks(array, dim, size):
    before, after = (array.shape[:dim], array.shape[dim + 1 :])
    return jnp.moveaxis(array.reshape(*before, size, -1, *after), dim, 0)


def sum_by_axis_2(array, axes, turns, dim):
    size = lax.axis_size(axes)
    return reduced_to_own(in_blocks(array, dim, size), axes, turns)


def sent_together(arrays, axis, dim, along):
    widths = [a.shape[along] for a in arrays]
    both = jnp.concatenate(arrays, axis=along)
    whole = lax.psum_scatter(both, axis, scatter_dimension=dim, tiled=True)
    return tuple(jnp.split(whole, [sum(widths[:k]) for k in range(1, len(widths))], axis=along))


def sum_at_owner(array, axis, dim):
    size = lax.axis_size(axis)
    tiles = lax.all_to_all(in_blocks(array, dim, size), axis, 0, 0, tiled=True)
    return jnp.sum(tiles.astype(jnp.float32), axis=0)


def norm_forward(inputs, norm_gain, norm_shift):
    row_mean = jnp.mean(inputs, -1, keepdims=True)
    centred = inputs - row_mean
    inverse = lax.rsqrt(jnp.mean(centred * centred, -1, keepdims=True) + epsilon)
    normed = centred * inverse
    return (normed * norm_gain + norm_shift, normed, inverse)


def norm_backward(grad_output, normed, inverse, norm_gain):
    grad_normed = grad_output * norm_gain
    inner = jnp.mean(grad_normed * normed, -1, keepdims=True)
    grad_inputs = inverse * (
        grad_normed - jnp.mean(grad_normed, -1, keepdims=True) - normed * inner
    )
    return (grad_inputs, jnp.sum(grad_output * normed, 0), jnp.sum(grad_output, 0))


def gelu_tanh(values):
    return jax.nn.gelu(values, approximate=True)


def contract_last(left_side, right_side):
    return lax.dot_general(
        left_side, right_side, (((1,), (1,)), ((), ())), preferred_element_type=jnp.float32
    )


def contract_first(left_side, right_side):
    return lax.dot_general(
        left_side, right_side, (((0,), (0,)), ((), ())), preferred_element_type=jnp.float32
    )


def column_terms(operand_pairs):
    products = [contract_first(left_side, right_side) for left_side, right_side in operand_pairs]
    return jnp.concatenate(products, 1) if len(products) > 1 else products[0]


def column_sums(values):
    return jnp.sum(values.astype(jnp.float32), 0)


def body(
    tokens,
    cotangent,
    attn_gain,
    attn_shift,
    qkv_weight,
    query_bias,
    value_bias,
    out_weight,
    out_bias,
    mlp_gain,
    mlp_shift,
    up_weight,
    up_bias,
    down_weight,
    down_bias,
):
    images, local_rows, model_width = tokens.shape
    token_rows = images * local_rows
    head_count = model_width // HEAD_DIM
    score_scale = HEAD_DIM ** (-0.5)
    attn_shards = (attn_gain, attn_shift, qkv_weight, query_bias, value_bias, out_weight, out_bias)
    mlp_shards = (mlp_gain, mlp_shift, up_weight, up_bias, down_weight, down_bias)
    attn_full = gather_turned(
        (
            attn_shards[0],
            attn_shards[1],
            attn_shards[2],
            attn_shards[3],
            attn_shards[4],
            attn_shards[5],
            attn_shards[6],
        ),
        SHARD,
        (0, 0, 0, 0, 0, 0, 0),
    )
    inputs = tokens.reshape(token_rows, model_width).astype(jnp.float32)
    first_gain = attn_full[0].astype(jnp.float32)
    first, first_unit, first_inverse = norm_forward(
        inputs, first_gain, attn_full[1].astype(jnp.float32)
    )
    first = first.astype(jnp.bfloat16)
    projected = jnp.dot(first, attn_full[2], preferred_element_type=jnp.float32)
    query = (projected[:, :model_width] + attn_full[3].astype(jnp.float32)).astype(jnp.bfloat16)
    key_own = projected[:, model_width : 2 * model_width].astype(jnp.bfloat16)
    value_own = (projected[:, 2 * model_width :] + attn_full[4].astype(jnp.float32)).astype(
        jnp.bfloat16
    )
    all_keys, all_values = in_one_piece(
        (
            key_own.reshape(images, local_rows, model_width),
            value_own.reshape(images, local_rows, model_width),
        ),
        SHARD,
        1,
        0,
    )
    query_heads = query.reshape(images, local_rows, head_count, HEAD_DIM)
    key_heads = all_keys.reshape(images, -1, head_count, HEAD_DIM)
    value_heads = all_values.reshape(images, -1, head_count, HEAD_DIM)
    scores = (
        jnp.einsum("blhe,bshe->bhls", query_heads, key_heads, preferred_element_type=jnp.float32)
        * score_scale
    )
    row_max = jnp.max(scores, -1, keepdims=True)
    exponentials = jnp.exp(scores - row_max)
    row_total = jnp.sum(exponentials, -1, keepdims=True)
    log_total = row_max + jnp.log(row_total)
    weights_low = (exponentials / row_total).astype(jnp.bfloat16)
    attended = jnp.einsum(
        "bhls,bshe->blhe", weights_low, value_heads, preferred_element_type=jnp.float32
    )
    attended = attended.reshape(token_rows, model_width).astype(jnp.bfloat16)
    branch = jnp.dot(attended, attn_full[5], preferred_element_type=jnp.float32) + attn_full[
        6
    ].astype(jnp.float32)
    resid = inputs + branch
    mlp_full = (
        lax.all_gather(mlp_shards[0], SHARD, axis=0, tiled=True),
        *side_by_side((mlp_shards[1], mlp_shards[2]), SHARD, 0, 1),
        *side_by_side((mlp_shards[3], mlp_shards[4]), SHARD, 0, 1),
        lax.all_gather(mlp_shards[5], SHARD, axis=0, tiled=True),
    )
    second_gain = mlp_full[0].astype(jnp.float32)
    second, second_unit, second_inverse = norm_forward(
        resid, second_gain, mlp_full[1].astype(jnp.float32)
    )
    second = second.astype(jnp.bfloat16)
    upper = jnp.dot(second, mlp_full[2], preferred_element_type=jnp.float32) + mlp_full[3].astype(
        jnp.float32
    )
    active, gelu_pull = jax.vjp(gelu_tanh, upper)
    active_low = active.astype(jnp.bfloat16)
    outcome = jnp.dot(active_low, mlp_full[4], preferred_element_type=jnp.float32) + mlp_full[
        5
    ].astype(jnp.float32)
    block_out = (resid + outcome).astype(jnp.bfloat16).reshape(images, local_rows, model_width)
    grad_low = cotangent.reshape(token_rows, model_width)
    grad_output = grad_low.astype(jnp.float32)
    down_part = sum_by_axis_2(
        column_terms(((active_low, grad_low),)).astype(jnp.bfloat16), SHARD, (1, 0), 0
    ).astype(jnp.float32)
    grad_active = contract_last(grad_low, mlp_full[4])
    grad_upper = gelu_pull(grad_active)[0].astype(jnp.bfloat16)
    up_part = lax.psum_scatter(
        column_terms(((second, grad_upper),)).astype(jnp.bfloat16),
        SHARD,
        scatter_dimension=0,
        tiled=True,
    )
    grad_second = contract_last(grad_upper, mlp_full[2])
    grad_from_second, second_gain_grad, second_shift_grad = norm_backward(
        grad_second, second_unit, second_inverse, mlp_full[0].astype(jnp.float32)
    )
    grad_resid = grad_output + grad_from_second
    grad_branch = grad_resid.astype(jnp.bfloat16)
    grad_attended = contract_last(grad_branch, attn_full[5]).astype(jnp.bfloat16)
    grad_heads = grad_attended.reshape(images, local_rows, head_count, HEAD_DIM)
    scores_again = (
        jnp.einsum("blhe,bshe->bhls", query_heads, key_heads, preferred_element_type=jnp.float32)
        * score_scale
    )
    probs = jnp.exp(scores_again - log_total)
    grad_probs = jnp.einsum(
        "blhe,bshe->bhls", grad_heads, value_heads, preferred_element_type=jnp.float32
    )
    inner = jnp.sum(probs * grad_probs, -1, keepdims=True)
    grad_scores = (probs * (grad_probs - inner)).astype(jnp.bfloat16)
    grad_query = (
        (
            jnp.einsum(
                "bhls,bshe->blhe", grad_scores, key_heads, preferred_element_type=jnp.float32
            )
            * score_scale
        )
        .astype(jnp.bfloat16)
        .reshape(token_rows, model_width)
    )
    key_term = (
        jnp.einsum("bhls,blhe->bshe", grad_scores, query_heads, preferred_element_type=jnp.float32)
        * score_scale
    )
    value_term = jnp.einsum(
        "bhls,blhe->bshe",
        probs.astype(jnp.bfloat16),
        grad_heads,
        preferred_element_type=jnp.float32,
    )
    key_grad, value_grad = tuple(
        (
            part.astype(jnp.float32)
            for part in sent_together(
                (
                    key_term.reshape(images, -1, model_width).astype(jnp.bfloat16),
                    value_term.reshape(images, -1, model_width).astype(jnp.bfloat16),
                ),
                SHARD,
                1,
                0,
            )
        )
    )
    key_grad = key_grad.astype(jnp.bfloat16).reshape(token_rows, model_width)
    value_grad = value_grad.astype(jnp.bfloat16).reshape(token_rows, model_width)
    grad_qkv = jnp.concatenate([grad_query, key_grad, value_grad], 1)
    attn_part = lax.psum_scatter(
        column_terms(((first, grad_qkv), (attended, grad_branch))).astype(jnp.bfloat16),
        SHARD,
        scatter_dimension=0,
        tiled=True,
    )
    grad_first = contract_last(grad_qkv, attn_full[2])
    grad_from_first, first_gain_grad, first_shift_grad = norm_backward(
        grad_first, first_unit, first_inverse, attn_full[0].astype(jnp.float32)
    )
    input_grad = (
        (grad_resid + grad_from_first).astype(jnp.bfloat16).reshape(images, local_rows, model_width)
    )
    vector_parts = (
        sum_at_owner(first_gain_grad.astype(jnp.bfloat16), SHARD, 0),
        sum_at_owner(first_shift_grad.astype(jnp.bfloat16), SHARD, 0),
        sum_at_owner(column_sums(grad_query).astype(jnp.bfloat16), SHARD, 0),
        sum_at_owner(column_sums(value_grad).astype(jnp.bfloat16), SHARD, 0),
        sum_at_owner(column_sums(grad_branch).astype(jnp.bfloat16), SHARD, 0),
        sum_at_owner(second_gain_grad.astype(jnp.bfloat16), SHARD, 0),
        sum_at_owner(second_shift_grad.astype(jnp.bfloat16), SHARD, 0),
        sum_at_owner(column_sums(grad_upper).astype(jnp.bfloat16), SHARD, 0),
        sum_at_owner(column_sums(grad_low).astype(jnp.bfloat16), SHARD, 0),
    )
    summed = (
        lax.psum(vector_parts[0].astype(jnp.bfloat16), "replica").astype(jnp.float32),
        lax.psum(vector_parts[1].astype(jnp.bfloat16), "replica").astype(jnp.float32),
        lax.psum(vector_parts[2].astype(jnp.bfloat16), "replica").astype(jnp.float32),
        lax.psum(vector_parts[3].astype(jnp.bfloat16), "replica").astype(jnp.float32),
        lax.psum(vector_parts[4].astype(jnp.bfloat16), "replica").astype(jnp.float32),
        lax.psum(vector_parts[5].astype(jnp.bfloat16), "replica").astype(jnp.float32),
        lax.psum(vector_parts[6].astype(jnp.bfloat16), "replica").astype(jnp.float32),
        lax.psum(vector_parts[7].astype(jnp.bfloat16), "replica").astype(jnp.float32),
        lax.psum(vector_parts[8].astype(jnp.bfloat16), "replica").astype(jnp.float32),
        lax.psum(attn_part, "replica").astype(jnp.float32),
        lax.psum(up_part, "replica").astype(jnp.float32),
        lax.psum(down_part.astype(jnp.bfloat16), "replica").astype(jnp.float32),
    )
    attn_total = summed[9]
    return (
        block_out,
        input_grad,
        summed[0],
        summed[1],
        attn_total[:, : 3 * model_width],
        summed[2],
        summed[3],
        attn_total[:, 3 * model_width :],
        summed[4],
        summed[5],
        summed[6],
        summed[10],
        summed[7],
        summed[11],
        summed[8],
    )


def solution(mesh):
    torus = Mesh(
        mesh.devices.reshape(mesh.shape["replica"], 2, 4), ("replica", "shard_0", "shard_1")
    )
    return jax.shard_map(
        body,
        mesh=torus,
        in_specs=(
            P("replica", SHARD, None),
            P("replica", SHARD, None),
            P(SHARD),
            P(SHARD),
            P(SHARD, None),
            P(SHARD),
            P(SHARD),
            P(SHARD, None),
            P(SHARD),
            P(SHARD),
            P(SHARD),
            P(SHARD, None),
            P(SHARD),
            P(SHARD, None),
            P(SHARD),
        ),
        out_specs=(
            P("replica", SHARD, None),
            P("replica", SHARD, None),
            P(SHARD),
            P(SHARD),
            P(SHARD, None),
            P(SHARD),
            P(SHARD),
            P(SHARD, None),
            P(SHARD),
            P(SHARD),
            P(SHARD),
            P(SHARD, None),
            P(SHARD),
            P(SHARD, None),
            P(SHARD),
        ),
        check_vma=False,
    )
```

profile of v0, /device:TPU:1, one launch (start us, length us, event | category | flops | bytes accessed | tf_op | source)
XLA Modules:
  0.0 1096.2 jit_solution(14717375816943219890)
XLA Ops:
  11.3 3.5 concatenate.22
  18.9 110.2 %all-gather.7.cloned.1.call-done = bf16[1024,4101]{1,0:T(8,128)(2,1)} async-done(((bf16[128,4101]{1,0:T(8,128)(2,1)}), bf16[1024,4101]{1,0:T(8,128)(2,1)}) %all-gather.7.cloned.1.call-update) | async-done | bytes 8398864 | tf_op jit(solution)/shard_map/all_gather | solution.py:20
  132.1 5.1 fusion.10
  138.3 14.9 %all-gather = bf16[8,1,128]{2,1,0:T(2,128)(2,1)S(1)} all-gather(bf16[1,1,128]{2,1,0:T(2,128)(2,1)S(1)} %bitcast.129), channel_id=1, replica_groups=mesh['replica'=16,'shard_0'=2,'shard_1'=4] {'shard_0','shard_1'}, dimensions={0}, use_global_device_ids=true | all-gather | bytes 2304 | tf_op jit(solution)/shard_map/all_gather | solution.py:201
  153.2 87.9 %all-gather.11.cloned.1.call-done = bf16[1024,4097]{1,0:T(8,128)(2,1)} async-done(((bf16[128,4097]{1,0:T(8,128)(2,1)}), bf16[1024,4097]{1,0:T(8,128)(2,1)}) %all-gather.11.cloned.1.call-update) | async-done | bytes 8390672 | tf_op jit(solution)/shard_map/all_gather | solution.py:44
  242.2 118.1 %all-gather.13.cloned.1.call-done = bf16[4096,1025]{1,0:T(8,128)(2,1)} async-done(((bf16[512,1025]{1,0:T(8,128)(2,1)}), bf16[4096,1025]{1,0:T(8,128)(2,1)}) %all-gather.13.cloned.1.call-update) | async-done | bytes 8396816 | tf_op jit(solution)/shard_map/all_gather | solution.py:44
  363.4 73.2 %all-gather.9.cloned.1.call-done = bf16[4,576,1024]{2,1,0:T(8,128)(2,1)} async-done(((bf16[4,72,1024]{2,1,0:T(8,128)(2,1)}), bf16[4,576,1024]{2,1,0:T(8,128)(2,1)}) %all-gather.9.cloned.1.call-update) | async-done | bytes 4718608 | tf_op jit(solution)/shard_map/all_gather | solution.py:32
  436.7 5.0 fusion.71
  441.7 3.3 copy.96
  445.0 4.9 copy.95
  460.6 6.4 fusion.16
  467.0 5.7 convolution_convert_fusion
  472.8 7.6 copy.116
  480.9 9.8 fusion.74
  490.7 8.2 multiply_reduce_fusion.2
  504.2 5.7 fusion.34
  509.9 4.7 copy.106
  514.6 6.0 multiply_reduce_fusion
  529.2 3.6 copy.119
  532.8 5.2 copy.124
  539.3 5.8 convolution_convert_fusion.1
  545.2 14.0 %reduce-scatter.12.cloned.1.call-done = bf16[2,512,1024]{2,1,0:T(8,128)(2,1)} async-done(((bf16[8,512,1024]{2,1,0:T(8,128)(2,1)}), bf16[2,512,1024]{2,1,0:T(8,128)(2,1)}) %reduce-scatter.12.cloned.1.call-update) | async-done | bytes 2097168 | tf_op jit(solution)/shard_map/reduce_scatter | solution.py:54
  559.3 3.6 fusion.73
  567.4 82.7 %reduce-scatter.16.cloned.1.call-done = bf16[72,4096]{1,0:T(8,128)(2,1)} async-done(((bf16[576,4096]{1,0:T(8,128)(2,1)}), bf16[72,4096]{1,0:T(8,128)(2,1)}) %reduce-scatter.16.cloned.1.call-update) | async-done | bytes 589840
  653.1 5.4 convolution_convert_fusion.2
  658.5 7.1 pad_maximum_fusion
  665.8 102.9 %reduce-scatter.10.cloned.1.call-done = bf16[128,4096]{1,0:T(8,128)(2,1)} async-done(((bf16[1024,4096]{1,0:T(8,128)(2,1)}), bf16[128,4096]{1,0:T(8,128)(2,1)}) %reduce-scatter.10.cloned.1.call-update) | async-done | bytes 1048592 | tf_op jit(solution)/shard_map/reduce_scatter | solution.py:227
  768.7 36.7 %reduce-scatter.14.cloned.1.call-done = bf16[1,512,1024]{2,1,0:T(8,128)(2,1)} async-done(((bf16[2,512,1024]{2,1,0:T(8,128)(2,1)}), bf16[1,512,1024]{2,1,0:T(8,128)(2,1)}) %reduce-scatter.14.cloned.1.call-update) | async-done | bytes 1048592 | tf_op jit(solution)/shard_map/reduce_scatter | solution.py:54
  805.5 117.8 %reduce-scatter.8.cloned.1.call-done = bf16[128,4096]{1,0:T(8,128)(2,1)} async-done(((bf16[1024,4096]{1,0:T(8,128)(2,1)}), bf16[128,4096]{1,0:T(8,128)(2,1)}) %reduce-scatter.8.cloned.1.call-update) | async-done | bytes 1048592 | tf_op jit(solution)/shard_map/reduce_scatter | solution.py:288
  924.0 3.3 all-to-all-start.8
  927.9 5.8 all-to-all-done.8
  933.7 3.3 all-to-all-start.6
  937.6 5.8 all-to-all-done.6
  943.3 3.3 all-to-all-start.4
  947.3 5.8 all-to-all-done.4
  953.0 3.3 all-to-all-start.5
  957.0 5.7 all-to-all-done.5
  962.7 3.3 all-to-all-start.2
  966.0 19.5 %all-gather.1 = bf16[8,1,128]{2,1,0:T(2,128)(2,1)S(1)} all-gather(bf16[1,1,128]{2,1,0:T(2,128)(2,1)S(1)} %bitcast.130), channel_id=1, replica_groups=mesh['replica'=16,'shard_0'=2,'shard_1'=4] {'shard_0','shard_1'}, dimensions={0}, use_global_device_ids=true | all-gather | bytes 2304 | tf_op jit(solution)/shard_map/all_gather | solution.py:204
  987.4 3.6 all-to-all-start.7
  991.1 8.7 fusion.57
  1000.5 6.6 all-to-all-start.3
  1007.2 5.9 multiply_reduce_fusion.8
  1013.7 6.6 all-to-all-start.1
  1020.9 5.8 all-to-all-done.1
  1026.8 3.3 all-to-all-start
  1031.1 5.3 all-to-all-done
  1036.5 40.2 %all-reduce = (bf16[128]{0:T(256)(128)(2,1)S(1)}, bf16[128]{0:T(256)(128)(2,1)S(1)}, bf16[128]{0:T(256)(128)(2,1)S(1)}, bf16[128]{0:T(256)(128)(2,1)S(1)}, bf16[...) all-reduce(bf16[128]{0:T(256)(128)(2,1)S(1)} %reduce_sum.305, ...), channel_id=1, replica_groups=mesh['replica'=16,'shard_0'=2,'shard_1'=4] {'replica'}, use_global_device_ids=true, to_apply=%region_14.0 | all-reduce | flops 1536 | bytes 6144 | tf_op jit(solution)/shard_map/psum | solution.py:313
  (198 shorter events, 70.4 us)
Async XLA Ops:
  7.2 7.7 copy-start.35
  7.2 7.8 copy-start.22
  7.2 121.9 %all-gather.7.cloned.1.call-start = ((), (), s32[]{:S(2)}) async-start(), calls=%async_computation.14 | async-start | bytes 9732096 | tf_op jit(solution)/shard_map/all_gather | solution.py:20
  14.8 226.3 %all-gather.11.cloned.1.call-start = ((), (), s32[]{:S(2)}) async-start(), calls=%async_computation.16 | async-start | bytes 9732096 | tf_op jit(solution)/shard_map/all_gather | solution.py:44
  16.4 343.9 %all-gather.13.cloned.1.call-start = ((), (), s32[]{:S(2)}) async-start(), calls=%async_computation.17 | async-start | bytes 10616832 | tf_op jit(solution)/shard_map/all_gather | solution.py:44
  18.2 418.4 %all-gather.9.cloned.1.call-start = ((), (), s32[]{:S(2)}) async-start(), calls=%async_computation.15 | async-start | bytes 5308416 | tf_op jit(solution)/shard_map/all_gather | solution.py:32
  18.9 118.3 %copy-start.27 = (f32[144]{0:T(256)}, f32[144]{0:T(256)S(1)}, u32[]{:S(2)}) copy-start(f32[144]{0:T(256)S(1)} %rsqrt.20) | copy-start | bytes 1732
  132.0 5.1 copy-start.12
  138.2 421.0 %reduce-scatter.12.cloned.1.call-start = ((), (), s32[]{:S(2)}) async-start(), calls=%async_computation.20 | async-start | bytes 10485760 | tf_op jit(solution)/shard_map/reduce_scatter | solution.py:54
  363.4 86.4 %copy-start.7 = (bf16[2,72,16,64]{1,3,2,0:T(8,128)(2,1)}, bf16[2,72,16,64]{1,3,2,0:T(8,128)(2,1)S(1)}, u32[]{:S(2)}) copy-start(bf16[2,72,16,64]{1,3,2,0:T(8,128)(2,1)S(1)} %copy.97) | copy-start | bytes 884740
  445.0 6.1 copy-start.3
  451.0 2.9 copy-start
  451.1 3.7 copy-start.4
  457.1 3.4 copy-start.26
  457.5 9.5 copy-start.14
  460.6 6.5 copy-start.15
  467.0 5.8 copy-start.38
  480.4 169.8 %reduce-scatter.16.cloned.1.call-start = ((), (), s32[]{:S(2)}) async-start(), calls=%async_computation.22 | async-start | bytes 5308416
  490.7 8.2 copy-start.17
  499.8 4.5 copy-start.25
  509.9 10.7 slice-start
  514.6 6.0 slice-start.1
  538.0 230.7 %reduce-scatter.10.cloned.1.call-start = ((), (), s32[]{:S(2)}) async-start(), calls=%async_computation.19 | async-start | bytes 9437184 | tf_op jit(solution)/shard_map/reduce_scatter | solution.py:227
  545.1 14.2 %copy-start.2 = (bf16[2,16,72,576]{3,2,1,0:T(8,128)(2,1)S(1)}, bf16[2,16,72,576]{3,2,1,0:T(8,128)(2,1)}, u32[]{:S(2)}) copy-start(bf16[2,16,72,576]{3,2,1,0:T(8,128)(2,1)} %copy-done.1) | copy-start | bytes 7962628
  545.1 260.3 %reduce-scatter.14.cloned.1.call-start = ((), (), s32[]{:S(2)}) async-start(), calls=%async_computation.21 | async-start | bytes 3145728 | tf_op jit(solution)/shard_map/reduce_scatter | solution.py:54
  559.2 364.0 %reduce-scatter.8.cloned.1.call-start = ((), (), s32[]{:S(2)}) async-start(), calls=%async_computation.18 | async-start | bytes 9437184 | tf_op jit(solution)/shard_map/reduce_scatter | solution.py:288
  665.7 257.6 %copy-start.16 = (bf16[2,72,1024]{2,1,0:T(8,128)(2,1)S(1)}, bf16[2,72,1024]{2,1,0:T(8,128)(2,1)}, u32[]{:S(2)}) copy-start(bf16[2,72,1024]{2,1,0:T(8,128)(2,1)} %param.16) | copy-start | bytes 884740
  665.7 261.6 %copy-start.33 = (bf16[1024]{0:T(1024)(128)(2,1)S(1)}, bf16[1024]{0:T(1024)(128)(2,1)}, u32[]{:S(2)}) copy-start(bf16[1024]{0:T(1024)(128)(2,1)} %get-tuple-element.26) | copy-start | bytes 6148
  665.7 271.2 %copy-start.29 = (bf16[1024]{0:T(1024)(128)(2,1)S(1)}, bf16[1024]{0:T(1024)(128)(2,1)}, u32[]{:S(2)}) copy-start(bf16[1024]{0:T(1024)(128)(2,1)} %get-tuple-element.40) | copy-start | bytes 6148
  665.7 280.9 %copy-start.32 = (bf16[1024]{0:T(1024)(128)(2,1)S(1)}, bf16[1024]{0:T(1024)(128)(2,1)}, u32[]{:S(2)}) copy-start(bf16[1024]{0:T(1024)(128)(2,1)} %get-tuple-element.20) | copy-start | bytes 6148
  665.8 300.3 %copy-start.37 = (bf16[128]{0:T(256)(128)(2,1)S(1)}, bf16[128]{0:T(256)(128)(2,1)}, u32[]{:S(2)}) copy-start(bf16[128]{0:T(256)(128)(2,1)} %param.29) | copy-start | bytes 772
  665.8 319.8 %copy-start.30 = (bf16[4096]{0:T(1024)(128)(2,1)S(1)}, bf16[4096]{0:T(1024)(128)(2,1)}, u32[]{:S(2)}) copy-start(bf16[4096]{0:T(1024)(128)(2,1)} %get-tuple-element.59) | copy-start | bytes 24580
  665.8 415.6 %all-reduce.4.cloned.1.call-start = ((), (), s32[]{:S(2)}) async-start(), calls=%async_computation.23 | async-start | bytes 6291456 | tf_op jit(solution)/shard_map/psum | solution.py:322
  924.0 9.7 all-to-all-start.8
  933.7 9.7 all-to-all-start.6
  943.3 9.7 all-to-all-start.4
  953.0 9.7 all-to-all-start.5
  962.7 24.7 %all-to-all-start.2 = ((bf16[8,1,128]{2,1,0:T(2,128)(2,1)}), bf16[8,1,128]{2,1,0:T(2,128)(2,1)S(1)}, u32[]{:S(2)}, u32[]{:S(2)}) async-start(bf16[8,1,128]{2,1,0:T(2,128)(2,1)} %all_to_all.60), calls=%async_computation.3 | async-start | bytes 8192 | tf_op jit(solution)/shard_map/all_to_all | solution.py:77
  987.4 12.4 %all-to-all-start.7 = ((bf16[8,2,256]{2,1,0:T(2,128)(2,1)}), bf16[8,2,256]{2,1,0:T(2,128)(2,1)S(1)}, u32[]{:S(2)}, u32[]{:S(2)}) async-start(bf16[8,2,256]{2,1,0:T(2,128)(2,1)} %reshape.354), calls=%async_computation.9 | async-start | bytes 16384 | tf_op jit(solution)/shard_map/all_to_all | solution.py:77
  991.0 16.1 %copy-start.11 = (bf16[2,72,1024]{2,1,0:T(8,128)(2,1)S(1)}, bf16[2,72,1024]{2,1,0:T(8,128)(2,1)}, u32[]{:S(2)}) copy-start(bf16[2,72,1024]{2,1,0:T(8,128)(2,1)} %param.15) | copy-start | bytes 884740
  991.0 16.1 %copy-start.19 = (bf16[144,1024]{1,0:T(8,128)(2,1)S(1)}, bf16[144,1024]{1,0:T(8,128)(2,1)}, u32[]{:S(2)}) copy-start(bf16[144,1024]{1,0:T(8,128)(2,1)} %reshape.325) | copy-start | bytes 884740
  991.0 16.1 %copy-start.28 = (f32[144]{0:T(256)S(1)}, f32[144]{0:T(256)}, u32[]{:S(2)}) copy-start(f32[144]{0:T(256)} %copy-done.27) | copy-start | bytes 1732
  1000.5 13.2 %all-to-all-start.3 = ((bf16[8,1,128]{2,1,0:T(2,128)(2,1)}), bf16[8,1,128]{2,1,0:T(2,128)(2,1)S(1)}, u32[]{:S(2)}, u32[]{:S(2)}) async-start(bf16[8,1,128]{2,1,0:T(2,128)(2,1)} %copy.111), calls=%async_computation.4 | async-start | bytes 8192 | tf_op jit(solution)/shard_map/all_to_all | solution.py:77
  1007.1 23.0 %copy-start.6 = (f32[144,1024]{1,0:T(8,128)S(1)}, f32[144,1024]{1,0:T(8,128)}, u32[]{:S(2)}) copy-start(f32[144,1024]{1,0:T(8,128)} %copy-done.5) | copy-start | bytes 1769476
  1013.7 13.1 %all-to-all-start.1 = ((bf16[8,1,128]{2,1,0:T(2,128)(2,1)}), bf16[8,1,128]{2,1,0:T(2,128)(2,1)S(1)}, u32[]{:S(2)}, u32[]{:S(2)}) async-start(bf16[8,1,128]{2,1,0:T(2,128)(2,1)} %copy.108), calls=%async_computation.1 | async-start | bytes 8192 | tf_op jit(solution)/shard_map/all_to_all | solution.py:77
  1026.8 9.7 all-to-all-start
  1081.4 4.4 copy-start.21
  1083.3 4.1 copy-start.20
  (12 other events, 21.1 us)
Sparse Core Ops, SparseCore 0:
  14.9 114.1 all-gather.6
  132.0 109.0 all-gather.10
  244.0 116.2 all-gather.12
  363.0 73.6 all-gather.8
  480.5 78.6 reduce-scatter.11
  563.0 87.0 reduce-scatter.15
  654.6 114.1 reduce-scatter.9
  771.2 34.2 reduce-scatter.13
  809.3 113.8 reduce-scatter.7
  925.9 124.7 all-reduce.3
where the time goes:
time: 1100 us
  waiting for transfers between devices  778 us (71%)
  matrix products  87.7 us (8%)
  blocking collectives  74.6 us (7%)
  local copies, waits for them, and re-layouts  67.7 us (6%)
  starting transfers between devices  37.7 us (3%)
  other arithmetic  35 us (3%)
  between operations  15.4 us (1%)
    all_gather x2, waiting for transfers between devices, side_by_side(): whole = lax.all_gather(both, axis, axis=dim, tiled=True)  206 us
    reduce_scatter x1, waiting for transfers between devices, body(): lax.psum_scatter(column_terms(((first, grad_qkv), (attended, grad_branch)...  118 us
    all_gather x1, waiting for transfers between devices, gather_turned(): whole = lax.all_gather(both, axis, axis=0, tiled=True)  110 us
    reduce_scatter x1, waiting for transfers between devices, body(): lax.psum_scatter(column_terms(((second, grad_upper),)).astype(jnp.bfloat1...  103 us
    unnamed x11, waiting for transfers between devices  82.9 us
    all_gather x1, waiting for transfers between devices, in_one_piece(): whole, at, done = (lax.all_gather(both, axis, axis=dim, tiled=True), 0, [])  73.2 us
    reduce_scatter x2, waiting for transfers between devices, reduced_to_own(): tiles = lax.psum_scatter(tiles, axes[k], scatter_dimension=0, tiled=True)  50.7 us
    psum x1, blocking collectives, body(): lax.psum(vector_parts[0].astype(jnp.bfloat16), 'replica')  40.2 us
  transfers between devices with their start and end apart: 19, of which 15 were waited for; matrix products, arithmetic and copies ran while one was open for 12% of the time, Pallas kernels for 0%

commit v1 on v0

v1 whole, which is shorter than its diff:
```python
import jax
import jax.numpy as jnp
from jax import lax
from jax.experimental import pallas as pl
from jax.experimental.pallas import tpu as pltpu
from jax.sharding import PartitionSpec as P

HEAD_DIM = 64
EPS = 1e-06
F32 = jnp.float32
BF16 = jnp.bfloat16
SCALE = HEAD_DIM ** (-0.5)


def dot(a, b):
    return lax.dot_general(a, b, (((1,), (0,)), ((), ())), preferred_element_type=F32)


def dot_last(a, b):
    return lax.dot_general(a, b, (((1,), (1,)), ((), ())), preferred_element_type=F32)


def dot_first(a, b):
    return lax.dot_general(a, b, (((0,), (0,)), ((), ())), preferred_element_type=F32)


def norm_unit(v):
    mean = jnp.mean(v, -1, keepdims=True)
    centred = v - mean
    inverse = lax.rsqrt(jnp.mean(centred * centred, -1, keepdims=True) + EPS)
    return centred * inverse, inverse


def norm_back(grad, unit, inverse, gain):
    gn = grad * gain
    inner = jnp.mean(gn * unit, -1, keepdims=True)
    return inverse * (gn - jnp.mean(gn, -1, keepdims=True) - unit * inner)


def head_masks(shape):
    low = lax.broadcasted_iota(jnp.int32, shape, 1) < HEAD_DIM
    return (low, jnp.logical_not(low))


def attend_kernel(qkv_ref, out_ref, lse_ref):
    q, k, v = (qkv_ref[0, :, i * 128 : (i + 1) * 128] for i in range(3))
    zero = jnp.zeros_like(q)
    total = jnp.zeros(q.shape, F32)
    for h, mask in enumerate(head_masks(q.shape)):
        s = dot_last(jnp.where(mask, q, zero), k) * SCALE
        top = jnp.max(s, -1, keepdims=True)
        e = jnp.exp(s - top)
        row = jnp.sum(e, -1, keepdims=True)
        p = (e * (1.0 / row)).astype(BF16)
        total += dot(p, jnp.where(mask, v, zero))
        lse_ref[0, :, h : h + 1] = top + jnp.log(row)
    out_ref[0] = total.astype(BF16)


def attend(qkv):
    images, seq, width = qkv.shape
    return pl.pallas_call(
        attend_kernel,
        grid=(images,),
        in_specs=[pl.BlockSpec((1, seq, width), lambda i: (i, 0, 0))],
        out_specs=[
            pl.BlockSpec((1, seq, 128), lambda i: (i, 0, 0)),
            pl.BlockSpec((1, seq, 2), lambda i: (i, 0, 0)),
        ],
        out_shape=[
            jax.ShapeDtypeStruct((images, seq, 128), BF16),
            jax.ShapeDtypeStruct((images, seq, 2), F32),
        ],
        name="attend",
        compiler_params=pltpu.CompilerParams(vmem_limit_bytes=40 << 20),
    )(qkv)


def attend_back_kernel(qkv_ref, lse_ref, grad_ref, out_ref):
    q, k, v = (qkv_ref[0, :, i * 128 : (i + 1) * 128] for i in range(3))
    grad = grad_ref[0]
    zero = jnp.zeros_like(q)
    dq = jnp.zeros(q.shape, F32)
    dk, dv = dq, dq
    for h, mask in enumerate(head_masks(q.shape)):
        qh, kh, gh = (jnp.where(mask, a, zero) for a in (q, k, grad))
        p = jnp.exp(dot_last(qh, k) * SCALE - lse_ref[0, :, h : h + 1])
        dp = dot_last(gh, v)
        inner = jnp.sum(p * dp, -1, keepdims=True)
        ds = (p * (dp - inner)).astype(BF16)
        dq += dot(ds, kh)
        dk += dot_first(ds, qh)
        dv += dot_first(p.astype(BF16), gh)
    out_ref[0, :, 0:128] = (dq * SCALE).astype(BF16)
    out_ref[0, :, 128:256] = (dk * SCALE).astype(BF16)
    out_ref[0, :, 256:384] = dv.astype(BF16)


def attend_back(qkv, lse, grad):
    images, seq, width = qkv.shape
    return pl.pallas_call(
        attend_back_kernel,
        grid=(images,),
        in_specs=[
            pl.BlockSpec((1, seq, width), lambda i: (i, 0, 0)),
            pl.BlockSpec((1, seq, 2), lambda i: (i, 0, 0)),
            pl.BlockSpec((1, seq, 128), lambda i: (i, 0, 0)),
        ],
        out_specs=pl.BlockSpec((1, seq, width), lambda i: (i, 0, 0)),
        out_shape=jax.ShapeDtypeStruct((images, seq, width), BF16),
        name="attend_back",
        compiler_params=pltpu.CompilerParams(vmem_limit_bytes=40 << 20),
    )(qkv, lse, grad)


def gather(a):
    return lax.all_gather(a, "shard", axis=0, tiled=True)


def scatter(a):
    return lax.psum_scatter(a.astype(BF16), "shard", scatter_dimension=0, tiled=True).astype(F32)


def turn(a):
    return lax.all_to_all(a, "shard", 0, 0, tiled=True)


def by_image(a):
    return a.reshape(8, 2, 72, a.shape[-1]).swapaxes(0, 1).reshape(2, 576, a.shape[-1])


def by_device(a):
    return a.reshape(2, 8, 72, a.shape[-1]).swapaxes(0, 1).reshape(1152, a.shape[-1])


def body(
    tokens,
    cotangent,
    attn_gain,
    attn_shift,
    qkv_weight,
    query_bias,
    value_bias,
    out_weight,
    out_bias,
    mlp_gain,
    mlp_shift,
    up_weight,
    up_bias,
    down_weight,
    down_bias,
):
    D = 1024
    shard = lax.axis_index("shard")
    columns = jnp.concatenate(
        [qkv_weight.reshape(128, 3, 8, 128), up_weight.reshape(128, 8, 4, 128).swapaxes(1, 2)], 1
    )
    columns = columns.transpose(2, 0, 1, 3).reshape(8, 128, 896)
    vectors = jnp.stack([attn_gain, attn_shift, mlp_gain, mlp_shift, out_bias, down_bias])
    vectors = jnp.broadcast_to(jnp.pad(vectors, ((0, 10), (0, 768))), (8, 16, 896))
    turned = turn(jnp.concatenate([columns, vectors], 1))
    weights = turned[:, :128].reshape(D, 896)
    qkv_columns, up_columns = weights[:, :384], weights[:, 384:]
    vectors = turned[:, 128:134, :128].swapaxes(0, 1).reshape(6, D).astype(F32)
    gain1, shift1, gain2, shift2, bias_out, bias_down = vectors

    x = tokens.reshape(144, D).astype(F32)
    unit1, inverse1 = norm_unit(x)
    first = gather((unit1 * gain1 + shift1).astype(BF16))
    grad_all = gather(cotangent.reshape(144, D))
    zeros = jnp.zeros((128,), F32)
    qkv_bias = jnp.concatenate([query_bias.astype(F32), zeros, value_bias.astype(F32)])
    qkv = by_image((dot(first, qkv_columns) + qkv_bias).astype(BF16))
    attended, lse = attend(qkv)
    attended = by_device(attended)
    resid = x + (scatter(dot(attended, out_weight)) + bias_out)
    unit2, inverse2 = norm_unit(resid)
    second = gather((unit2 * gain2 + shift2).astype(BF16))
    upper = dot(second, up_columns) + up_bias.astype(F32)
    active, gelu_pull = jax.vjp(lambda u: jax.nn.gelu(u, approximate=True), upper)
    active = active.astype(BF16)
    outcome = scatter(dot(active, down_weight)) + bias_down
    block_out = (resid + outcome).astype(BF16).reshape(2, 72, D)

    down_grad = dot_first(active, grad_all)
    grad_upper32 = gelu_pull(dot_last(grad_all, down_weight))[0]
    grad_upper = grad_upper32.astype(BF16)
    up_grad = dot_first(second, grad_upper)
    up_bias_grad = jnp.sum(grad_upper.astype(F32), 0)
    grad_second = scatter(dot_last(grad_upper, up_columns))
    grad_resid = cotangent.reshape(144, D).astype(F32) + norm_back(
        grad_second, unit2, inverse2, gain2
    )
    gain2_grad = jnp.sum(grad_second * unit2, 0)
    shift2_grad = jnp.sum(grad_second, 0)
    branch_all = gather(grad_resid.astype(BF16))
    out_grad = dot_first(attended, branch_all)
    grad_attended = dot_last(branch_all, out_weight).astype(BF16)
    grad_qkv = by_device(attend_back(qkv, lse, by_image(grad_attended)))
    qkv_grad = dot_first(first, grad_qkv)
    qkv_bias_grad = jnp.sum(grad_qkv.astype(F32), 0)
    grad_first = scatter(dot_last(grad_qkv, qkv_columns))
    input_grad = (grad_resid + norm_back(grad_first, unit1, inverse1, gain1)).astype(BF16)
    input_grad = input_grad.reshape(2, 72, D)
    gain1_grad = jnp.sum(grad_first * unit1, 0)
    shift1_grad = jnp.sum(grad_first, 0)

    own = lambda a: lax.dynamic_slice_in_dim(a, shard * 128, 128, axis=1)
    out_bias_grad = jnp.sum(own(branch_all).astype(F32), 0)
    down_bias_grad = jnp.sum(own(grad_all).astype(F32), 0)

    up_turned = turn(up_grad.astype(BF16).reshape(8, 128, 512))
    early = jnp.concatenate([down_grad.astype(BF16), up_turned.reshape(512, D)], 0)
    early = lax.psum(early, "replica").astype(F32)
    four = jnp.stack([gain1_grad, shift1_grad, gain2_grad, shift2_grad]).reshape(4, 8, 128)
    four = jnp.pad(four.swapaxes(0, 1), ((0, 0), (0, 12), (0, 256)))
    late = turn(jnp.concatenate([qkv_grad.reshape(8, 128, 384), four], 1).astype(BF16))
    four = jnp.sum(late[:, 128:132, :128].astype(F32), 0).reshape(512)
    small = jnp.concatenate(
        [four, qkv_bias_grad[:128], qkv_bias_grad[256:], out_bias_grad, down_bias_grad]
    )
    small = jnp.pad(jnp.stack([small, jnp.pad(up_bias_grad, (0, 512))]), ((0, 14), (0, 0)))
    late = jnp.concatenate(
        [out_grad.astype(BF16), late[:, :128].reshape(384, D), small.astype(BF16)], 0
    )
    late = lax.psum(late, "replica").astype(F32)
    out_weight_grad = late[:128]
    qkv_weight_grad = late[128:512].reshape(8, 128, 3, 128)
    qkv_weight_grad = qkv_weight_grad.transpose(1, 2, 0, 3).reshape(128, 3 * D)
    small = late[512].reshape(8, 128)
    down_weight_grad = early[:512]
    up_weight_grad = early[512:].reshape(8, 128, 512).swapaxes(0, 1).reshape(128, 4096)
    return (
        block_out,
        input_grad,
        small[0],
        small[1],
        qkv_weight_grad,
        small[4],
        small[5],
        out_weight_grad,
        small[6],
        small[2],
        small[3],
        up_weight_grad,
        late[513, :512],
        down_weight_grad,
        small[7],
    )


def solution(mesh):
    row, cube, flat = P("shard"), P("replica", "shard", None), P("shard", None)
    return jax.shard_map(
        body,
        mesh=mesh,
        in_specs=(cube, cube, row, row, flat, row, row, flat, row, row, row, flat, row, flat, row),
        out_specs=(cube, cube, row, row, flat, row, row, flat, row, row, row, flat, row, flat, row),
        check_vma=False,
    )
```

time: 1100 us -> 821 us (0.75)
  waiting for transfers between devices: 778 us -> 670 us
  blocking collectives: 74.6 us -> 0 us
  matrix products: 87.7 us -> 45.4 us
  local copies, waits for them, and re-layouts: 67.7 us -> 42.1 us
  starting transfers between devices: 37.7 us -> 17.1 us
  other arithmetic: 35 us -> 22.7 us
    all_gather x4, waiting for transfers between devices: 389 us -> 221 us  [gather(): return lax.all_gather(a, 'shard', axis=0, tiled=True)]
    psum x1, waiting for transfers between devices: 0.01 us -> 124 us  [body(): early = lax.psum(early, 'replica').astype(F32)]
    unnamed x11 -> x9, waiting for transfers between devices: 82.9 us -> 0.81 us
    dot_general x18 -> x12, matrix products: 87.7 us -> 45.4 us  [the longest x4 17.3 us: dot(): lax.dot_general(a, b, (((1,), (0,)), ((), ())), preferred_element_type=F32)]
    psum x1 -> x0, blocking collectives: 40.2 us -> none  [body(): lax.psum(vector_parts[0].astype(jnp.bfloat16), 'replica')]
    all_gather x2 -> x0, blocking collectives: 34.4 us -> none  [the longest x1 19.5 us: body(): lax.all_gather(mlp_shards[5], SHARD, axis=0, tiled=True)]
    reduce_scatter x4, waiting for transfers between devices: 271 us -> 293 us  [scatter(): lax.psum_scatter(a.astype(BF16), 'shard', scatter_dimension=0, tiled=True)]
    all_to_all x9 -> x3, starting transfers between devices: 36.7 us -> 16.1 us  [turn(): return lax.all_to_all(a, 'shard', 0, 0, tiled=True)]
  transfers between devices with their start and end apart: 19 -> 12, of which waited for: 15 -> 11; matrix products, arithmetic and copies ran while one was open for 12% -> 5% of each run, Pallas kernels for 0% -> 0%
where the time goes in v1:
time: 821 us; the launch traced here: 820 us
  waiting for transfers between devices  670 us (82%)
  matrix products  45.4 us (6%)
  local copies, waits for them, and re-layouts  42.1 us (5%)
  other arithmetic  22.7 us (3%)
  starting transfers between devices  17.1 us (2%)
  between operations  14.3 us (2%)
  Pallas kernels  8.41 us (1%)
    reduce_scatter x4, waiting for transfers between devices, scatter(): lax.psum_scatter(a.astype(BF16), 'shard', scatter_dimension=0, tiled=True)  293 us
    all_gather x4, waiting for transfers between devices, gather(): return lax.all_gather(a, 'shard', axis=0, tiled=True)  221 us
    psum x1, waiting for transfers between devices, body(): early = lax.psum(early, 'replica').astype(F32)  124 us
    all_to_all x3, waiting for transfers between devices, turn(): return lax.all_to_all(a, 'shard', 0, 0, tiled=True)  31.6 us
    dot_general x4, matrix products, dot(): lax.dot_general(a, b, (((1,), (0,)), ((), ())), preferred_element_type=F32)  17.3 us
  transfers between devices with their start and end apart: 12, of which 11 were waited for; matrix products, arithmetic and copies ran while one was open for 5% of the time, Pallas kernels for 0%

profile of v1, /device:TPU:1, one launch (start us, length us, event | category | flops | bytes accessed | tf_op | source)
XLA Modules:
  0.0 820.0 jit_solution(11849345716500720904)
XLA Ops:
  8.2 1.5 copy.67
  9.7 1.6 copy.68
  11.7 2.6 pad_maximum_fusion
  14.3 4.6 copy.71
  18.9 8.3 %all-to-all-start = ((bf16[8,144,896]{2,1,0:T(8,128)(2,1)}), bf16[8,144,896]{2,1,0:T(8,128)(2,1)S(1)}, u32[]{:S(2)}, u32[]{:S(2)}) async-start(bf16[8,144,896]{2,1,0:T(8,128)(2,1)} %copy.71), calls=%async_computation | async-start | bytes 4128768 | tf_op jit(solution)/shard_map/all_to_all | solution.py:125
  27.8 27.6 %all-to-all-done = bf16[8,144,896]{2,1,0:T(8,128)(2,1)S(1)} async-done(((bf16[8,144,896]{2,1,0:T(8,128)(2,1)}), bf16[8,144,896]{2,1,0:T(8,128)(2,1)S(1)}, u32[]{:S(2)}, u32[]{:S(2)}) %all-to-all-start) | async-done | bytes 2064416 | tf_op jit(solution)/shard_map/all_to_all | solution.py:125
  56.5 1.5 slice.110
  58.0 55.0 %all-gather.5.cloned.1.call-done = bf16[1152,1024]{1,0:T(8,128)(2,1)} async-done(((bf16[144,1024]{1,0:T(8,128)(2,1)}), bf16[1152,1024]{1,0:T(8,128)(2,1)}) %all-gather.5.cloned.1.call-update) | async-done | bytes 2359312 | tf_op jit(solution)/shard_map/all_gather | solution.py:117
  113.1 3.2 fusion
  116.4 3.3 attend.1
  119.8 2.2 convolution_convert_fusion.3
  122.8 74.9 %reduce-scatter.5.cloned.1.call-done = bf16[144,1024]{1,0:T(8,128)(2,1)} async-done(((bf16[1152,1024]{1,0:T(8,128)(2,1)}), bf16[144,1024]{1,0:T(8,128)(2,1)}) %reduce-scatter.5.cloned.1.call-update) | async-done | bytes 294928 | tf_op jit(solution)/shard_map/reduce_scatter | solution.py:121
  200.4 55.7 %all-gather.9.cloned.1.call-done = bf16[1152,1024]{1,0:T(8,128)(2,1)} async-done(((bf16[144,1024]{1,0:T(8,128)(2,1)}), bf16[1152,1024]{1,0:T(8,128)(2,1)}) %all-gather.9.cloned.1.call-update) | async-done | bytes 2359312 | tf_op jit(solution)/shard_map/all_gather | solution.py:117
  256.1 4.6 fusion.40
  260.7 53.9 %all-gather.7.cloned.1.call-done = bf16[1152,1024]{1,0:T(8,128)(2,1)} async-done(((bf16[144,1024]{1,0:T(8,128)(2,1)}), bf16[1152,1024]{1,0:T(8,128)(2,1)}) %all-gather.7.cloned.1.call-update) | async-done | bytes 2359312 | tf_op jit(solution)/shard_map/all_gather | solution.py:117
  314.6 7.2 fusion.34
  322.9 2.9 convolution_convert_fusion.1
  325.9 4.7 convolution_convert_fusion.2
  330.6 71.0 %reduce-scatter.9.cloned.1.call-done = bf16[144,1024]{1,0:T(8,128)(2,1)} async-done(((bf16[1152,1024]{1,0:T(8,128)(2,1)}), bf16[144,1024]{1,0:T(8,128)(2,1)}) %reduce-scatter.9.cloned.1.call-update) | async-done | bytes 294928 | tf_op jit(solution)/shard_map/reduce_scatter | solution.py:121
  401.6 1.4 fusion.24
  402.9 78.1 %reduce-scatter.7.cloned.1.call-done = bf16[144,1024]{1,0:T(8,128)(2,1)} async-done(((bf16[1152,1024]{1,0:T(8,128)(2,1)}), bf16[144,1024]{1,0:T(8,128)(2,1)}) %reduce-scatter.7.cloned.1.call-update) | async-done | bytes 294928 | tf_op jit(solution)/shard_map/reduce_scatter | solution.py:121
  481.0 2.4 fusion.36
  483.7 56.2 %all-gather.11.cloned.1.call-done = bf16[1152,1024]{1,0:T(8,128)(2,1)} async-done(((bf16[144,1024]{1,0:T(8,128)(2,1)}), bf16[1152,1024]{1,0:T(8,128)(2,1)}) %all-gather.11.cloned.1.call-update) | async-done | bytes 2359312 | tf_op jit(solution)/shard_map/all_gather | solution.py:117
  539.9 2.4 convolution_convert_fusion.4
  542.4 5.1 attend_back.1
  548.5 4.0 convolution_convert_fusion
  552.6 4.2 convolution_convert_fusion.5
  556.8 3.6 all-to-all-start.2
  561.5 4.4 copy.85
  566.0 3.3 convolution_convert_fusion.7
  569.3 69.1 %reduce-scatter.11.cloned.1.call-done = bf16[144,1024]{1,0:T(8,128)(2,1)} async-done(((bf16[1152,1024]{1,0:T(8,128)(2,1)}), bf16[144,1024]{1,0:T(8,128)(2,1)}) %reduce-scatter.11.cloned.1.call-update) | async-done | bytes 294928 | tf_op jit(solution)/shard_map/reduce_scatter | solution.py:121
  639.5 1.4 fusion.14
  641.9 4.2 all-to-all-start.1
  646.5 5.0 convolution_convert_fusion.6
  652.7 3.2 pad_maximum_fusion.1
  656.3 1.5 convolution_convert_fusion.8
  657.8 4.0 all-to-all-done.1
  668.2 123.5 %all-reduce.7.cloned.1.call-done = (bf16[1024,1024]{1,0:T(8,128)(2,1)}, bf16[528,1024]{1,0:T(8,128)(2,1)}) async-done(((bf16[1024,1024]{1,0:T(8,128)(2,1)}, bf16[528,1024]{1,0:T(8,128)(2,1)}), (bf16[1024,1024]{1,0:T(8,128)(2,1)}, bf16[528,1024]{1,0:T(8,128)(2,1)})) %all-reduce.7.cloned.1.call-update) | async-done | bytes 3178512 | tf_op jit(solution)/shard_map/psum | solution.py:214
  791.8 1.4 slice.125
  793.2 1.8 slice.120
  794.9 2.5 slice.117
  797.4 1.6 convert_element_type.153
  799.0 2.6 reshape.228
  801.6 1.6 copy.82
  803.1 3.2 copy.84
  807.6 2.5 fusion.38
  810.1 1.8 reshape.232
  811.9 1.6 copy.88
  (123 shorter events, 21.9 us)
Async XLA Ops:
  7.2 248.9 %copy-start = (bf16[512,1024]{1,0:T(8,128)(2,1)S(1)}, bf16[512,1024]{1,0:T(8,128)(2,1)}, u32[]{:S(2)}) copy-start(bf16[512,1024]{1,0:T(8,128)(2,1)} %param.28) | copy-start | bytes 3145732
  18.9 8.4 %copy-start.3 = (bf16[2,72,1024]{2,1,0:T(8,128)(2,1)S(1)}, bf16[2,72,1024]{2,1,0:T(8,128)(2,1)}, u32[]{:S(2)}) copy-start(bf16[2,72,1024]{2,1,0:T(8,128)(2,1)} %param.15) | copy-start | bytes 884740
  18.9 37.6 %copy-start.17 = (bf16[128]{0:T(256)(128)(2,1)S(1)}, bf16[128]{0:T(256)(128)(2,1)}, u32[]{:S(2)}) copy-start(bf16[128]{0:T(256)(128)(2,1)} %param.20) | copy-start | bytes 772
  18.9 37.6 %copy-start.18 = (bf16[128]{0:T(256)(128)(2,1)S(1)}, bf16[128]{0:T(256)(128)(2,1)}, u32[]{:S(2)}) copy-start(bf16[128]{0:T(256)(128)(2,1)} %param.21) | copy-start | bytes 772
  18.9 36.5 %all-to-all-start = ((bf16[8,144,896]{2,1,0:T(8,128)(2,1)}), bf16[8,144,896]{2,1,0:T(8,128)(2,1)S(1)}, u32[]{:S(2)}, u32[]{:S(2)}) async-start(bf16[8,144,896]{2,1,0:T(8,128)(2,1)} %copy.71), calls=%async_computation | async-start | bytes 4128768 | tf_op jit(solution)/shard_map/all_to_all | solution.py:125
  27.2 85.9 %all-gather.5.cloned.1.call-start = ((), (), s32[]{:S(2)}) async-start(), calls=%async_computation.7 | async-start | bytes 2654208 | tf_op jit(solution)/shard_map/all_gather | solution.py:117
  56.4 141.4 %reduce-scatter.5.cloned.1.call-start = ((), (), s32[]{:S(2)}) async-start(), calls=%async_computation.8 | async-start | bytes 2654208 | tf_op jit(solution)/shard_map/reduce_scatter | solution.py:121
  116.3 3.5 copy-start.13
  119.8 2.3 copy-start.9
  122.0 78.3 %copy-start.16 = (bf16[512]{0:T(512)(128)(2,1)S(1)}, bf16[512]{0:T(512)(128)(2,1)}, u32[]{:S(2)}) copy-start(bf16[512]{0:T(512)(128)(2,1)} %param.27) | copy-start | bytes 3076
  122.0 134.1 %all-gather.9.cloned.1.call-start = ((), (), s32[]{:S(2)}) async-start(), calls=%async_computation.11 | async-start | bytes 2654208 | tf_op jit(solution)/shard_map/all_gather | solution.py:117
  122.8 191.9 %all-gather.7.cloned.1.call-start = ((), (), s32[]{:S(2)}) async-start(), calls=%async_computation.9 | async-start | bytes 2654208 | tf_op jit(solution)/shard_map/all_gather | solution.py:117
  200.1 201.5 %reduce-scatter.9.cloned.1.call-start = ((), (), s32[]{:S(2)}) async-start(), calls=%async_computation.12 | async-start | bytes 2654208 | tf_op jit(solution)/shard_map/reduce_scatter | solution.py:121
  314.6 8.3 %copy-start.11 = (bf16[8,128,896]{2,1,0:T(8,128)(2,1)S(1)}, bf16[8,128,896]{2,1,0:T(8,128)(2,1)}, u32[]{:S(2)}) copy-start(bf16[8,128,896]{2,1,0:T(8,128)(2,1)} %slice.110) | copy-start | bytes 5505028
  321.9 1.0 copy-start.19
  325.8 155.2 %reduce-scatter.7.cloned.1.call-start = ((), (), s32[]{:S(2)}) async-start(), calls=%async_computation.10 | async-start | bytes 2654208 | tf_op jit(solution)/shard_map/reduce_scatter | solution.py:121
  330.5 150.5 %copy-start.12 = (bf16[2,72,1024]{2,1,0:T(8,128)(2,1)S(1)}, bf16[2,72,1024]{2,1,0:T(8,128)(2,1)}, u32[]{:S(2)}) copy-start(bf16[2,72,1024]{2,1,0:T(8,128)(2,1)} %param.16) | copy-start | bytes 884740
  330.5 209.4 %copy-start.14 = (bf16[128,1024]{1,0:T(8,128)(2,1)S(1)}, bf16[128,1024]{1,0:T(8,128)(2,1)}, u32[]{:S(2)}) copy-start(bf16[128,1024]{1,0:T(8,128)(2,1)} %param.22) | copy-start | bytes 786436
  330.6 209.4 %all-gather.11.cloned.1.call-start = ((), (), s32[]{:S(2)}) async-start(), calls=%async_computation.13 | async-start | bytes 2654208 | tf_op jit(solution)/shard_map/all_gather | solution.py:117
  483.5 155.0 %reduce-scatter.11.cloned.1.call-start = ((), (), s32[]{:S(2)}) async-start(), calls=%async_computation.14 | async-start | bytes 2654208 | tf_op jit(solution)/shard_map/reduce_scatter | solution.py:121
  547.6 0.9 copy-start.15
  548.5 4.1 copy-start.20
  556.8 85.1 %all-to-all-start.2 = ((bf16[8,128,512]{2,1,0:T(8,128)(2,1)}), bf16[8,128,512]{2,1,0:T(8,128)(2,1)S(1)}, u32[]{:S(2)}, u32[]{:S(2)}) async-start(bf16[8,128,512]{2,1,0:T(8,128)(2,1)} %bitcast.134), calls=%async_computation.6 | async-start | bytes 2097152 | tf_op jit(solution)/shard_map/all_to_all | solution.py:125
  561.5 4.4 copy-start.8
  641.9 19.8 %all-to-all-start.1 = ((bf16[8,144,384]{2,1,0:T(8,128)(2,1)}), bf16[8,144,384]{2,1,0:T(8,128)(2,1)}, u32[]{:S(2)}, u32[]{:S(2)}) async-start(bf16[8,144,384]{2,1,0:T(8,128)(2,1)} %fusion.11), calls=%async_computation.5 | async-start | bytes 1769472 | tf_op jit(solution)/shard_map/all_to_all | solution.py:125
  646.2 145.6 %all-reduce.7.cloned.1.call-start = ((), (), s32[]{:S(2)}) async-start(), calls=%async_computation.15 | async-start | bytes 6356992 | tf_op jit(solution)/shard_map/psum | solution.py:214
  652.7 3.4 copy-start.2
  665.6 1.1 copy-start.4
  665.6 1.2 copy-start.7
  665.6 1.6 copy-start.10
  791.8 5.6 copy-start.5
  803.1 4.4 copy-start.6
  810.1 3.4 copy-start.1
Sparse Core Ops, SparseCore 0:
  56.5 56.4 all-gather.4
  122.1 75.5 reduce-scatter.4
  200.4 55.6 all-gather.8
  259.1 55.4 all-gather.6
  325.9 75.5 reduce-scatter.8
  405.2 75.7 reduce-scatter.6
  484.2 55.6 all-gather.10
  552.7 85.6 reduce-scatter.10
  666.9 124.8 all-reduce.6

commit v2 on v1

v2 whole, which is shorter than its diff:
```python
import jax
import jax.numpy as jnp
from jax import lax
from jax.experimental import pallas as pl
from jax.experimental.pallas import tpu as pltpu
from jax.sharding import PartitionSpec as P

HEAD_DIM = 64
EPS = 1e-06
F32 = jnp.float32
BF16 = jnp.bfloat16
SCALE = HEAD_DIM ** (-0.5)
MESH = pl.DeviceIdType.MESH
D = 1024
ROWS = 144
HALF = 512
GELU = 0.7978845608028654


def dot(a, b):
    return lax.dot_general(a, b, (((1,), (0,)), ((), ())), preferred_element_type=F32)


def dot_last(a, b):
    return lax.dot_general(a, b, (((1,), (1,)), ((), ())), preferred_element_type=F32)


def dot_first(a, b):
    return lax.dot_general(a, b, (((0,), (0,)), ((), ())), preferred_element_type=F32)


def norm_unit(v):
    mean = jnp.mean(v, -1, keepdims=True)
    centred = v - mean
    inverse = lax.rsqrt(jnp.mean(centred * centred, -1, keepdims=True) + EPS)
    return centred * inverse, inverse


def norm_back(grad, unit, inverse, gain):
    gn = grad * gain
    inner = jnp.mean(gn * unit, -1, keepdims=True)
    return inverse * (gn - jnp.mean(gn, -1, keepdims=True) - unit * inner)


def head_masks(shape):
    low = lax.broadcasted_iota(jnp.int32, shape, 1) < HEAD_DIM
    return (low, jnp.logical_not(low))


def add(*terms):
    total = terms[0].astype(F32)
    for term in terms[1:]:
        total = total + term.astype(F32)
    return total


class Net:
    def __init__(self, send, recv):
        self.send, self.recv, self.count, self.open = send, recv, 0, []
        self.s = lax.axis_index("shard")
        self.h, self.x = self.s // 4, lax.rem(self.s, 4)
        r = lax.axis_index("replica")
        self.core, self.y = lax.rem(r, 2), lax.rem(r // 2, 4)
        zlow = r // 8
        base = r - self.y * 2
        self.right = {"shard": self.at(self.h, self.x + 1)}
        self.left = {"shard": self.at(self.h, self.x + 3)}
        self.across = {"shard": self.at(1 - self.h, self.x)}
        self.twin = {"replica": r + 1 - 2 * self.core}
        self.up = {"replica": base + lax.rem(self.y + 1, 4) * 2}
        self.down = {"replica": base + lax.rem(self.y + 3, 4) * 2}
        self.beside = {"replica": r + 8 - 16 * zlow}
        self.peers = [{"shard": lax.rem(self.s + k, 8)} for k in range(1, 8)]

    def at(self, h, x):
        return h * 4 + lax.rem(x, 4)

    def copy(self, src, dst, to):
        i = self.count
        self.count += 1
        made = pltpu.make_async_remote_copy(
            src_ref=src,
            dst_ref=dst,
            send_sem=self.send.at[i],
            recv_sem=self.recv.at[i],
            device_id=to,
            device_id_type=MESH,
        )
        made.start()
        self.open.append(made)
        return made

    def drain(self):
        for made in self.open:
            made.wait_send()
        self.open = []

    def barrier(self, others):
        semaphore = pltpu.get_barrier_semaphore()
        for other in others:
            pl.semaphore_signal(semaphore, inc=1, device_id=other, device_id_type=MESH)
        pl.semaphore_wait(semaphore, len(others))


class Gather:
    def __init__(self, net, whole):
        self.net, self.whole = net, whole
        own = whole.at[net.s]
        self.z = net.copy(own, own, net.across)
        self.a = net.copy(own, own, net.right)
        self.b = net.copy(own, own, net.left)

    def piece(self, block, first, to):
        part = self.whole.at[block, :, pl.ds(0 if first else HALF, HALF)]
        return self.net.copy(part, part, to)

    def relay_one(self):
        net = self.net
        self.z.wait_recv()
        part = self.whole.at[net.at(1 - net.h, net.x)]
        self.za = net.copy(part, part, net.right)
        self.zb = net.copy(part, part, net.left)
        self.a.wait_recv()
        self.c = self.piece(net.at(net.h, net.x + 3), True, net.right)
        self.b.wait_recv()
        self.d = self.piece(net.at(net.h, net.x + 1), False, net.left)

    def relay_two(self):
        net = self.net
        self.za.wait_recv()
        self.e = self.piece(net.at(1 - net.h, net.x + 3), True, net.right)
        self.zb.wait_recv()
        self.f = self.piece(net.at(1 - net.h, net.x + 1), False, net.left)

    def finish(self):
        for made in (self.c, self.d, self.e, self.f):
            made.wait_recv()


class Scatter:
    def __init__(self, net, part, far, near, passed, kept, came):
        self.net, self.part = net, part
        self.far, self.near, self.passed, self.kept, self.came = far, near, passed, kept, came
        self.rows = (1 - net.h, net.h)
        halves = (pl.ds(0, HALF), pl.ds(HALF, HALF))
        self.first, self.second = halves
        self.fars, self.nears, self.passes = [], [], [None, None]
        for j, h in enumerate(self.rows):
            block = net.at(h, net.x + 2)
            self.fars.append(
                (
                    net.copy(part.at[block, :, self.first], far.at[0, j], net.right),
                    net.copy(part.at[block, :, self.second], far.at[1, j], net.left),
                )
            )
        for j, h in enumerate(self.rows):
            r, l = net.at(h, net.x + 1), net.at(h, net.x + 3)
            self.nears.append(
                (
                    net.copy(part.at[r, :, self.second], near.at[0, j], net.right),
                    net.copy(part.at[l, :, self.first], near.at[1, j], net.left),
                )
            )

    def relay(self, j):
        net, part, far, passed = self.net, self.part, self.far, self.passed
        h = self.rows[j]
        made = []
        steps = ((0, net.at(h, net.x + 1), self.first, net.right),)
        steps += ((1, net.at(h, net.x + 3), self.second, net.left),)
        for k, block, half, to in steps:
            self.fars[j][k].wait_recv()
            far[k, j] = add(far[k, j], part[block, :, half]).astype(BF16)
            made.append(net.copy(far.at[k, j], passed.at[k, j], to))
        self.passes[j] = made

    def halves(self, j):
        for made in (*self.nears[j], *self.passes[j]):
            made.wait_recv()
        own = self.net.at(self.rows[j], self.net.x)
        part, near, passed = self.part, self.near, self.passed
        return (
            add(part[own, :, self.first], passed[0, j], near[1, j]),
            add(part[own, :, self.second], passed[1, j], near[0, j]),
        )

    def over(self):
        one, two = self.halves(0)
        self.kept[:, 0:HALF] = one.astype(BF16)
        self.kept[:, HALF:D] = two.astype(BF16)
        self.z = self.net.copy(self.kept, self.came, self.net.across)

    def finish(self):
        one, two = self.halves(1)
        self.z.wait_recv()
        return jnp.concatenate(
            [add(one, self.came[:, 0:HALF]), add(two, self.came[:, HALF:D])], axis=1
        )


def layer_kernel(
    tokens,
    cotangent,
    vectors,
    qkv_weight,
    up_weight,
    out_weight,
    down_weight,
    qkv_bias,
    up_bias,
    block_out,
    input_grad,
    rows_grad,
    columns_grad,
    small_grad,
    all_vectors,
    columns,
    first,
    cot,
    second,
    branch,
    mixed,
    qkv_low,
    heads,
    lse,
    attended,
    active,
    grad_upper,
    grad_qkv,
    resid_ref,
    grad_resid_ref,
    small,
    fours,
    fours_in,
    parts,
    far,
    near,
    passed,
    kept,
    came,
    send,
    recv,
):
    net = Net(send, recv)
    s, core = net.s, net.core
    net.barrier([*net.peers, net.twin])
    source = [lax.rem(s + 8 - k, 8) for k in range(1, 8)]
    mine = pl.ds(pl.multiple_of(core * 64, 64), 64)

    def scatter(i):
        return Scatter(
            net, parts.at[i], far.at[i], near.at[i], passed.at[i], kept.at[i], came.at[i]
        )

    vec = [net.copy(vectors, all_vectors.at[s], to) for to in net.peers]
    all_vectors[s] = vectors[...]
    qkv_in, up_in = [], []
    for k, to in enumerate(net.peers):
        t = to["shard"]
        qkv_in.append(
            [
                net.copy(
                    qkv_weight.at[mine, pl.ds(pl.multiple_of(i * D + t * 128, 128), 128)],
                    columns.at[s, mine, pl.ds(i * 128, 128)],
                    to,
                )
                for i in range(3)
            ]
        )
    for i in range(3):
        columns[s, :, i * 128 : (i + 1) * 128] = qkv_weight[
            :, pl.ds(pl.multiple_of(i * D + s * 128, 128), 128)
        ]
    columns[s, :, 384:896] = up_weight[:, pl.ds(pl.multiple_of(s * 512, 512), 512)]
    cot[s] = cotangent[...]
    x = tokens[...].astype(F32)
    unit1, inverse1 = norm_unit(x)
    for made in vec:
        made.wait_recv()
    table = [all_vectors[j].astype(F32) for j in range(8)]
    gain1, shift1, gain2, shift2, bias_out, bias_down = (
        jnp.concatenate([t[i : i + 1] for t in table], axis=1) for i in range(6)
    )
    first[s] = (unit1 * gain1 + shift1).astype(BF16)
    ag = Gather(net, first)
    qkv_pass = []
    for k in range(7):
        for made in qkv_in[k]:
            made.wait_recv()
        block = columns.at[source[k], mine, pl.ds(0, 384)]
        qkv_pass.append(net.copy(block, block, net.twin))
    ag.relay_one()
    ag.relay_two()
    for k, to in enumerate(net.peers):
        up_in.append(
            net.copy(
                up_weight.at[mine, pl.ds(pl.multiple_of(to["shard"] * 512, 512), 512)],
                columns.at[s, mine, pl.ds(384, 512)],
                to,
            )
        )
    ag.finish()
    for made in qkv_pass:
        made.wait_recv()
    ag_cot = Gather(net, cot)

    def project(b, carry):
        value = dot(first[b], columns[:, :, 0:384].reshape(D, 384)) + qkv_bias[...]
        at = pl.multiple_of(b * 72, 8)
        mixed[0, pl.ds(at, 72), :] = value[0:72]
        mixed[1, pl.ds(at, 72), :] = value[72:144]
        return carry

    lax.fori_loop(0, 8, project, 0)
    qkv_low[...] = mixed[...].astype(BF16)
    ag_cot.relay_one()

    def attend(image, carry):
        q, k, v = (qkv_low[image, :, i * 128 : (i + 1) * 128] for i in range(3))
        zero = jnp.zeros_like(q)
        total = jnp.zeros(q.shape, F32)
        for h, mask in enumerate(head_masks(q.shape)):
            score = dot_last(jnp.where(mask, q, zero), k) * SCALE
            top = jnp.max(score, -1, keepdims=True)
            e = jnp.exp(score - top)
            row = jnp.sum(e, -1, keepdims=True)
            p = (e * (1.0 / row)).astype(BF16)
            total += dot(p, jnp.where(mask, v, zero))
            lse[image, :, h : h + 1] = top + jnp.log(row)
        heads[image] = total
        return carry

    lax.fori_loop(0, 2, attend, 0)
    ag_cot.relay_two()
    up_pass = []
    for k in range(7):
        up_in[k].wait_recv()
        block = columns.at[source[k], mine, pl.ds(384, 512)]
        up_pass.append(net.copy(block, block, net.twin))

    def by_device(ref, b):
        at = pl.multiple_of(b * 72, 8)
        both = [ref[i, pl.ds(at, 72), :] for i in range(2)]
        return jnp.concatenate(both, axis=0).astype(BF16)

    def outward(b, carry):
        value = by_device(heads, b)
        attended[b] = value
        parts[0, b] = dot(value, out_weight[...]).astype(BF16)
        return carry

    lax.fori_loop(0, 8, outward, 0)
    rs = scatter(0)
    rs.relay(0)
    rs.relay(1)
    rs.over()
    resid = tokens[...].astype(F32) + (rs.finish() + bias_out)
    resid_ref[...] = resid
    unit2, inverse2 = norm_unit(resid)
    second[s] = (unit2 * gain2 + shift2).astype(BF16)
    ag = Gather(net, second)
    ag.relay_one()
    ag.relay_two()
    ag_cot.finish()
    for made in up_pass:
        made.wait_recv()
    ag.finish()

    def feed(b, total):
        up = columns[:, :, 384:896].reshape(D, 512)
        u = dot(second[b], up) + up_bias[...]
        square = u * u
        t = jnp.tanh(GELU * (u + 0.044715 * u * square))
        act = (0.5 * u * (1.0 + t)).astype(BF16)
        slope = 0.5 * (1.0 + t) + (0.5 * GELU) * u * (1.0 - t * t) * (
            1.0 + 0.134145 * square
        )
        active[b] = act
        gu = (dot_last(cot[b], down_weight[...]) * slope).astype(BF16)
        grad_upper[b] = gu
        parts[1, b] = dot_last(gu, up).astype(BF16)
        parts[2, b] = dot(act, down_weight[...]).astype(BF16)
        return total + jnp.sum(gu.astype(F32), 0, keepdims=True)

    up_bias_grad = lax.fori_loop(0, 8, feed, jnp.zeros((1, 512), F32))
    rs = scatter(1)
    own = pl.ds(pl.multiple_of(s * 128, 128), 128)
    small[...] = jnp.zeros_like(small)
    for i in range(4):
        small[8 + i : 9 + i, 0:128] = up_bias_grad[:, i * 128 : (i + 1) * 128]
    small[7:8, 0:128] = jnp.sum(cot[:, :, own].astype(F32).reshape(1152, 128), 0, keepdims=True)

    def down_tile(i):
        at = pl.ds(i * 256, 256)
        value = dot_first(
            active[...].reshape(1152, 512), cot[:, :, at].reshape(1152, 256)
        ).astype(BF16)
        for q in range(8):
            rows_grad[q, 0:64, at] = value[q * 64 : (q + 1) * 64]

    down_tile(0)
    rs.relay(0)
    down_tile(1)
    rs.relay(1)
    down_tile(2)
    rs.over()
    down_tile(3)
    grad_second = rs.finish()
    unit2, inverse2 = norm_unit(resid_ref[...])
    grad_resid = cotangent[...].astype(F32) + norm_back(grad_second, unit2, inverse2, gain2)
    grad_resid_ref[...] = grad_resid
    branch[s] = grad_resid.astype(BF16)
    ag = Gather(net, branch)
    gain2_grad = jnp.sum(grad_second * unit2, 0, keepdims=True)
    shift2_grad = jnp.sum(grad_second, 0, keepdims=True)

    def up_tile(i):
        value = dot_first(
            second[:, :, i * 256 : (i + 1) * 256].reshape(1152, 256),
            grad_upper[...].reshape(1152, 512),
        ).astype(BF16)
        for j in range(2):
            for q in range(8):
                columns_grad[q, (2 * i + j) * 16 : (2 * i + j + 1) * 16, 384:896] = value[
                    j * 128 + q * 16 : j * 128 + (q + 1) * 16
                ]

    up_tile(0)
    ag.relay_one()
    up_tile(1)
    ag.relay_two()
    rs_out = scatter(2)
    up_tile(2)
    up_tile(3)
    ag.finish()

    def back_heads(b, carry):
        value = dot_last(branch[b], out_weight[...])
        at = pl.multiple_of(b * 72, 8)
        heads[0, pl.ds(at, 72), :] = value[0:72]
        heads[1, pl.ds(at, 72), :] = value[72:144]
        return carry

    lax.fori_loop(0, 8, back_heads, 0)
    rs_out.relay(0)

    def attend_back(image, carry):
        q, k, v = (qkv_low[image, :, i * 128 : (i + 1) * 128] for i in range(3))
        grad = heads[image].astype(BF16)
        zero = jnp.zeros_like(q)
        dq = jnp.zeros(q.shape, F32)
        dk, dv = dq, dq
        for h, mask in enumerate(head_masks(q.shape)):
            qh, kh, gh = (jnp.where(mask, a, zero) for a in (q, k, grad))
            p = jnp.exp(dot_last(qh, k) * SCALE - lse[image, :, h : h + 1])
            dp = dot_last(gh, v)
            inner = jnp.sum(p * dp, -1, keepdims=True)
            ds = (p * (dp - inner)).astype(BF16)
            dq += dot(ds, kh)
            dk += dot_first(ds, qh)
            dv += dot_first(p.astype(BF16), gh)
        mixed[image, :, 0:128] = dq * SCALE
        mixed[image, :, 128:256] = dk * SCALE
        mixed[image, :, 256:384] = dv
        return carry

    lax.fori_loop(0, 2, attend_back, 0)
    rs_out.relay(1)

    def back_first(b, total):
        value = by_device(mixed, b)
        grad_qkv[b] = value
        parts[3, b] = dot_last(value, columns[:, :, 0:384].reshape(D, 384)).astype(BF16)
        return total + jnp.sum(value.astype(F32), 0, keepdims=True)

    qkv_bias_grad = lax.fori_loop(0, 8, back_first, jnp.zeros((1, 384), F32))
    rs = scatter(3)
    rs_out.over()
    small[4:5, 0:128] = qkv_bias_grad[:, 0:128]
    small[5:6, 0:128] = qkv_bias_grad[:, 256:384]
    small[6:7, 0:128] = jnp.sum(branch[:, :, own].astype(F32).reshape(1152, 128), 0, keepdims=True)

    def qkv_tile(i):
        value = dot_first(
            first[:, :, i * 256 : (i + 1) * 256].reshape(1152, 256),
            grad_qkv[...].reshape(1152, 384),
        ).astype(BF16)
        for j in range(2):
            for q in range(8):
                columns_grad[q, (2 * i + j) * 16 : (2 * i + j + 1) * 16, 0:384] = value[
                    j * 128 + q * 16 : j * 128 + (q + 1) * 16
                ]

    qkv_tile(0)
    rs.relay(0)
    qkv_tile(1)
    rs.relay(1)
    qkv_tile(2)
    qkv_tile(3)
    rs.over()
    value = dot_first(attended[...].reshape(1152, 128), branch[...].reshape(1152, D)).astype(BF16)
    for q in range(8):
        rows_grad[q, 64:80, :] = value[q * 16 : (q + 1) * 16]
    block_out[...] = (resid_ref[...] + (rs_out.finish() + bias_down)).astype(BF16)
    grad_first = rs.finish()
    unit1, inverse1 = norm_unit(tokens[...].astype(F32))
    input_grad[...] = (
        grad_resid_ref[...] + norm_back(grad_first, unit1, inverse1, gain1)
    ).astype(BF16)
    gain1_grad = jnp.sum(grad_first * unit1, 0, keepdims=True)
    shift1_grad = jnp.sum(grad_first, 0, keepdims=True)
    four = jnp.concatenate(
        [gain1_grad, shift1_grad, gain2_grad, shift2_grad, jnp.zeros((12, D), F32)], axis=0
    ).astype(BF16)
    for t in range(8):
        fours[t] = four[:, t * 128 : (t + 1) * 128]
    moved = [net.copy(fours.at[to["shard"]], fours_in.at[s], to) for to in net.peers]
    fours_in[s] = fours[s]
    for made in moved:
        made.wait_recv()
    total = jnp.sum(fours_in[...].astype(F32), 0)
    small[0:4, 0:128] = total[0:4]
    small_grad[...] = jnp.zeros_like(small_grad)
    small_grad[0] = small[...].astype(BF16)
    net.drain()


def layer(*arguments):
    vmem = lambda *shape: pltpu.VMEM(shape, BF16)
    wide = lambda *shape: pltpu.VMEM(shape, F32)
    space = pl.BlockSpec(memory_space=pltpu.VMEM)
    shape = lambda *sizes: jax.ShapeDtypeStruct(sizes, BF16)
    return pl.pallas_call(
        layer_kernel,
        out_shape=[
            shape(ROWS, D),
            shape(ROWS, D),
            shape(8, 80, D),
            shape(8, 128, 896),
            shape(8, 16, 256),
        ],
        in_specs=[space] * 9,
        out_specs=[space] * 5,
        scratch_shapes=[
            vmem(8, 16, 128),
            vmem(8, 128, 896),
            vmem(8, ROWS, D),
            vmem(8, ROWS, D),
            vmem(8, ROWS, D),
            vmem(8, ROWS, D),
            wide(2, 576, 384),
            vmem(2, 576, 384),
            wide(2, 576, 128),
            wide(2, 576, 128),
            vmem(8, ROWS, 128),
            vmem(8, ROWS, 512),
            vmem(8, ROWS, 512),
            vmem(8, ROWS, 384),
            wide(ROWS, D),
            wide(ROWS, D),
            wide(16, 256),
            vmem(8, 16, 128),
            vmem(8, 16, 128),
            vmem(4, 8, ROWS, D),
            vmem(4, 2, 2, ROWS, HALF),
            vmem(4, 2, 2, ROWS, HALF),
            vmem(4, 2, 2, ROWS, HALF),
            vmem(4, ROWS, D),
            vmem(4, ROWS, D),
            pltpu.SemaphoreType.DMA((160,)),
            pltpu.SemaphoreType.DMA((160,)),
        ],
        name="layer",
        cost_estimate=pl.CostEstimate(
            flops=11 * 10**9, bytes_accessed=12 * 10**6, transcendentals=0
        ),
        compiler_params=pltpu.CompilerParams(
            collective_id=1, has_side_effects=True, vmem_limit_bytes=60 << 20
        ),
    )(*arguments)


def sum_kernel(*refs):
    inputs, refs = refs[:3], refs[3:]
    outs, refs = refs[:5], refs[5:]
    sent, refs = refs[:3], refs[3:]
    work, refs = refs[:3], refs[3:]
    far, near, passed = refs[:3], refs[3:6], refs[6:9]
    kept, came, final = refs[9:12], refs[12:15], refs[15:18]
    turned, send, recv = refs[18:]
    net = Net(send, recv)
    net.barrier([net.twin, net.up, net.down, net.beside, *net.peers])
    core, y, s = net.core, net.y, net.s
    half = [512, 512, 128]
    width = [D, 896, 256]
    mine = pl.ds(core * 4, 4)
    up, down, facing = (lax.rem(y + k, 4) for k in (1, 3, 2))
    q = core * 4 + y

    moved = [net.copy(a.at[pl.ds((1 - core) * 4, 4)], b, net.twin) for a, b in zip(inputs, sent)]
    for i in range(3):
        moved[i].wait_recv()
        work[i][...] = add(inputs[i][mine], sent[i][...]).astype(BF16)

    halves = [(pl.ds(0, n), pl.ds(n, w - n)) for n, w in zip(half, width)]
    fars, nears, passes = [], [], []
    for i in range(3):
        one, two = halves[i]
        fars.append(
            (
                net.copy(work[i].at[facing, :, one], far[i].at[:, one], net.up),
                net.copy(work[i].at[facing, :, two], far[i].at[:, two], net.down),
            )
        )
    for i in range(3):
        one, two = halves[i]
        nears.append(
            (
                net.copy(work[i].at[up, :, two], near[i].at[:, two], net.up),
                net.copy(work[i].at[down, :, one], near[i].at[:, one], net.down),
            )
        )
    for i in range(3):
        made = []
        for k, (block, to) in enumerate(((up, net.up), (down, net.down))):
            fars[i][k].wait_recv()
            part = halves[i][k]
            far[i][:, part] = add(far[i][:, part], work[i][block, :, part]).astype(BF16)
            made.append(net.copy(far[i].at[:, part], passed[i].at[:, part], to))
        passes.append(made)
    over = []
    for i in range(3):
        for made in (*nears[i], *passes[i]):
            made.wait_recv()
        kept[i][...] = add(work[i][y], near[i][...], passed[i][...]).astype(BF16)
        over.append(net.copy(kept[i], came[i], net.beside))
    over[1].wait_recv()
    turned[...] = add(kept[1][...], came[1][...]).astype(BF16).reshape(8, 16, 896)
    place = lambda t: pl.ds(pl.multiple_of(t * 16, 16), 16)
    crossed = [
        net.copy(turned.at[to["shard"]], final[1].at[q, place(s)], to) for to in net.peers
    ]
    final[1][q, place(s)] = turned[s]
    for i in (0, 2):
        over[i].wait_recv()
        final[i][q] = add(kept[i][...], came[i][...]).astype(BF16)
    for made in crossed:
        made.wait_recv()

    steps = []
    for i in range(3):
        own = final[i].at[q]
        steps.append((net.copy(own, own, net.up), net.copy(own, own, net.down)))
    lasts = []
    for i in range(3):
        one, two = halves[i]
        steps[i][0].wait_recv()
        part = final[i].at[core * 4 + down, :, one]
        lasts.append(net.copy(part, part, net.up))
        steps[i][1].wait_recv()
        part = final[i].at[core * 4 + up, :, two]
        lasts.append(net.copy(part, part, net.down))
    ends = []
    for i in range(3):
        lasts[2 * i].wait_recv()
        lasts[2 * i + 1].wait_recv()
        part = final[i].at[mine]
        ends.append(net.copy(part, part, net.twin))
    for made in ends:
        made.wait_recv()
    qkv_grad, out_grad, up_grad, down_grad, small = outs
    for k in range(8):
        down_grad[k * 64 : (k + 1) * 64, :] = final[0][k, 0:64, :]
        out_grad[k * 16 : (k + 1) * 16, :] = final[0][k, 64:80, :]
        rows = slice(k * 16, (k + 1) * 16)
        for t in range(8):
            block = final[1][k, t * 16 : (t + 1) * 16, :]
            up_grad[rows, t * 512 : (t + 1) * 512] = block[:, 384:896]
            for i in range(3):
                at = i * D + t * 128
                qkv_grad[rows, at : at + 128] = block[:, i * 128 : (i + 1) * 128]
    small[...] = final[2][0]
    net.drain()


def sum_replicas(*arguments):
    space = pl.BlockSpec(memory_space=pltpu.VMEM)
    shape = lambda *sizes: jax.ShapeDtypeStruct(sizes, BF16)
    sizes = ((80, D), (128, 896), (16, 256))
    vmem = lambda *lead: [pltpu.VMEM((*lead, *size), BF16) for size in sizes]
    return pl.pallas_call(
        sum_kernel,
        out_shape=[
            shape(128, 3 * D),
            shape(128, D),
            shape(128, 4096),
            shape(512, D),
            shape(16, 256),
        ],
        in_specs=[space] * 3,
        out_specs=[space] * 5,
        scratch_shapes=[
            *vmem(4),
            *vmem(4),
            *vmem(),
            *vmem(),
            *vmem(),
            *vmem(),
            *vmem(),
            *vmem(8),
            pltpu.VMEM((8, 16, 896), BF16),
            pltpu.SemaphoreType.DMA((64,)),
            pltpu.SemaphoreType.DMA((64,)),
        ],
        name="sum_replicas",
        compiler_params=pltpu.CompilerParams(
            collective_id=2, has_side_effects=True, vmem_limit_bytes=48 << 20
        ),
    )(*arguments)


def body(
    tokens,
    cotangent,
    attn_gain,
    attn_shift,
    qkv_weight,
    query_bias,
    value_bias,
    out_weight,
    out_bias,
    mlp_gain,
    mlp_shift,
    up_weight,
    up_bias,
    down_weight,
    down_bias,
):
    vectors = jnp.stack([attn_gain, attn_shift, mlp_gain, mlp_shift, out_bias, down_bias])
    vectors = jnp.pad(vectors, ((0, 10), (0, 0)))
    zeros = jnp.zeros((128,), F32)
    qkv_bias = jnp.concatenate([query_bias.astype(F32), zeros, value_bias.astype(F32)])
    block_out, input_grad, *grads = layer(
        tokens.reshape(ROWS, D),
        cotangent.reshape(ROWS, D),
        vectors,
        qkv_weight,
        up_weight,
        out_weight,
        down_weight,
        qkv_bias.reshape(1, 384),
        up_bias.astype(F32).reshape(1, 512),
    )
    sums = [a.astype(F32) for a in sum_replicas(*grads)]
    qkv_grad, out_grad, up_grad, down_grad, small = sums
    small = small[:, :128]
    return (
        block_out.reshape(2, 72, D),
        input_grad.reshape(2, 72, D),
        small[0],
        small[1],
        qkv_grad,
        small[4],
        small[5],
        out_grad,
        small[6],
        small[2],
        small[3],
        up_grad,
        small[8:12].reshape(512),
        down_grad,
        small[7],
    )


def solution(mesh):
    row, cube, flat = P("shard"), P("replica", "shard", None), P("shard", None)
    return jax.shard_map(
        body,
        mesh=mesh,
        in_specs=(cube, cube, row, row, flat, row, row, flat, row, row, row, flat, row, flat, row),
        out_specs=(cube, cube, row, row, flat, row, row, flat, row, row, row, flat, row, flat, row),
        check_vma=False,
    )
```

time: 821 us -> 285 us (0.35)
  waiting for transfers between devices: 670 us -> 0 us
  Pallas kernels: 8.41 us -> 269 us
  matrix products: 45.4 us -> 0 us
  local copies, waits for them, and re-layouts: 42.1 us -> 6.64 us
  starting transfers between devices: 17.1 us -> 0 us
  other arithmetic: 22.7 us -> 7.82 us
  between operations: 14.3 us -> 0.69 us
    reduce_scatter x4 -> x0, waiting for transfers between devices: 293 us -> none  [scatter(): lax.psum_scatter(a.astype(BF16), 'shard', scatter_dimension=0, tiled=True)]
    pallas_call x2, Pallas kernels: 8.41 us -> 269 us  [the longest x1 209 us: layer(): pl.pallas_call(layer_kernel, out_shape=[shape(ROWS, D), shape(ROWS, D), s...]
    all_gather x4 -> x0, waiting for transfers between devices: 221 us -> none  [gather(): return lax.all_gather(a, 'shard', axis=0, tiled=True)]
    psum x1 -> x0, waiting for transfers between devices: 124 us -> none  [body(): early = lax.psum(early, 'replica').astype(F32)]
    dot_general x12 -> x0, matrix products: 45.4 us -> none  [the longest x4 17.3 us: dot(): lax.dot_general(a, b, (((1,), (0,)), ((), ())), preferred_element_type=F32)]
    all_to_all x3 -> x0, waiting for transfers between devices: 31.6 us -> none  [turn(): return lax.all_to_all(a, 'shard', 0, 0, tiled=True)]
    all_to_all x3 -> x0, starting transfers between devices: 16.1 us -> none  [turn(): return lax.all_to_all(a, 'shard', 0, 0, tiled=True)]
    slice x8 -> x0, local copies, waits for them, and re-layouts: 10.8 us -> none  [the longest x1 2.48 us: body(): down_weight_grad = early[:512]]
  transfers between devices with their start and end apart: 12 -> 0, of which waited for: 11 -> 0; matrix products, arithmetic and copies ran while one was open for 5% -> 0% of each run, Pallas kernels for 0% -> 0%
where the time goes in v2:
time: 285 us
  Pallas kernels  269 us (94%)
  other arithmetic  7.82 us (3%)
  local copies, waits for them, and re-layouts  6.64 us (2%)
    pallas_call x1, Pallas kernels, layer(): pl.pallas_call(layer_kernel, out_shape=[shape(ROWS, D), shape(ROWS, D), s...  209 us
    pallas_call x1, Pallas kernels, sum_replicas(): pl.pallas_call(sum_kernel, out_shape=[shape(128, 3 * D), shape(128, D), s...  60.8 us

profile of v2, /device:TPU:1, one launch (start us, length us, event | category | flops | bytes accessed | tf_op | source)
XLA Modules:
  0.0 284.5 jit_solution(16630426545857799219)
XLA Ops:
  0.6 0.8 stack.27
  1.4 0.6 pad.4.vectors
  2.0 0.7 convert_element_type.24
  2.7 0.7 convert_element_type.25
  3.3 0.6 reshape.55.qkv_bias
  3.9 1.3 reshape.61
  5.2 208.6 %layer.1 = (bf16[144,1024]{1,0:T(8,128)(2,1)}, bf16[144,1024]{1,0:T(8,128)(2,1)}, bf16[8,80,1024]{2,1,0:T(8,128)(2,1)}, bf16[8,128,896]{2,1,0:T(8,128)(2,1)}, bf16[8,16,256]{2,1,0:T(8,128)(2,1)}) custom-call(bf16[144,1024]{1,0:T(8,128)(2,1)} %bitcast.38, bf16[144,1024]{1,0:T(8,128)(2,1)} %bitcast.39, bf16[16,128]{1,0:T(8,128)(2,1)} %pad.4.vectors, ...), custom_call_target="tpu_custom_call" | custom-call | flops 11000000512 | bytes 12000000 | tf_op jit(solution)/shard_map/layer/pallas_call | solution.py:533
  213.7 0.0 copy-start
  213.7 1.3 copy-done
  215.1 0.0 copy-start.1
  215.1 0.8 copy-done.1
  215.9 60.8 %sum_replicas.1 = (bf16[128,3072]{1,0:T(8,128)(2,1)S(1)}, bf16[128,1024]{1,0:T(8,128)(2,1)S(1)}, bf16[128,4096]{1,0:T(8,128)(2,1)S(1)}, bf16[512,1024]{1,0:T(8,128)(2,1)S(1)}, bf16[16,256]{1,0:T(8,128)(2,1)S(1)}) custom-call(bf16[8,80,1024]{2,1,0:T(8,128)(2,1)S(1)} %copy-done, bf16[8,128,896]{2,1,0:T(8,128)(2,1)} %get-tuple-element.28.refs_1_, ...), custom_call_target="tpu_custom_call" | custom-call | tf_op jit(solution)/shard_map/sum_replicas/pallas_call | solution.py:691
  276.7 0.5 slice_bitcast_fusion.1
  277.3 0.6 slice_bitcast_fusion
  277.9 1.5 convert_element_type.29
  279.4 1.6 convert_element_type.30
  281.0 0.0 copy-start.3
  281.0 0.0 copy-start.2
  281.0 1.3 convert_element_type.27
  282.3 0.8 convert_element_type.28
  283.1 0.0 copy-done.3
  283.1 0.7 copy.32
  283.8 0.0 copy-done.2
  283.8 0.7 copy.33
  (3 shorter events, 0.0 us)
Async XLA Ops:
  213.7 1.3 copy-start
  215.1 0.8 copy-start.1
  281.0 2.1 copy-start.3
  281.0 2.9 %copy-start.2 = (bf16[144,1024]{1,0:T(8,128)(2,1)S(1)}, bf16[144,1024]{1,0:T(8,128)(2,1)}, u32[]{:S(2)}) copy-start(bf16[144,1024]{1,0:T(8,128)(2,1)} %get-tuple-element.26) | copy-start | bytes 884740

commit v3 on v2

--- a/solution.py
+++ b/solution.py
@@ -105,96 +105,108 @@
 class Gather:
     def __init__(self, net, whole):
         self.net, self.whole = net, whole
+        self.a = self.piece(net.s, 0, net.right)
+        self.b = self.piece(net.s, 1, net.left)
         own = whole.at[net.s]
         self.z = net.copy(own, own, net.across)
-        self.a = net.copy(own, own, net.right)
-        self.b = net.copy(own, own, net.left)
-
-    def piece(self, block, first, to):
-        part = self.whole.at[block, :, pl.ds(0 if first else HALF, HALF)]
+        self.more = [self.piece(net.s, 1, net.right), self.piece(net.s, 0, net.left)]
+
+    def piece(self, block, second, to):
+        part = self.whole.at[block, :, pl.ds(second * HALF, HALF)]
         return self.net.copy(part, part, to)
 
     def relay_one(self):
+        net = self.net
+        self.a.wait_recv()
+        self.c = self.piece(net.at(net.h, net.x + 3), 0, net.right)
+        self.b.wait_recv()
+        self.d = self.piece(net.at(net.h, net.x + 1), 1, net.left)
+
+    def relay_two(self):
         net = self.net
         self.z.wait_recv()
         part = self.whole.at[net.at(1 - net.h, net.x)]
-        self.za = net.copy(part, part, net.right)
-        self.zb = net.copy(part, part, net.left)
-        self.a.wait_recv()
-        self.c = self.piece(net.at(net.h, net.x + 3), True, net.right)
-        self.b.wait_recv()
-        self.d = self.piece(net.at(net.h, net.x + 1), False, net.left)
-
-    def relay_two(self):
-        net = self.net
-        self.za.wait_recv()
-        self.e = self.piece(net.at(1 - net.h, net.x + 3), True, net.right)
-        self.zb.wait_recv()
-        self.f = self.piece(net.at(1 - net.h, net.x + 1), False, net.left)
+        self.rest = [net.copy(part, part, net.right), net.copy(part, part, net.left)]
+        block = net.at(net.h, net.x + 2)
+        self.c.wait_recv()
+        self.rest.append(self.piece(block, 0, net.across))
+        self.d.wait_recv()
+        self.rest.append(self.piece(block, 1, net.across))
+
+    def row(self):
+        for made in self.more:
+            made.wait_recv()
 
     def finish(self):
-        for made in (self.c, self.d, self.e, self.f):
+        for made in self.rest:
             made.wait_recv()
 
 
 class Scatter:
-    def __init__(self, net, part, far, near, passed, kept, came):
-        self.net, self.part = net, part
-        self.far, self.near, self.passed, self.kept, self.came = far, near, passed, kept, came
-        self.rows = (1 - net.h, net.h)
-        halves = (pl.ds(0, HALF), pl.ds(HALF, HALF))
-        self.first, self.second = halves
-        self.fars, self.nears, self.passes = [], [], [None, None]
-        for j, h in enumerate(self.rows):
-            block = net.at(h, net.x + 2)
-            self.fars.append(
-                (
-                    net.copy(part.at[block, :, self.first], far.at[0, j], net.right),
-                    net.copy(part.at[block, :, self.second], far.at[1, j], net.left),
-                )
-            )
-        for j, h in enumerate(self.rows):
-            r, l = net.at(h, net.x + 1), net.at(h, net.x + 3)
-            self.nears.append(
-                (
-                    net.copy(part.at[r, :, self.second], near.at[0, j], net.right),
-                    net.copy(part.at[l, :, self.first], near.at[1, j], net.left),
-                )
-            )
-
-    def relay(self, j):
-        net, part, far, passed = self.net, self.part, self.far, self.passed
-        h = self.rows[j]
-        made = []
-        steps = ((0, net.at(h, net.x + 1), self.first, net.right),)
-        steps += ((1, net.at(h, net.x + 3), self.second, net.left),)
-        for k, block, half, to in steps:
-            self.fars[j][k].wait_recv()
-            far[k, j] = add(far[k, j], part[block, :, half]).astype(BF16)
-            made.append(net.copy(far.at[k, j], passed.at[k, j], to))
-        self.passes[j] = made
-
-    def halves(self, j):
-        for made in (*self.nears[j], *self.passes[j]):
+    def __init__(self, net, part, hop, side, near, far, passed, kept, came):
+        self.net, self.part, self.hop_in, self.side_in = net, part, hop, side
+        self.near_in, self.far_in, self.passed, self.kept, self.came = near, far, passed, kept, came
+        self.one, self.two = pl.ds(0, HALF), pl.ds(HALF, HALF)
+        h, x = net.h, net.x
+        self.own, self.facing = net.s, net.at(h, x + 2)
+        self.right, self.left = net.at(h, x + 1), net.at(h, x + 3)
+        self.other = [net.at(1 - h, x + k) for k in range(4)]
+
+    def hop(self):
+        self.hopped = self.net.copy(self.part.at[self.other[2]], self.hop_in, self.net.across)
+
+    def side(self):
+        net, part = self.net, self.part
+        self.sides = [
+            net.copy(part.at[self.other[1]], self.side_in.at[0], net.right),
+            net.copy(part.at[self.other[3]], self.side_in.at[1], net.left),
+        ]
+
+    def near(self):
+        net, part = self.net, self.part
+        self.nears = [
+            net.copy(part.at[self.right, :, self.two], self.near_in.at[0], net.right),
+            net.copy(part.at[self.left, :, self.one], self.near_in.at[1], net.left),
+        ]
+
+    def far(self):
+        net, hop = self.net, self.hop_in
+        self.hopped.wait_recv()
+        hop[...] = add(hop[...], self.part[self.facing]).astype(BF16)
+        self.fars = [
+            net.copy(hop.at[:, self.one], self.far_in.at[0], net.right),
+            net.copy(hop.at[:, self.two], self.far_in.at[1], net.left),
+        ]
+
+    def over(self):
+        for made in self.sides:
             made.wait_recv()
-        own = self.net.at(self.rows[j], self.net.x)
-        part, near, passed = self.part, self.near, self.passed
-        return (
-            add(part[own, :, self.first], passed[0, j], near[1, j]),
-            add(part[own, :, self.second], passed[1, j], near[0, j]),
-        )
-
-    def over(self):
-        one, two = self.halves(0)
-        self.kept[:, 0:HALF] = one.astype(BF16)
-        self.kept[:, HALF:D] = two.astype(BF16)
-        self.z = self.net.copy(self.kept, self.came, self.net.across)
+        self.kept[...] = add(
+            self.part[self.other[0]], self.side_in[0], self.side_in[1]
+        ).astype(BF16)
+        self.crossed = self.net.copy(self.kept, self.came, self.net.across)
+
+    def relay(self):
+        net, part, far = self.net, self.part, self.far_in
+        self.fars[0].wait_recv()
+        far[0] = add(far[0], part[self.right, :, self.one]).astype(BF16)
+        passes = [net.copy(far.at[0], self.passed.at[0], net.right)]
+        self.fars[1].wait_recv()
+        far[1] = add(far[1], part[self.left, :, self.two]).astype(BF16)
+        passes.append(net.copy(far.at[1], self.passed.at[1], net.left))
+        self.last = [*self.nears, *passes, self.crossed]
 
     def finish(self):
-        one, two = self.halves(1)
-        self.z.wait_recv()
+        for made in self.last:
+            made.wait_recv()
+        part, near, passed, came = self.part, self.near_in, self.passed, self.came
+        one, two = self.one, self.two
         return jnp.concatenate(
-            [add(one, self.came[:, 0:HALF]), add(two, self.came[:, HALF:D])], axis=1
+            [
+                add(part[self.own, :, one], passed[0], near[1], came[:, one]),
+                add(part[self.own, :, two], passed[1], near[0], came[:, two]),
+            ],
+            axis=1,
         )
 
 
@@ -233,8 +245,10 @@
     fours,
     fours_in,
     parts,
+    hop,
+    side,
+    near,
     far,
-    near,
     passed,
     kept,
     came,
@@ -248,9 +262,29 @@
     mine = pl.ds(pl.multiple_of(core * 64, 64), 64)
 
     def scatter(i):
-        return Scatter(
-            net, parts.at[i], far.at[i], near.at[i], passed.at[i], kept.at[i], came.at[i]
-        )
+        buffers = (parts, hop, side, near, far, passed, kept, came)
+        return Scatter(net, *(buffer.at[i] for buffer in buffers))
+
+    def each(work, least, end, carry=0):
+        def step(i, carry):
+            row, j = i // 4, lax.rem(i, 4)
+            same = j + j // 2 - 2 * (j // 3)
+            cross = lax.rem(2 * j, 3) + 3 * (j // 3)
+            h = net.h + row - 2 * net.h * row
+            return work(net.at(h, net.x + (1 - row) * same + row * cross), carry)
+
+        return lax.fori_loop(least, end, step, carry)
+
+    def each_sent(rs, work, carry):
+        carry = each(work, 5, 6, carry)
+        rs.hop()
+        carry = each(work, 6, 8, carry)
+        rs.side()
+        carry = each(work, 1, 3, carry)
+        rs.near()
+        carry = each(work, 3, 5, carry)
+        rs.far()
+        return each(work, 0, 1, carry)
 
     vec = [net.copy(vectors, all_vectors.at[s], to) for to in net.peers]
     all_vectors[s] = vectors[...]
@@ -299,10 +333,9 @@
                 to,
             )
         )
-    ag.finish()
     for made in qkv_pass:
         made.wait_recv()
-    ag_cot = Gather(net, cot)
+    ag.row()
 
     def project(b, carry):
         value = dot(first[b], columns[:, :, 0:384].reshape(D, 384)) + qkv_bias[...]
@@ -311,7 +344,10 @@
         mixed[1, pl.ds(at, 72), :] = value[72:144]
         return carry
 
-    lax.fori_loop(0, 8, project, 0)
+    each(project, 0, 5)
+    ag.finish()
+    ag_cot = Gather(net, cot)
+    each(project, 5, 8)
     qkv_low[...] = mixed[...].astype(BF16)
     ag_cot.relay_one()
 
@@ -349,22 +385,19 @@
         parts[0, b] = dot(value, out_weight[...]).astype(BF16)
         return carry
 
-    lax.fori_loop(0, 8, outward, 0)
     rs = scatter(0)
-    rs.relay(0)
-    rs.relay(1)
+    each_sent(rs, outward, 0)
     rs.over()
+    rs.relay()
     resid = tokens[...].astype(F32) + (rs.finish() + bias_out)
     resid_ref[...] = resid
     unit2, inverse2 = norm_unit(resid)
     second[s] = (unit2 * gain2 + shift2).astype(BF16)
     ag = Gather(net, second)
-    ag.relay_one()
-    ag.relay_two()
+    ag_cot.row()
     ag_cot.finish()
     for made in up_pass:
         made.wait_recv()
-    ag.finish()
 
     def feed(b, total):
         up = columns[:, :, 384:896].reshape(D, 512)
@@ -382,8 +415,18 @@
         parts[2, b] = dot(act, down_weight[...]).astype(BF16)
         return total + jnp.sum(gu.astype(F32), 0, keepdims=True)
 
-    up_bias_grad = lax.fori_loop(0, 8, feed, jnp.zeros((1, 512), F32))
+    ag.relay_one()
+    up_bias_grad = each(feed, 0, 1, jnp.zeros((1, 512), F32))
+    ag.relay_two()
+    ag.row()
+    up_bias_grad = each(feed, 1, 5, up_bias_grad)
+    ag.finish()
     rs = scatter(1)
+    up_bias_grad = each(feed, 5, 6, up_bias_grad)
+    rs.hop()
+    up_bias_grad = each(feed, 6, 8, up_bias_grad)
+    rs.side()
+    rs.near()
     own = pl.ds(pl.multiple_of(s * 128, 128), 128)
     small[...] = jnp.zeros_like(small)
     for i in range(4):
@@ -399,11 +442,11 @@
             rows_grad[q, 0:64, at] = value[q * 64 : (q + 1) * 64]
 
     down_tile(0)
-    rs.relay(0)
+    rs.far()
     down_tile(1)
-    rs.relay(1)
+    rs.over()
+    rs.relay()
     down_tile(2)
-    rs.over()
     down_tile(3)
     grad_second = rs.finish()
     unit2, inverse2 = norm_unit(resid_ref[...])
@@ -425,14 +468,17 @@
                     j * 128 + q * 16 : j * 128 + (q + 1) * 16
                 ]
 
+    ag.relay_one()
     up_tile(0)
-    ag.relay_one()
+    ag.relay_two()
+    ag.row()
     up_tile(1)
-    ag.relay_two()
+    up_tile(2)
+    ag.finish()
     rs_out = scatter(2)
-    up_tile(2)
-    up_tile(3)
-    ag.finish()
+    rs_out.hop()
+    rs_out.side()
+    rs_out.near()
 
     def back_heads(b, carry):
         value = dot_last(branch[b], out_weight[...])
@@ -441,8 +487,9 @@
         heads[1, pl.ds(at, 72), :] = value[72:144]
         return carry
 
-    lax.fori_loop(0, 8, back_heads, 0)
-    rs_out.relay(0)
+    each(back_heads, 0, 8)
+    up_tile(3)
+    rs_out.far()
 
     def attend_back(image, carry):
         q, k, v = (qkv_low[image, :, i * 128 : (i + 1) * 128] for i in range(3))
@@ -465,7 +512,8 @@
         return carry
 
     lax.fori_loop(0, 2, attend_back, 0)
-    rs_out.relay(1)
+    rs_out.over()
+    rs_out.relay()
 
     def back_first(b, total):
         value = by_device(mixed, b)
@@ -473,9 +521,8 @@
         parts[3, b] = dot_last(value, columns[:, :, 0:384].reshape(D, 384)).astype(BF16)
         return total + jnp.sum(value.astype(F32), 0, keepdims=True)
 
-    qkv_bias_grad = lax.fori_loop(0, 8, back_first, jnp.zeros((1, 384), F32))
     rs = scatter(3)
-    rs_out.over()
+    qkv_bias_grad = each_sent(rs, back_first, jnp.zeros((1, 384), F32))
     small[4:5, 0:128] = qkv_bias_grad[:, 0:128]
     small[5:6, 0:128] = qkv_bias_grad[:, 256:384]
     small[6:7, 0:128] = jnp.sum(branch[:, :, own].astype(F32).reshape(1152, 128), 0, keepdims=True)
@@ -492,12 +539,11 @@
                 ]
 
     qkv_tile(0)
-    rs.relay(0)
+    rs.over()
     qkv_tile(1)
-    rs.relay(1)
+    rs.relay()
     qkv_tile(2)
     qkv_tile(3)
-    rs.over()
     value = dot_first(attended[...].reshape(1152, 128), branch[...].reshape(1152, D)).astype(BF16)
     for q in range(8):
         rows_grad[q, 64:80, :] = value[q * 16 : (q + 1) * 16]
@@ -562,9 +608,11 @@
             vmem(8, 16, 128),
             vmem(8, 16, 128),
             vmem(4, 8, ROWS, D),
-            vmem(4, 2, 2, ROWS, HALF),
-            vmem(4, 2, 2, ROWS, HALF),
-            vmem(4, 2, 2, ROWS, HALF),
+            vmem(4, ROWS, D),
+            vmem(4, 2, ROWS, D),
+            vmem(4, 2, ROWS, HALF),
+            vmem(4, 2, ROWS, HALF),
+            vmem(4, 2, ROWS, HALF),
             vmem(4, ROWS, D),
             vmem(4, ROWS, D),
             pltpu.SemaphoreType.DMA((160,)),

time: 285 us -> 246 us (0.86)
  Pallas kernels: 269 us -> 231 us
    pallas_call x1, Pallas kernels: 209 us -> 165 us  [layer(): pl.pallas_call(layer_kernel, out_shape=[shape(ROWS, D), shape(ROWS, D), s...]
    pallas_call x1, Pallas kernels: 60.8 us -> 66.4 us  [sum_replicas(): pl.pallas_call(sum_kernel, out_shape=[shape(128, 3 * D), shape(128, D), s...]
where the time goes in v3:
time: 246 us
  Pallas kernels  231 us (94%)
  other arithmetic  7.82 us (3%)
  local copies, waits for them, and re-layouts  6.64 us (3%)
    pallas_call x1, Pallas kernels, layer(): pl.pallas_call(layer_kernel, out_shape=[shape(ROWS, D), shape(ROWS, D), s...  165 us
    pallas_call x1, Pallas kernels, sum_replicas(): pl.pallas_call(sum_kernel, out_shape=[shape(128, 3 * D), shape(128, D), s...  66.4 us
    convert_element_type x5, other arithmetic, body(): sums = [a.astype(F32) for a in sum_replicas(*grads)]  5.24 us

profile of v3, /device:TPU:1, one launch (start us, length us, event | category | flops | bytes accessed | tf_op | source)
XLA Modules:
  0.0 246.2 jit_solution(6636380498499060042)
XLA Ops:
  0.6 0.8 stack.27
  1.4 0.6 pad.4.vectors
  2.0 0.7 convert_element_type.24
  2.7 0.7 convert_element_type.25
  3.3 0.6 reshape.55.qkv_bias
  3.9 1.3 reshape.61
  5.2 164.6 %layer.1 = (bf16[144,1024]{1,0:T(8,128)(2,1)}, bf16[144,1024]{1,0:T(8,128)(2,1)}, bf16[8,80,1024]{2,1,0:T(8,128)(2,1)}, bf16[8,128,896]{2,1,0:T(8,128)(2,1)}, bf16[8,16,256]{2,1,0:T(8,128)(2,1)}) custom-call(bf16[144,1024]{1,0:T(8,128)(2,1)} %bitcast.38, bf16[144,1024]{1,0:T(8,128)(2,1)} %bitcast.39, bf16[16,128]{1,0:T(8,128)(2,1)} %pad.4.vectors, ...), custom_call_target="tpu_custom_call" | custom-call | flops 11000000512 | bytes 12000000 | tf_op jit(solution)/shard_map/layer/pallas_call | solution.py:579
  169.8 0.0 copy-start
  169.8 1.3 copy-done
  171.1 0.0 copy-start.1
  171.1 0.8 copy-done.1
  172.0 66.4 %sum_replicas.1 = (bf16[128,3072]{1,0:T(8,128)(2,1)S(1)}, bf16[128,1024]{1,0:T(8,128)(2,1)S(1)}, bf16[128,4096]{1,0:T(8,128)(2,1)S(1)}, bf16[512,1024]{1,0:T(8,128)(2,1)S(1)}, bf16[16,256]{1,0:T(8,128)(2,1)S(1)}) custom-call(bf16[8,80,1024]{2,1,0:T(8,128)(2,1)S(1)} %copy-done, bf16[8,128,896]{2,1,0:T(8,128)(2,1)} %get-tuple-element.28.refs_1_, ...), custom_call_target="tpu_custom_call" | custom-call | tf_op jit(solution)/shard_map/sum_replicas/pallas_call | solution.py:739
  238.4 0.5 slice_bitcast_fusion.1
  239.0 0.6 slice_bitcast_fusion
  239.5 1.5 convert_element_type.29
  241.1 1.6 convert_element_type.30
  242.6 0.0 copy-start.3
  242.6 0.0 copy-start.2
  242.6 1.3 convert_element_type.27
  243.9 0.8 convert_element_type.28
  244.8 0.0 copy-done.3
  244.8 0.7 copy.32
  245.5 0.0 copy-done.2
  245.5 0.7 copy.33
  (3 shorter events, 0.0 us)
Async XLA Ops:
  169.8 1.3 copy-start
  171.1 0.8 copy-start.1
  242.6 2.1 copy-start.3
  242.6 2.9 %copy-start.2 = (bf16[144,1024]{1,0:T(8,128)(2,1)S(1)}, bf16[144,1024]{1,0:T(8,128)(2,1)}, u32[]{:S(2)}) copy-start(bf16[144,1024]{1,0:T(8,128)(2,1)} %get-tuple-element.26) | copy-start | bytes 884740

commit v4 on v3

--- a/solution.py
+++ b/solution.py
@@ -69,6 +69,7 @@
         self.twin = {"replica": r + 1 - 2 * self.core}
         self.up = {"replica": base + lax.rem(self.y + 1, 4) * 2}
         self.down = {"replica": base + lax.rem(self.y + 3, 4) * 2}
+        self.facing = {"replica": base + lax.rem(self.y + 2, 4) * 2}
         self.beside = {"replica": r + 8 - 16 * zlow}
         self.peers = [{"shard": lax.rem(self.s + k, 8)} for k in range(1, 8)]
 
@@ -95,6 +96,11 @@
             made.wait_send()
         self.open = []
 
+    def settle(self, copies):
+        for made in copies:
+            made.wait_send()
+            self.open = [other for other in self.open if other is not made]
+
     def barrier(self, others):
         semaphore = pltpu.get_barrier_semaphore()
         for other in others:
@@ -210,6 +216,106 @@
         )
 
 
+class Reduce:
+    def __init__(self, net, grad, pair, ring, out, turned=None):
+        self.net, self.grad, self.out, self.turned = net, grad, out, turned
+        self.sent, self.work = pair
+        self.near_in, self.far_in, self.passed, self.kept, self.came = ring
+        width = grad.shape[-1]
+        cut = max(width // 256, 1) * 128 if width != 384 else 256
+        self.one, self.two = pl.ds(0, cut), pl.ds(cut, width - cut)
+        self.mine = pl.ds(net.core * 4, 4)
+        self.q = net.core * 4 + net.y
+        self.at_up, self.at_facing, self.at_down = (lax.rem(net.y + k, 4) for k in (1, 2, 3))
+
+    def core(self):
+        net = self.net
+        self.moved = net.copy(self.grad.at[pl.ds((1 - net.core) * 4, 4)], self.sent, net.twin)
+
+    def ring(self):
+        net, work, near, far = self.net, self.work, self.near_in, self.far_in
+        one, two = self.one, self.two
+        self.moved.wait_recv()
+        work[...] = add(self.grad[self.mine], self.sent[...]).astype(BF16)
+        self.fars = [
+            net.copy(work.at[self.at_facing, :, one], far.at[:, one], net.up),
+            net.copy(work.at[self.at_facing, :, two], far.at[:, two], net.down),
+        ]
+        self.nears = [
+            net.copy(work.at[self.at_up, :, two], near.at[:, two], net.up),
+            net.copy(work.at[self.at_down, :, one], near.at[:, one], net.down),
+        ]
+
+    def relay(self):
+        net, far = self.net, self.far_in
+        steps = ((self.one, self.at_up, net.up), (self.two, self.at_down, net.down))
+        for k, (part, block, to) in enumerate(steps):
+            self.fars[k].wait_recv()
+            far[:, part] = add(far[:, part], self.work[block, :, part]).astype(BF16)
+            self.nears.append(net.copy(far.at[:, part], self.passed.at[:, part], to))
+
+    def beside(self):
+        net = self.net
+        for made in self.nears:
+            made.wait_recv()
+        self.kept[...] = add(self.work[net.y], self.near_in[...], self.passed[...]).astype(BF16)
+        self.over = net.copy(self.kept, self.came, net.beside)
+
+    def place(self, q, eighths=1):
+        rows = self.out.shape[0] // 8
+        return pl.ds(pl.multiple_of(q * rows, 16), rows * eighths)
+
+    def cross(self):
+        net = self.net
+        self.over.wait_recv()
+        total = add(self.kept[...], self.came[...]).astype(BF16)
+        if self.turned is None:
+            self.out[self.place(self.q)] = total
+            return
+        away, back = self.turned
+        away[...] = total.reshape(away.shape)
+        self.crossed = [
+            net.copy(away.at[to["shard"]], back.at[net.s], to) for to in net.peers
+        ]
+        back[net.s] = away[net.s]
+
+    def back(self):
+        net, out = self.net, self.out
+        own = self.place(self.q)
+        if self.turned is not None:
+            for made in self.crossed:
+                made.wait_recv()
+            incoming = self.turned[1]
+            blocks = [incoming[t] for t in range(8)]
+            width = blocks[0].shape[-1]
+            for i in range(width // 128 if width == 384 else 1):
+                size = 128 if width == 384 else width
+                for t in range(8):
+                    at = i * D + t * size
+                    out[own, at : at + size] = blocks[t][:, i * 128 : i * 128 + size]
+        part = out.at[own]
+        self.shared = [net.copy(part, part, net.up), net.copy(part, part, net.down)]
+
+    def back_relay(self):
+        net, out = self.net, self.out
+        half = out.shape[1] // 2
+        self.lasts = []
+        steps = ((0, self.at_down, net.up), (half, self.at_up, net.down))
+        for k, (at, block, to) in enumerate(steps):
+            self.shared[k].wait_recv()
+            part = out.at[self.place(net.core * 4 + block), pl.ds(at, half)]
+            self.lasts.append(net.copy(part, part, to))
+
+    def swap(self):
+        for made in self.lasts:
+            made.wait_recv()
+        part = self.out.at[self.place(self.net.core * 4, 4)]
+        self.ended = self.net.copy(part, part, self.net.twin)
+
+    def end(self):
+        self.ended.wait_recv()
+
+
 def layer_kernel(
     tokens,
     cotangent,
@@ -222,9 +328,15 @@
     up_bias,
     block_out,
     input_grad,
-    rows_grad,
-    columns_grad,
-    small_grad,
+    down_sum,
+    out_sum,
+    up_sum,
+    qkv_sum,
+    small_sum,
+    down_grad,
+    out_grad,
+    up_grad,
+    qkv_grad,
     all_vectors,
     columns,
     first,
@@ -252,18 +364,43 @@
     passed,
     kept,
     came,
+    small_low,
+    small_twin,
+    small_ring,
+    small_away,
+    small_came,
+    down_pair,
+    down_ring,
+    out_pair,
+    out_ring,
+    up_pair,
+    up_ring,
+    up_turned,
+    qkv_pair,
+    qkv_ring,
+    qkv_turned,
     send,
     recv,
 ):
     net = Net(send, recv)
     s, core = net.s, net.core
-    net.barrier([*net.peers, net.twin])
+    net.barrier([*net.peers, net.twin, net.up, net.down, net.facing, net.beside])
+
+    def reduce(grad, pair, ring, out, turned=None):
+        split = lambda ref, n: [ref.at[i] for i in range(n)]
+        turned = None if turned is None else split(turned, 2)
+        return Reduce(net, grad, split(pair, 2), split(ring, 5), out, turned)
+
+    down_all = reduce(down_grad, down_pair, down_ring, down_sum)
+    out_all = reduce(out_grad, out_pair, out_ring, out_sum)
+    up_all = reduce(up_grad, up_pair, up_ring, up_sum, up_turned)
+    qkv_all = reduce(qkv_grad, qkv_pair, qkv_ring, qkv_sum, qkv_turned)
     source = [lax.rem(s + 8 - k, 8) for k in range(1, 8)]
     mine = pl.ds(pl.multiple_of(core * 64, 64), 64)
 
     def scatter(i):
-        buffers = (parts, hop, side, near, far, passed, kept, came)
-        return Scatter(net, *(buffer.at[i] for buffer in buffers))
+        buffers = (hop, side, near, far, passed, kept, came)
+        return Scatter(net, parts.at[i % 3], *(buffer.at[i] for buffer in buffers))
 
     def each(work, least, end, carry=0):
         def step(i, carry):
@@ -385,7 +522,7 @@
         parts[0, b] = dot(value, out_weight[...]).astype(BF16)
         return carry
 
-    rs = scatter(0)
+    rs = rs_branch = scatter(0)
     each_sent(rs, outward, 0)
     rs.over()
     rs.relay()
@@ -430,8 +567,8 @@
     own = pl.ds(pl.multiple_of(s * 128, 128), 128)
     small[...] = jnp.zeros_like(small)
     for i in range(4):
-        small[8 + i : 9 + i, 0:128] = up_bias_grad[:, i * 128 : (i + 1) * 128]
-    small[7:8, 0:128] = jnp.sum(cot[:, :, own].astype(F32).reshape(1152, 128), 0, keepdims=True)
+        small[8 + i : 9 + i, :] = up_bias_grad[:, i * 128 : (i + 1) * 128]
+    small[7:8, :] = jnp.sum(cot[:, :, own].astype(F32).reshape(1152, 128), 0, keepdims=True)
 
     def down_tile(i):
         at = pl.ds(i * 256, 256)
@@ -439,7 +576,7 @@
             active[...].reshape(1152, 512), cot[:, :, at].reshape(1152, 256)
         ).astype(BF16)
         for q in range(8):
-            rows_grad[q, 0:64, at] = value[q * 64 : (q + 1) * 64]
+            down_grad[q, :, at] = value[q * 64 : (q + 1) * 64]
 
     down_tile(0)
     rs.far()
@@ -448,6 +585,7 @@
     rs.relay()
     down_tile(2)
     down_tile(3)
+    down_all.core()
     grad_second = rs.finish()
     unit2, inverse2 = norm_unit(resid_ref[...])
     grad_resid = cotangent[...].astype(F32) + norm_back(grad_second, unit2, inverse2, gain2)
@@ -464,21 +602,24 @@
         ).astype(BF16)
         for j in range(2):
             for q in range(8):
-                columns_grad[q, (2 * i + j) * 16 : (2 * i + j + 1) * 16, 384:896] = value[
+                up_grad[q, (2 * i + j) * 16 : (2 * i + j + 1) * 16, :] = value[
                     j * 128 + q * 16 : j * 128 + (q + 1) * 16
                 ]
 
     ag.relay_one()
+    down_all.ring()
     up_tile(0)
     ag.relay_two()
     ag.row()
     up_tile(1)
+    down_all.relay()
     up_tile(2)
     ag.finish()
     rs_out = scatter(2)
     rs_out.hop()
     rs_out.side()
     rs_out.near()
+    down_all.beside()
 
     def back_heads(b, carry):
         value = dot_last(branch[b], out_weight[...])
@@ -489,7 +630,14 @@
 
     each(back_heads, 0, 8)
     up_tile(3)
+    value = dot_first(attended[...].reshape(1152, 128), branch[...].reshape(1152, D)).astype(BF16)
+    for q in range(8):
+        out_grad[q] = value[q * 16 : (q + 1) * 16]
     rs_out.far()
+    up_all.core()
+    out_all.core()
+    down_all.cross()
+    down_all.back()
 
     def attend_back(image, carry):
         q, k, v = (qkv_low[image, :, i * 128 : (i + 1) * 128] for i in range(3))
@@ -511,21 +659,28 @@
         mixed[image, :, 256:384] = dv
         return carry
 
-    lax.fori_loop(0, 2, attend_back, 0)
+    lax.fori_loop(0, 1, attend_back, 0)
+    up_all.ring()
+    out_all.ring()
     rs_out.over()
+    lax.fori_loop(1, 2, attend_back, 0)
     rs_out.relay()
+    down_all.back_relay()
+    up_all.relay()
+    out_all.relay()
 
     def back_first(b, total):
         value = by_device(mixed, b)
         grad_qkv[b] = value
-        parts[3, b] = dot_last(value, columns[:, :, 0:384].reshape(D, 384)).astype(BF16)
+        parts[0, b] = dot_last(value, columns[:, :, 0:384].reshape(D, 384)).astype(BF16)
         return total + jnp.sum(value.astype(F32), 0, keepdims=True)
 
+    net.settle([rs_branch.hopped, *rs_branch.sides, *rs_branch.nears])
     rs = scatter(3)
     qkv_bias_grad = each_sent(rs, back_first, jnp.zeros((1, 384), F32))
-    small[4:5, 0:128] = qkv_bias_grad[:, 0:128]
-    small[5:6, 0:128] = qkv_bias_grad[:, 256:384]
-    small[6:7, 0:128] = jnp.sum(branch[:, :, own].astype(F32).reshape(1152, 128), 0, keepdims=True)
+    small[4:5, :] = qkv_bias_grad[:, 0:128]
+    small[5:6, :] = qkv_bias_grad[:, 256:384]
+    small[6:7, :] = jnp.sum(branch[:, :, own].astype(F32).reshape(1152, 128), 0, keepdims=True)
 
     def qkv_tile(i):
         value = dot_first(
@@ -534,20 +689,29 @@
         ).astype(BF16)
         for j in range(2):
             for q in range(8):
-                columns_grad[q, (2 * i + j) * 16 : (2 * i + j + 1) * 16, 0:384] = value[
+                qkv_grad[q, (2 * i + j) * 16 : (2 * i + j + 1) * 16, :] = value[
                     j * 128 + q * 16 : j * 128 + (q + 1) * 16
                 ]
 
     qkv_tile(0)
+    up_all.beside()
+    out_all.beside()
+    qkv_tile(1)
     rs.over()
-    qkv_tile(1)
+    qkv_tile(2)
+    down_all.swap()
+    qkv_tile(3)
+    qkv_all.core()
     rs.relay()
-    qkv_tile(2)
-    qkv_tile(3)
-    value = dot_first(attended[...].reshape(1152, 128), branch[...].reshape(1152, D)).astype(BF16)
-    for q in range(8):
-        rows_grad[q, 64:80, :] = value[q * 16 : (q + 1) * 16]
     block_out[...] = (resid_ref[...] + (rs_out.finish() + bias_down)).astype(BF16)
+    qkv_all.ring()
+    up_all.cross()
+    out_all.cross()
+    out_all.back()
+    qkv_all.relay()
+    up_all.back()
+    out_all.back_relay()
+    qkv_all.beside()
     grad_first = rs.finish()
     unit1, inverse1 = norm_unit(tokens[...].astype(F32))
     input_grad[...] = (
@@ -562,12 +726,31 @@
         fours[t] = four[:, t * 128 : (t + 1) * 128]
     moved = [net.copy(fours.at[to["shard"]], fours_in.at[s], to) for to in net.peers]
     fours_in[s] = fours[s]
+    qkv_all.cross()
+    up_all.back_relay()
+    out_all.swap()
     for made in moved:
         made.wait_recv()
     total = jnp.sum(fours_in[...].astype(F32), 0)
-    small[0:4, 0:128] = total[0:4]
-    small_grad[...] = jnp.zeros_like(small_grad)
-    small_grad[0] = small[...].astype(BF16)
+    small[0:4, :] = total[0:4]
+    small_low[...] = small[...].astype(BF16)
+    moved = net.copy(small_low, small_twin, net.twin)
+    qkv_all.back()
+    moved.wait_recv()
+    small_ring[net.y] = add(small_low[...], small_twin[...]).astype(BF16)
+    own = small_ring.at[net.y]
+    moved = [net.copy(own, own, to) for to in (net.up, net.down, net.facing)]
+    up_all.swap()
+    qkv_all.back_relay()
+    for made in moved:
+        made.wait_recv()
+    small_away[...] = add(*(small_ring[k] for k in range(4))).astype(BF16)
+    moved = net.copy(small_away, small_came, net.beside)
+    qkv_all.swap()
+    moved.wait_recv()
+    small_sum[...] = add(small_away[...], small_came[...]).astype(BF16)
+    for every in (down_all, out_all, up_all, qkv_all):
+        every.end()
     net.drain()
 
 
@@ -581,13 +764,19 @@
         out_shape=[
             shape(ROWS, D),
             shape(ROWS, D),
-            shape(8, 80, D),
-            shape(8, 128, 896),
-            shape(8, 16, 256),
+            shape(512, D),
+            shape(128, D),
+            shape(128, 4096),
+            shape(128, 3 * D),
+            shape(16, 128),
         ],
         in_specs=[space] * 9,
-        out_specs=[space] * 5,
+        out_specs=[space] * 7,
         scratch_shapes=[
+            vmem(8, 64, D),
+            vmem(8, 16, D),
+            vmem(8, 128, 512),
+            vmem(8, 128, 384),
             vmem(8, 16, 128),
             vmem(8, 128, 896),
             vmem(8, ROWS, D),
@@ -604,10 +793,10 @@
             vmem(8, ROWS, 384),
             wide(ROWS, D),
             wide(ROWS, D),
-            wide(16, 256),
+            wide(16, 128),
             vmem(8, 16, 128),
             vmem(8, 16, 128),
-            vmem(4, 8, ROWS, D),
+            vmem(3, 8, ROWS, D),
             vmem(4, ROWS, D),
             vmem(4, 2, ROWS, D),
             vmem(4, 2, ROWS, HALF),
@@ -615,154 +804,30 @@
             vmem(4, 2, ROWS, HALF),
             vmem(4, ROWS, D),
             vmem(4, ROWS, D),
-            pltpu.SemaphoreType.DMA((160,)),
-            pltpu.SemaphoreType.DMA((160,)),
+            vmem(16, 128),
+            vmem(16, 128),
+            vmem(4, 16, 128),
+            vmem(16, 128),
+            vmem(16, 128),
+            vmem(2, 4, 64, D),
+            vmem(5, 64, D),
+            vmem(2, 4, 16, D),
+            vmem(5, 16, D),
+            vmem(2, 4, 128, 512),
+            vmem(5, 128, 512),
+            vmem(2, 8, 16, 512),
+            vmem(2, 4, 128, 384),
+            vmem(5, 128, 384),
+            vmem(2, 8, 16, 384),
+            pltpu.SemaphoreType.DMA((240,)),
+            pltpu.SemaphoreType.DMA((240,)),
         ],
         name="layer",
         cost_estimate=pl.CostEstimate(
             flops=11 * 10**9, bytes_accessed=12 * 10**6, transcendentals=0
         ),
         compiler_params=pltpu.CompilerParams(
-            collective_id=1, has_side_effects=True, vmem_limit_bytes=60 << 20
-        ),
-    )(*arguments)
-
-
-def sum_kernel(*refs):
-    inputs, refs = refs[:3], refs[3:]
-    outs, refs = refs[:5], refs[5:]
-    sent, refs = refs[:3], refs[3:]
-    work, refs = refs[:3], refs[3:]
-    far, near, passed = refs[:3], refs[3:6], refs[6:9]
-    kept, came, final = refs[9:12], refs[12:15], refs[15:18]
-    turned, send, recv = refs[18:]
-    net = Net(send, recv)
-    net.barrier([net.twin, net.up, net.down, net.beside, *net.peers])
-    core, y, s = net.core, net.y, net.s
-    half = [512, 512, 128]
-    width = [D, 896, 256]
-    mine = pl.ds(core * 4, 4)
-    up, down, facing = (lax.rem(y + k, 4) for k in (1, 3, 2))
-    q = core * 4 + y
-
-    moved = [net.copy(a.at[pl.ds((1 - core) * 4, 4)], b, net.twin) for a, b in zip(inputs, sent)]
-    for i in range(3):
-        moved[i].wait_recv()
-        work[i][...] = add(inputs[i][mine], sent[i][...]).astype(BF16)
-
-    halves = [(pl.ds(0, n), pl.ds(n, w - n)) for n, w in zip(half, width)]
-    fars, nears, passes = [], [], []
-    for i in range(3):
-        one, two = halves[i]
-        fars.append(
-            (
-                net.copy(work[i].at[facing, :, one], far[i].at[:, one], net.up),
-                net.copy(work[i].at[facing, :, two], far[i].at[:, two], net.down),
-            )
-        )
-    for i in range(3):
-        one, two = halves[i]
-        nears.append(
-            (
-                net.copy(work[i].at[up, :, two], near[i].at[:, two], net.up),
-                net.copy(work[i].at[down, :, one], near[i].at[:, one], net.down),
-            )
-        )
-    for i in range(3):
-        made = []
-        for k, (block, to) in enumerate(((up, net.up), (down, net.down))):
-            fars[i][k].wait_recv()
-            part = halves[i][k]
-            far[i][:, part] = add(far[i][:, part], work[i][block, :, part]).astype(BF16)
-            made.append(net.copy(far[i].at[:, part], passed[i].at[:, part], to))
-        passes.append(made)
-    over = []
-    for i in range(3):
-        for made in (*nears[i], *passes[i]):
-            made.wait_recv()
-        kept[i][...] = add(work[i][y], near[i][...], passed[i][...]).astype(BF16)
-        over.append(net.copy(kept[i], came[i], net.beside))
-    over[1].wait_recv()
-    turned[...] = add(kept[1][...], came[1][...]).astype(BF16).reshape(8, 16, 896)
-    place = lambda t: pl.ds(pl.multiple_of(t * 16, 16), 16)
-    crossed = [
-        net.copy(turned.at[to["shard"]], final[1].at[q, place(s)], to) for to in net.peers
-    ]
-    final[1][q, place(s)] = turned[s]
-    for i in (0, 2):
-        over[i].wait_recv()
-        final[i][q] = add(kept[i][...], came[i][...]).astype(BF16)
-    for made in crossed:
-        made.wait_recv()
-
-    steps = []
-    for i in range(3):
-        own = final[i].at[q]
-        steps.append((net.copy(own, own, net.up), net.copy(own, own, net.down)))
-    lasts = []
-    for i in range(3):
-        one, two = halves[i]
-        steps[i][0].wait_recv()
-        part = final[i].at[core * 4 + down, :, one]
-        lasts.append(net.copy(part, part, net.up))
-        steps[i][1].wait_recv()
-        part = final[i].at[core * 4 + up, :, two]
-        lasts.append(net.copy(part, part, net.down))
-    ends = []
-    for i in range(3):
-        lasts[2 * i].wait_recv()
-        lasts[2 * i + 1].wait_recv()
-        part = final[i].at[mine]
-        ends.append(net.copy(part, part, net.twin))
-    for made in ends:
-        made.wait_recv()
-    qkv_grad, out_grad, up_grad, down_grad, small = outs
-    for k in range(8):
-        down_grad[k * 64 : (k + 1) * 64, :] = final[0][k, 0:64, :]
-        out_grad[k * 16 : (k + 1) * 16, :] = final[0][k, 64:80, :]
-        rows = slice(k * 16, (k + 1) * 16)
-        for t in range(8):
-            block = final[1][k, t * 16 : (t + 1) * 16, :]
-            up_grad[rows, t * 512 : (t + 1) * 512] = block[:, 384:896]
-            for i in range(3):
-                at = i * D + t * 128
-                qkv_grad[rows, at : at + 128] = block[:, i * 128 : (i + 1) * 128]
-    small[...] = final[2][0]
-    net.drain()
-
-
-def sum_replicas(*arguments):
-    space = pl.BlockSpec(memory_space=pltpu.VMEM)
-    shape = lambda *sizes: jax.ShapeDtypeStruct(sizes, BF16)
-    sizes = ((80, D), (128, 896), (16, 256))
-    vmem = lambda *lead: [pltpu.VMEM((*lead, *size), BF16) for size in sizes]
-    return pl.pallas_call(
-        sum_kernel,
-        out_shape=[
-            shape(128, 3 * D),
-            shape(128, D),
-            shape(128, 4096),
-            shape(512, D),
-            shape(16, 256),
-        ],
-        in_specs=[space] * 3,
-        out_specs=[space] * 5,
-        scratch_shapes=[
-            *vmem(4),
-            *vmem(4),
-            *vmem(),
-            *vmem(),
-            *vmem(),
-            *vmem(),
-            *vmem(),
-            *vmem(8),
-            pltpu.VMEM((8, 16, 896), BF16),
-            pltpu.SemaphoreType.DMA((64,)),
-            pltpu.SemaphoreType.DMA((64,)),
-        ],
-        name="sum_replicas",
-        compiler_params=pltpu.CompilerParams(
-            collective_id=2, has_side_effects=True, vmem_limit_bytes=48 << 20
+            collective_id=1, has_side_effects=True, vmem_limit_bytes=62 << 20
         ),
     )(*arguments)
 
@@ -788,7 +853,7 @@
     vectors = jnp.pad(vectors, ((0, 10), (0, 0)))
     zeros = jnp.zeros((128,), F32)
     qkv_bias = jnp.concatenate([query_bias.astype(F32), zeros, value_bias.astype(F32)])
-    block_out, input_grad, *grads = layer(
+    block_out, input_grad, *sums = layer(
         tokens.reshape(ROWS, D),
         cotangent.reshape(ROWS, D),
         vectors,
@@ -799,9 +864,7 @@
         qkv_bias.reshape(1, 384),
         up_bias.astype(F32).reshape(1, 512),
     )
-    sums = [a.astype(F32) for a in sum_replicas(*grads)]
-    qkv_grad, out_grad, up_grad, down_grad, small = sums
-    small = small[:, :128]
+    down_grad, out_grad, up_grad, qkv_grad, small = (a.astype(F32) for a in sums)
     return (
         block_out.reshape(2, 72, D),
         input_grad.reshape(2, 72, D),

time: 246 us -> 213 us (0.87)
  Pallas kernels: 231 us -> 198 us
    pallas_call x1 -> x0, Pallas kernels: 66.4 us -> none  [sum_replicas(): pl.pallas_call(sum_kernel, out_shape=[shape(128, 3 * D), shape(128, D), s...]
    pallas_call x1, Pallas kernels: 165 us -> 198 us  [layer(): pl.pallas_call(layer_kernel, out_shape=[shape(ROWS, D), shape(ROWS, D), s...]
where the time goes in v4:
time: 213 us
  Pallas kernels  198 us (93%)
  other arithmetic  9.81 us (5%)
  local copies, waits for them, and re-layouts  4.5 us (2%)
    pallas_call x1, Pallas kernels, layer(): pl.pallas_call(layer_kernel, out_shape=[shape(ROWS, D), shape(ROWS, D), s...  198 us
    convert_element_type x5, other arithmetic, body(): a.astype(F32)  7.22 us

profile of v4, /device:TPU:1, one launch (start us, length us, event | category | flops | bytes accessed | tf_op | source)
XLA Modules:
  0.0 212.7 jit_solution(7036503930634089603)
XLA Ops:
  0.6 0.8 stack.27
  1.4 0.6 pad.4.vectors
  2.0 0.7 convert_element_type.24
  2.7 0.7 convert_element_type.25
  3.3 0.6 reshape.55.qkv_bias
  3.9 1.3 reshape.61
  5.2 197.7 %layer.1 = (bf16[144,1024]{1,0:T(8,128)(2,1)}, bf16[144,1024]{1,0:T(8,128)(2,1)}, bf16[512,1024]{1,0:T(8,128)(2,1)}, bf16[128,1024]{1,0:T(8,128)(2,1)}, bf16[128...) custom-call(bf16[144,1024]{1,0:T(8,128)(2,1)} %bitcast.38, bf16[144,1024]{1,0:T(8,128)(2,1)} %bitcast.39, ...), custom_call_target="tpu_custom_call" | custom-call | flops 11000000512 | bytes 12000000 | tf_op jit(solution)/shard_map/layer/pallas_call | solution.py:762
  202.9 0.0 copy-start
  202.9 0.8 convert_element_type.26
  203.7 0.5 slice_bitcast_fusion.1
  204.2 0.6 slice_bitcast_fusion
  204.8 2.8 %convert_element_type.29 = f32[128,4096]{1,0:T(8,128)} convert(bf16[128,4096]{1,0:T(8,128)(2,1)} %get-tuple-element.27) | non-fusion elementwise | flops 524288 | bytes 3145728 | tf_op jit(solution)/shard_map/convert_element_type | solution.py:867
  207.6 0.0 copy-start.1
  207.6 0.0 copy-done
  207.6 0.0 copy-start.4
  207.6 1.6 convert_element_type.30
  209.1 0.0 copy-start.3
  209.1 0.0 copy-start.2
  209.1 0.0 copy-done.1
  209.1 1.3 convert_element_type.27
  210.4 0.0 copy-done.4
  210.4 0.8 convert_element_type.28
  211.3 0.0 copy-done.3
  211.3 0.7 copy.32
  212.0 0.0 copy-done.2
  212.0 0.7 copy.33
  (2 shorter events, 0.0 us)
Async XLA Ops:
  202.9 4.7 %copy-start = (bf16[512,1024]{1,0:T(8,128)(2,1)S(1)}, bf16[512,1024]{1,0:T(8,128)(2,1)}, u32[]{:S(2)}) copy-start(bf16[512,1024]{1,0:T(8,128)(2,1)} %get-tuple-element.28) | copy-start | bytes 3145732
  207.6 1.6 copy-start.1
  207.6 2.9 %copy-start.4 = (bf16[128,1024]{1,0:T(8,128)(2,1)S(1)}, bf16[128,1024]{1,0:T(8,128)(2,1)}, u32[]{:S(2)}) copy-start(bf16[128,1024]{1,0:T(8,128)(2,1)} %get-tuple-element.26) | copy-start | bytes 786436
  209.1 2.2 %copy-start.3 = (bf16[144,1024]{1,0:T(8,128)(2,1)S(1)}, bf16[144,1024]{1,0:T(8,128)(2,1)}, u32[]{:S(2)}) copy-start(bf16[144,1024]{1,0:T(8,128)(2,1)} %get-tuple-element.22) | copy-start | bytes 884740
  209.1 2.9 %copy-start.2 = (bf16[144,1024]{1,0:T(8,128)(2,1)S(1)}, bf16[144,1024]{1,0:T(8,128)(2,1)}, u32[]{:S(2)}) copy-start(bf16[144,1024]{1,0:T(8,128)(2,1)} %get-tuple-element.23) | copy-start | bytes 884740

commit v5 on v4

--- a/solution.py
+++ b/solution.py
@@ -71,6 +71,8 @@
         self.down = {"replica": base + lax.rem(self.y + 3, 4) * 2}
         self.facing = {"replica": base + lax.rem(self.y + 2, 4) * 2}
         self.beside = {"replica": r + 8 - 16 * zlow}
+        self.replicas = [{"replica": lax.rem(r + k, 16)} for k in range(1, 16)]
+        self.r = r
         self.peers = [{"shard": lax.rem(self.s + k, 8)} for k in range(1, 8)]
 
     def at(self, h, x):
@@ -324,8 +326,6 @@
     up_weight,
     out_weight,
     down_weight,
-    qkv_bias,
-    up_bias,
     block_out,
     input_grad,
     down_sum,
@@ -365,10 +365,7 @@
     kept,
     came,
     small_low,
-    small_twin,
     small_ring,
-    small_away,
-    small_came,
     down_pair,
     down_ring,
     out_pair,
@@ -384,7 +381,7 @@
 ):
     net = Net(send, recv)
     s, core = net.s, net.core
-    net.barrier([*net.peers, net.twin, net.up, net.down, net.facing, net.beside])
+    net.barrier([*net.peers, *net.replicas])
 
     def reduce(grad, pair, ring, out, turned=None):
         split = lambda ref, n: [ref.at[i] for i in range(n)]
@@ -395,8 +392,8 @@
     out_all = reduce(out_grad, out_pair, out_ring, out_sum)
     up_all = reduce(up_grad, up_pair, up_ring, up_sum, up_turned)
     qkv_all = reduce(qkv_grad, qkv_pair, qkv_ring, qkv_sum, qkv_turned)
-    source = [lax.rem(s + 8 - k, 8) for k in range(1, 8)]
     mine = pl.ds(pl.multiple_of(core * 64, 64), 64)
+    sixteen = pl.ds(pl.multiple_of(core * 64 + net.y * 16, 16), 16)
 
     def scatter(i):
         buffers = (hop, side, near, far, passed, kept, came)
@@ -426,23 +423,34 @@
     vec = [net.copy(vectors, all_vectors.at[s], to) for to in net.peers]
     all_vectors[s] = vectors[...]
     qkv_in, up_in = [], []
-    for k, to in enumerate(net.peers):
-        t = to["shard"]
-        qkv_in.append(
-            [
-                net.copy(
-                    qkv_weight.at[mine, pl.ds(pl.multiple_of(i * D + t * 128, 128), 128)],
-                    columns.at[s, mine, pl.ds(i * 128, 128)],
-                    to,
-                )
-                for i in range(3)
-            ]
-        )
+    thirds = [
+        lambda t, i=i: qkv_weight.at[sixteen, pl.ds(pl.multiple_of(i * D + t * 128, 128), 128)]
+        for i in range(3)
+    ]
+    quarter = lambda t: up_weight.at[sixteen, pl.ds(pl.multiple_of(t * 512, 512), 512)]
+    for to in net.peers:
+        for i in range(3):
+            there = columns.at[s, sixteen, pl.ds(i * 128, 128)]
+            qkv_in.append(net.copy(thirds[i](to["shard"]), there, to))
+    for to in net.peers:
+        there = columns.at[s, sixteen, pl.ds(384, 512)]
+        up_in.append(net.copy(quarter(to["shard"]), there, to))
     for i in range(3):
-        columns[s, :, i * 128 : (i + 1) * 128] = qkv_weight[
-            :, pl.ds(pl.multiple_of(i * D + s * 128, 128), 128)
-        ]
-    columns[s, :, 384:896] = up_weight[:, pl.ds(pl.multiple_of(s * 512, 512), 512)]
+        columns[s, sixteen, i * 128 : (i + 1) * 128] = thirds[i](s)[...]
+    columns[s, sixteen, 384:896] = quarter(s)[...]
+
+    def share(arrived, at):
+        for made in arrived:
+            made.wait_recv()
+        part = columns.at[:, sixteen, at]
+        return [net.copy(part, part, to) for to in (net.up, net.down, net.facing)]
+
+    def share_twin(arrived, at):
+        for made in arrived:
+            made.wait_recv()
+        part = columns.at[:, mine, at]
+        return net.copy(part, part, net.twin)
+
     cot[s] = cotangent[...]
     x = tokens[...].astype(F32)
     unit1, inverse1 = norm_unit(x)
@@ -454,28 +462,20 @@
     )
     first[s] = (unit1 * gain1 + shift1).astype(BF16)
     ag = Gather(net, first)
-    qkv_pass = []
-    for k in range(7):
-        for made in qkv_in[k]:
-            made.wait_recv()
-        block = columns.at[source[k], mine, pl.ds(0, 384)]
-        qkv_pass.append(net.copy(block, block, net.twin))
+    qkv_at, up_at = pl.ds(0, 384), pl.ds(384, 512)
+    qkv_in = share(qkv_in, qkv_at)
     ag.relay_one()
+    up_in = share(up_in, up_at)
     ag.relay_two()
-    for k, to in enumerate(net.peers):
-        up_in.append(
-            net.copy(
-                up_weight.at[mine, pl.ds(pl.multiple_of(to["shard"] * 512, 512), 512)],
-                columns.at[s, mine, pl.ds(384, 512)],
-                to,
-            )
-        )
-    for made in qkv_pass:
-        made.wait_recv()
+    qkv_pass = share_twin(qkv_in, qkv_at)
+    own = vectors[...].astype(F32)
+    qkv_bias = jnp.concatenate([own[6:7], jnp.zeros((1, 128), F32), own[7:8]], axis=1)
+    up_bias = jnp.concatenate([own[k : k + 1] for k in range(8, 12)], axis=1)
+    qkv_pass.wait_recv()
     ag.row()
 
     def project(b, carry):
-        value = dot(first[b], columns[:, :, 0:384].reshape(D, 384)) + qkv_bias[...]
+        value = dot(first[b], columns[:, :, 0:384].reshape(D, 384)) + qkv_bias
         at = pl.multiple_of(b * 72, 8)
         mixed[0, pl.ds(at, 72), :] = value[0:72]
         mixed[1, pl.ds(at, 72), :] = value[72:144]
@@ -504,12 +504,7 @@
         return carry
 
     lax.fori_loop(0, 2, attend, 0)
-    ag_cot.relay_two()
-    up_pass = []
-    for k in range(7):
-        up_in[k].wait_recv()
-        block = columns.at[source[k], mine, pl.ds(384, 512)]
-        up_pass.append(net.copy(block, block, net.twin))
+    up_pass = share_twin(up_in, up_at)
 
     def by_device(ref, b):
         at = pl.multiple_of(b * 72, 8)
@@ -526,19 +521,17 @@
     each_sent(rs, outward, 0)
     rs.over()
     rs.relay()
+    ag_cot.relay_two()
     resid = tokens[...].astype(F32) + (rs.finish() + bias_out)
     resid_ref[...] = resid
     unit2, inverse2 = norm_unit(resid)
     second[s] = (unit2 * gain2 + shift2).astype(BF16)
     ag = Gather(net, second)
-    ag_cot.row()
-    ag_cot.finish()
-    for made in up_pass:
-        made.wait_recv()
+    up_pass.wait_recv()
 
     def feed(b, total):
         up = columns[:, :, 384:896].reshape(D, 512)
-        u = dot(second[b], up) + up_bias[...]
+        u = dot(second[b], up) + up_bias
         square = u * u
         t = jnp.tanh(GELU * (u + 0.044715 * u * square))
         act = (0.5 * u * (1.0 + t)).astype(BF16)
@@ -553,6 +546,8 @@
         return total + jnp.sum(gu.astype(F32), 0, keepdims=True)
 
     ag.relay_one()
+    ag_cot.row()
+    ag_cot.finish()
     up_bias_grad = each(feed, 0, 1, jnp.zeros((1, 512), F32))
     ag.relay_two()
     ag.row()
@@ -734,21 +729,15 @@
     total = jnp.sum(fours_in[...].astype(F32), 0)
     small[0:4, :] = total[0:4]
     small_low[...] = small[...].astype(BF16)
-    moved = net.copy(small_low, small_twin, net.twin)
+    moved = [net.copy(small_low, small_ring.at[net.r], to) for to in net.replicas]
+    small_ring[net.r] = small_low[...]
     qkv_all.back()
-    moved.wait_recv()
-    small_ring[net.y] = add(small_low[...], small_twin[...]).astype(BF16)
-    own = small_ring.at[net.y]
-    moved = [net.copy(own, own, to) for to in (net.up, net.down, net.facing)]
     up_all.swap()
     qkv_all.back_relay()
     for made in moved:
         made.wait_recv()
-    small_away[...] = add(*(small_ring[k] for k in range(4))).astype(BF16)
-    moved = net.copy(small_away, small_came, net.beside)
+    small_sum[...] = add(*(small_ring[k] for k in range(16)))
     qkv_all.swap()
-    moved.wait_recv()
-    small_sum[...] = add(small_away[...], small_came[...]).astype(BF16)
     for every in (down_all, out_all, up_all, qkv_all):
         every.end()
     net.drain()
@@ -768,9 +757,9 @@
             shape(128, D),
             shape(128, 4096),
             shape(128, 3 * D),
-            shape(16, 128),
+            jax.ShapeDtypeStruct((16, 128), F32),
         ],
-        in_specs=[space] * 9,
+        in_specs=[space] * 7,
         out_specs=[space] * 7,
         scratch_shapes=[
             vmem(8, 64, D),
@@ -805,10 +794,7 @@
             vmem(4, ROWS, D),
             vmem(4, ROWS, D),
             vmem(16, 128),
-            vmem(16, 128),
-            vmem(4, 16, 128),
-            vmem(16, 128),
-            vmem(16, 128),
+            vmem(16, 16, 128),
             vmem(2, 4, 64, D),
             vmem(5, 64, D),
             vmem(2, 4, 16, D),
@@ -832,6 +818,36 @@
     )(*arguments)
 
 
+def cast_kernel(down, out, up, qkv, small, *outs):
+    for source, target in zip((down, out, up, qkv), outs[:4]):
+        target[...] = source[...].astype(F32)
+    for k, target in enumerate(outs[4:12]):
+        target[...] = small[k]
+    for k in range(4):
+        outs[12][k * 128 : (k + 1) * 128] = small[8 + k]
+
+
+def cast(down, out, up, qkv, small):
+    steps = 4
+    block = lambda a: pl.BlockSpec((a.shape[0] // steps, a.shape[1]), lambda i: (i, 0))
+    whole = lambda *sizes: pl.BlockSpec(sizes, lambda i: (0,) * len(sizes))
+    shape = lambda *sizes: jax.ShapeDtypeStruct(sizes, F32)
+    large = (down, out, up, qkv)
+    return pl.pallas_call(
+        cast_kernel,
+        grid=(steps,),
+        out_shape=[
+            *(shape(*a.shape) for a in large),
+            *(shape(128) for _ in range(8)),
+            shape(512),
+        ],
+        in_specs=[*map(block, large), whole(16, 128)],
+        out_specs=[*map(block, large), *(whole(128) for _ in range(8)), whole(512)],
+        name="cast",
+        compiler_params=pltpu.CompilerParams(vmem_limit_bytes=62 << 20),
+    )(*large, small)
+
+
 def body(
     tokens,
     cotangent,
@@ -849,10 +865,9 @@
     down_weight,
     down_bias,
 ):
-    vectors = jnp.stack([attn_gain, attn_shift, mlp_gain, mlp_shift, out_bias, down_bias])
-    vectors = jnp.pad(vectors, ((0, 10), (0, 0)))
-    zeros = jnp.zeros((128,), F32)
-    qkv_bias = jnp.concatenate([query_bias.astype(F32), zeros, value_bias.astype(F32)])
+    vectors = [attn_gain, attn_shift, mlp_gain, mlp_shift, out_bias, down_bias]
+    vectors = [a.reshape(-1, 128) for a in (*vectors, query_bias, value_bias, up_bias)]
+    vectors = jnp.concatenate([*vectors, jnp.zeros((4, 128), BF16)], axis=0)
     block_out, input_grad, *sums = layer(
         tokens.reshape(ROWS, D),
         cotangent.reshape(ROWS, D),
@@ -861,10 +876,8 @@
         up_weight,
         out_weight,
         down_weight,
-        qkv_bias.reshape(1, 384),
-        up_bias.astype(F32).reshape(1, 512),
     )
-    down_grad, out_grad, up_grad, qkv_grad, small = (a.astype(F32) for a in sums)
+    down_grad, out_grad, up_grad, qkv_grad, *small, up_bias_grad = cast(*sums)
     return (
         block_out.reshape(2, 72, D),
         input_grad.reshape(2, 72, D),
@@ -878,7 +891,7 @@
         small[2],
         small[3],
         up_grad,
-        small[8:12].reshape(512),
+        up_bias_grad,
         down_grad,
         small[7],
     )

time: 213 us -> 199 us (0.934)
  other arithmetic: 9.81 us -> 0 us
  Pallas kernels: 198 us -> 194 us
    convert_element_type x7 -> x0, other arithmetic: 8.54 us -> none  [the longest x5 7.22 us: body(): a.astype(F32)]
    pallas_call x1, Pallas kernels: 198 us -> 189 us  [layer(): pl.pallas_call(layer_kernel, out_shape=[shape(ROWS, D), shape(ROWS, D), s...]
    pallas_call x0 -> x1, Pallas kernels: none -> 5.08 us  [cast(): pl.pallas_call(cast_kernel, grid=(steps,), out_shape=[*(shape(*a.shape) f...]
    concatenate x0 -> x1, local copies, waits for them, and re-layouts: none -> 2.65 us  [body(): vectors = jnp.concatenate([*vectors, jnp.zeros((4, 128), BF16)], axis=0)]
where the time goes in v5:
time: 199 us
  Pallas kernels  194 us (97%)
  local copies, waits for them, and re-layouts  4.09 us (2%)
    pallas_call x1, Pallas kernels, layer(): pl.pallas_call(layer_kernel, out_shape=[shape(ROWS, D), shape(ROWS, D), s...  189 us
    pallas_call x1, Pallas kernels, cast(): pl.pallas_call(cast_kernel, grid=(steps,), out_shape=[*(shape(*a.shape) f...  5.08 us

profile of v5, /device:TPU:1, one launch (start us, length us, event | category | flops | bytes accessed | tf_op | source)
XLA Modules:
  0.0 199.2 jit_solution(15045478423704143930)
XLA Ops:
  0.7 2.6 %concatenate.3.vectors = bf16[16,128]{1,0:T(8,128)(2,1)} concatenate(bf16[1,128]{1,0:T(2,128)(2,1)} %bitcast.16, bf16[1,128]{1,0:T(2,128)(2,1)} %bitcast.17, bf16[1,128]{1,0:T(2,128)(2,1)} %bitcast.18, bf16[1,128]{1,0:T(2,128)(2,1)} %bitcast.19, bf16[1,128]{1,0:T(2,128)(2,1)} %bitcast.20, bf16[1,128]{1,0:T(2,128)(2,1)} %bitcast.21, bf16[1,128]{1,0:T(2,128)(2,1)} %bitcast.22, ...), dimensions={0} | concatenate | bytes 8192 | tf_op jit(solution)/shard_map/concatenate | solution.py:870
  3.3 189.3 %layer.1 = (bf16[144,1024]{1,0:T(8,128)(2,1)}, bf16[144,1024]{1,0:T(8,128)(2,1)}, bf16[512,1024]{1,0:T(8,128)(2,1)}, bf16[128,1024]{1,0:T(8,128)(2,1)}, bf16[128...) custom-call(bf16[144,1024]{1,0:T(8,128)(2,1)} %bitcast.24, bf16[144,1024]{1,0:T(8,128)(2,1)} %bitcast.25, ...), custom_call_target="tpu_custom_call" | custom-call | flops 11000000512 | bytes 12000000 | tf_op jit(solution)/shard_map/layer/pallas_call | solution.py:751
  192.6 0.0 copy-start.1
  192.6 0.0 copy-start
  192.6 5.1 %cast.1 = (f32[512,1024]{1,0:T(8,128)}, f32[128,1024]{1,0:T(8,128)}, f32[128,4096]{1,0:T(8,128)}, f32[128,3072]{1,0:T(8,128)}, f32[128]{0:T(128)}, /*index=5*/f3...) custom-call(bf16[512,1024]{1,0:T(8,128)(2,1)} %get-tuple-element.37., ...), custom_call_target="tpu_custom_call" | custom-call | tf_op jit(solution)/shard_map/cast/pallas_call | solution.py:836
  197.7 0.0 copy-done.1
  197.7 0.7 copy.32
  198.4 0.0 copy-done
  198.4 0.7 copy.33
  (1 shorter events, 0.0 us)
Async XLA Ops:
  192.6 5.1 %copy-start.1 = (bf16[144,1024]{1,0:T(8,128)(2,1)S(1)}, bf16[144,1024]{1,0:T(8,128)(2,1)}, u32[]{:S(2)}) copy-start(bf16[144,1024]{1,0:T(8,128)(2,1)} %get-tuple-element.35) | copy-start | bytes 884740
  192.6 5.8 %copy-start = (bf16[144,1024]{1,0:T(8,128)(2,1)S(1)}, bf16[144,1024]{1,0:T(8,128)(2,1)}, u32[]{:S(2)}) copy-start(bf16[144,1024]{1,0:T(8,128)(2,1)} %get-tuple-element.36) | copy-start | bytes 884740

commit v6 on v5

--- a/solution.py
+++ b/solution.py
@@ -318,10 +318,17 @@
         self.ended.wait_recv()
 
 
-def layer_kernel(
+def layer_kernel(*refs):
+    layer_steps(*refs[:2], refs[2:8], *refs[8:])
+
+
+def layer_steps(
     tokens,
     cotangent,
-    vectors,
+    singles,
+    query_bias,
+    value_bias,
+    up_bias,
     qkv_weight,
     up_weight,
     out_weight,
@@ -337,6 +344,8 @@
     out_grad,
     up_grad,
     qkv_grad,
+    wide_vectors,
+    vectors,
     all_vectors,
     columns,
     first,
@@ -420,8 +429,14 @@
         rs.far()
         return each(work, 0, 1, carry)
 
+    wide_vectors[...] = jnp.zeros_like(wide_vectors)
+    for k, single in enumerate(singles):
+        wide_vectors[k : k + 1, :] = single[...].astype(F32)
+    vectors[...] = wide_vectors[...].astype(BF16)
     vec = [net.copy(vectors, all_vectors.at[s], to) for to in net.peers]
     all_vectors[s] = vectors[...]
+    cot[s] = cotangent[...]
+    ag_cot = Gather(net, cot)
     qkv_in, up_in = [], []
     thirds = [
         lambda t, i=i: qkv_weight.at[sixteen, pl.ds(pl.multiple_of(i * D + t * 128, 128), 128)]
@@ -451,7 +466,6 @@
         part = columns.at[:, mine, at]
         return net.copy(part, part, net.twin)
 
-    cot[s] = cotangent[...]
     x = tokens[...].astype(F32)
     unit1, inverse1 = norm_unit(x)
     for made in vec:
@@ -468,9 +482,10 @@
     up_in = share(up_in, up_at)
     ag.relay_two()
     qkv_pass = share_twin(qkv_in, qkv_at)
-    own = vectors[...].astype(F32)
-    qkv_bias = jnp.concatenate([own[6:7], jnp.zeros((1, 128), F32), own[7:8]], axis=1)
-    up_bias = jnp.concatenate([own[k : k + 1] for k in range(8, 12)], axis=1)
+    qkv_bias = jnp.concatenate(
+        [query_bias[...].astype(F32), jnp.zeros((1, 128), F32), value_bias[...].astype(F32)], axis=1
+    )
+    up_bias = up_bias[...].astype(F32)
     qkv_pass.wait_recv()
     ag.row()
 
@@ -482,11 +497,11 @@
         return carry
 
     each(project, 0, 5)
+    ag_cot.relay_one()
     ag.finish()
-    ag_cot = Gather(net, cot)
+    ag_cot.relay_two()
     each(project, 5, 8)
     qkv_low[...] = mixed[...].astype(BF16)
-    ag_cot.relay_one()
 
     def attend(image, carry):
         q, k, v = (qkv_low[image, :, i * 128 : (i + 1) * 128] for i in range(3))
@@ -521,7 +536,6 @@
     each_sent(rs, outward, 0)
     rs.over()
     rs.relay()
-    ag_cot.relay_two()
     resid = tokens[...].astype(F32) + (rs.finish() + bias_out)
     resid_ref[...] = resid
     unit2, inverse2 = norm_unit(resid)
@@ -601,39 +615,31 @@
                     j * 128 + q * 16 : j * 128 + (q + 1) * 16
                 ]
 
+    def back_heads(b, carry):
+        value = dot_last(branch[b], out_weight[...])
+        at = pl.multiple_of(b * 72, 8)
+        heads[0, pl.ds(at, 72), :] = value[0:72]
+        heads[1, pl.ds(at, 72), :] = value[72:144]
+        return carry
+
     ag.relay_one()
     down_all.ring()
     up_tile(0)
     ag.relay_two()
+    up_tile(1)
     ag.row()
-    up_tile(1)
     down_all.relay()
     up_tile(2)
+    up_tile(3)
+    up_all.core()
+    each(back_heads, 0, 5)
     ag.finish()
     rs_out = scatter(2)
     rs_out.hop()
     rs_out.side()
     rs_out.near()
     down_all.beside()
-
-    def back_heads(b, carry):
-        value = dot_last(branch[b], out_weight[...])
-        at = pl.multiple_of(b * 72, 8)
-        heads[0, pl.ds(at, 72), :] = value[0:72]
-        heads[1, pl.ds(at, 72), :] = value[72:144]
-        return carry
-
-    each(back_heads, 0, 8)
-    up_tile(3)
-    value = dot_first(attended[...].reshape(1152, 128), branch[...].reshape(1152, D)).astype(BF16)
-    for q in range(8):
-        out_grad[q] = value[q * 16 : (q + 1) * 16]
-    rs_out.far()
-    up_all.core()
-    out_all.core()
-    down_all.cross()
-    down_all.back()
-
+    each(back_heads, 5, 8)
     def attend_back(image, carry):
         q, k, v = (qkv_low[image, :, i * 128 : (i + 1) * 128] for i in range(3))
         grad = heads[image].astype(BF16)
@@ -656,13 +662,11 @@
 
     lax.fori_loop(0, 1, attend_back, 0)
     up_all.ring()
-    out_all.ring()
+    rs_out.far()
+    down_all.cross()
+    down_all.back()
+    lax.fori_loop(1, 2, attend_back, 0)
     rs_out.over()
-    lax.fori_loop(1, 2, attend_back, 0)
-    rs_out.relay()
-    down_all.back_relay()
-    up_all.relay()
-    out_all.relay()
 
     def back_first(b, total):
         value = by_device(mixed, b)
@@ -673,6 +677,9 @@
     net.settle([rs_branch.hopped, *rs_branch.sides, *rs_branch.nears])
     rs = scatter(3)
     qkv_bias_grad = each_sent(rs, back_first, jnp.zeros((1, 384), F32))
+    up_all.relay()
+    rs_out.relay()
+    down_all.back_relay()
     small[4:5, :] = qkv_bias_grad[:, 0:128]
     small[5:6, :] = qkv_bias_grad[:, 256:384]
     small[6:7, :] = jnp.sum(branch[:, :, own].astype(F32).reshape(1152, 128), 0, keepdims=True)
@@ -689,29 +696,33 @@
                 ]
 
     qkv_tile(0)
+    qkv_tile(1)
     up_all.beside()
-    out_all.beside()
-    qkv_tile(1)
-    rs.over()
     qkv_tile(2)
-    down_all.swap()
     qkv_tile(3)
     qkv_all.core()
-    rs.relay()
-    block_out[...] = (resid_ref[...] + (rs_out.finish() + bias_down)).astype(BF16)
+    value = dot_first(attended[...].reshape(1152, 128), branch[...].reshape(1152, D)).astype(BF16)
+    for q in range(8):
+        out_grad[q] = value[q * 16 : (q + 1) * 16]
+    out_all.core()
+    rs.over()
     qkv_all.ring()
     up_all.cross()
+    out_all.ring()
+    rs.relay()
+    down_all.swap()
+    qkv_all.relay()
+    out_all.relay()
+    up_all.back()
+    qkv_all.beside()
+    out_all.beside()
+    block_out[...] = (resid_ref[...] + (rs_out.finish() + bias_down)).astype(BF16)
+    up_all.back_relay()
+    qkv_all.cross()
     out_all.cross()
     out_all.back()
-    qkv_all.relay()
-    up_all.back()
-    out_all.back_relay()
-    qkv_all.beside()
     grad_first = rs.finish()
     unit1, inverse1 = norm_unit(tokens[...].astype(F32))
-    input_grad[...] = (
-        grad_resid_ref[...] + norm_back(grad_first, unit1, inverse1, gain1)
-    ).astype(BF16)
     gain1_grad = jnp.sum(grad_first * unit1, 0, keepdims=True)
     shift1_grad = jnp.sum(grad_first, 0, keepdims=True)
     four = jnp.concatenate(
@@ -721,9 +732,12 @@
         fours[t] = four[:, t * 128 : (t + 1) * 128]
     moved = [net.copy(fours.at[to["shard"]], fours_in.at[s], to) for to in net.peers]
     fours_in[s] = fours[s]
-    qkv_all.cross()
-    up_all.back_relay()
-    out_all.swap()
+    qkv_all.back()
+    input_grad[...] = (
+        grad_resid_ref[...] + norm_back(grad_first, unit1, inverse1, gain1)
+    ).astype(BF16)
+    out_all.back_relay()
+    up_all.swap()
     for made in moved:
         made.wait_recv()
     total = jnp.sum(fours_in[...].astype(F32), 0)
@@ -731,9 +745,8 @@
     small_low[...] = small[...].astype(BF16)
     moved = [net.copy(small_low, small_ring.at[net.r], to) for to in net.replicas]
     small_ring[net.r] = small_low[...]
-    qkv_all.back()
-    up_all.swap()
     qkv_all.back_relay()
+    out_all.swap()
     for made in moved:
         made.wait_recv()
     small_sum[...] = add(*(small_ring[k] for k in range(16)))
@@ -759,13 +772,15 @@
             shape(128, 3 * D),
             jax.ShapeDtypeStruct((16, 128), F32),
         ],
-        in_specs=[space] * 7,
+        in_specs=[space] * 15,
         out_specs=[space] * 7,
         scratch_shapes=[
             vmem(8, 64, D),
             vmem(8, 16, D),
             vmem(8, 128, 512),
             vmem(8, 128, 384),
+            wide(16, 128),
+            vmem(16, 128),
             vmem(8, 16, 128),
             vmem(8, 128, 896),
             vmem(8, ROWS, D),
@@ -828,7 +843,7 @@
 
 
 def cast(down, out, up, qkv, small):
-    steps = 4
+    steps = 8
     block = lambda a: pl.BlockSpec((a.shape[0] // steps, a.shape[1]), lambda i: (i, 0))
     whole = lambda *sizes: pl.BlockSpec(sizes, lambda i: (0,) * len(sizes))
     shape = lambda *sizes: jax.ShapeDtypeStruct(sizes, F32)
@@ -865,13 +880,12 @@
     down_weight,
     down_bias,
 ):
-    vectors = [attn_gain, attn_shift, mlp_gain, mlp_shift, out_bias, down_bias]
-    vectors = [a.reshape(-1, 128) for a in (*vectors, query_bias, value_bias, up_bias)]
-    vectors = jnp.concatenate([*vectors, jnp.zeros((4, 128), BF16)], axis=0)
+    vectors = (attn_gain, attn_shift, mlp_gain, mlp_shift, out_bias, down_bias)
+    vectors = (*vectors, query_bias, value_bias, up_bias)
     block_out, input_grad, *sums = layer(
         tokens.reshape(ROWS, D),
         cotangent.reshape(ROWS, D),
-        vectors,
+        *(a.reshape(1, -1) for a in vectors),
         qkv_weight,
         up_weight,
         out_weight,

time: 199 us -> 208 us (1.045)
  Pallas kernels: 194 us -> 204 us
    pallas_call x1, Pallas kernels: 189 us -> 197 us  [layer(): pl.pallas_call(layer_kernel, out_shape=[shape(ROWS, D), shape(ROWS, D), s...]
    concatenate x1 -> x0, local copies, waits for them, and re-layouts: 2.65 us -> none  [body(): vectors = jnp.concatenate([*vectors, jnp.zeros((4, 128), BF16)], axis=0)]
where the time goes in v6:
time: 208 us; the launch traced here: 207 us
  Pallas kernels  204 us (98%)
  local copies, waits for them, and re-layouts  2.7 us (1%)
    pallas_call x1, Pallas kernels, layer(): pl.pallas_call(layer_kernel, out_shape=[shape(ROWS, D), shape(ROWS, D), s...  197 us
    pallas_call x1, Pallas kernels, cast(): pl.pallas_call(cast_kernel, grid=(steps,), out_shape=[*(shape(*a.shape) f...  7.08 us

profile of v6, /device:TPU:1, one launch (start us, length us, event | category | flops | bytes accessed | tf_op | source)
XLA Modules:
  0.0 207.4 jit_solution(18343919068283963378)
XLA Ops:
  0.6 1.3 reshape.79.refs_10_
  1.9 196.9 %layer.1 = (bf16[144,1024]{1,0:T(8,128)(2,1)}, bf16[144,1024]{1,0:T(8,128)(2,1)}, bf16[512,1024]{1,0:T(8,128)(2,1)}, bf16[128,1024]{1,0:T(8,128)(2,1)}, bf16[128...) custom-call(bf16[144,1024]{1,0:T(8,128)(2,1)} %bitcast.14, bf16[144,1024]{1,0:T(8,128)(2,1)} %bitcast.15, ...), custom_call_target="tpu_custom_call" | custom-call | flops 11000000512 | bytes 12000000 | tf_op jit(solution)/shard_map/layer/pallas_call | solution.py:764
  198.8 0.0 copy-start.1
  198.8 0.0 copy-start
  198.9 7.1 %cast.1 = (f32[512,1024]{1,0:T(8,128)}, f32[128,1024]{1,0:T(8,128)}, f32[128,4096]{1,0:T(8,128)}, f32[128,3072]{1,0:T(8,128)}, f32[128]{0:T(128)}, /*index=5*/f3...) custom-call(bf16[512,1024]{1,0:T(8,128)(2,1)} %get-tuple-element.37., ...), custom_call_target="tpu_custom_call" | custom-call | tf_op jit(solution)/shard_map/cast/pallas_call | solution.py:851
  205.9 0.0 copy-done.1
  206.0 0.7 copy.32
  206.7 0.0 copy-done
  206.7 0.7 copy.33
Async XLA Ops:
  198.8 7.1 %copy-start.1 = (bf16[144,1024]{1,0:T(8,128)(2,1)S(1)}, bf16[144,1024]{1,0:T(8,128)(2,1)}, u32[]{:S(2)}) copy-start(bf16[144,1024]{1,0:T(8,128)(2,1)} %get-tuple-element.35) | copy-start | bytes 884740
  198.8 7.8 %copy-start = (bf16[144,1024]{1,0:T(8,128)(2,1)S(1)}, bf16[144,1024]{1,0:T(8,128)(2,1)}, u32[]{:S(2)}) copy-start(bf16[144,1024]{1,0:T(8,128)(2,1)} %get-tuple-element.36) | copy-start | bytes 884740

commit v7 on v6

--- a/solution.py
+++ b/solution.py
@@ -222,10 +222,7 @@
     def __init__(self, net, grad, pair, ring, out, turned=None):
         self.net, self.grad, self.out, self.turned = net, grad, out, turned
         self.sent, self.work = pair
-        self.near_in, self.far_in, self.passed, self.kept, self.came = ring
-        width = grad.shape[-1]
-        cut = max(width // 256, 1) * 128 if width != 384 else 256
-        self.one, self.two = pl.ds(0, cut), pl.ds(cut, width - cut)
+        *self.three, self.kept, self.came = ring
         self.mine = pl.ds(net.core * 4, 4)
         self.q = net.core * 4 + net.y
         self.at_up, self.at_facing, self.at_down = (lax.rem(net.y + k, 4) for k in (1, 2, 3))
@@ -235,32 +232,20 @@
         self.moved = net.copy(self.grad.at[pl.ds((1 - net.core) * 4, 4)], self.sent, net.twin)
 
     def ring(self):
-        net, work, near, far = self.net, self.work, self.near_in, self.far_in
-        one, two = self.one, self.two
+        net, work = self.net, self.work
         self.moved.wait_recv()
         work[...] = add(self.grad[self.mine], self.sent[...]).astype(BF16)
-        self.fars = [
-            net.copy(work.at[self.at_facing, :, one], far.at[:, one], net.up),
-            net.copy(work.at[self.at_facing, :, two], far.at[:, two], net.down),
+        steps = ((self.at_up, net.up), (self.at_down, net.down), (self.at_facing, net.facing))
+        self.nears = [
+            net.copy(work.at[block], there, to) for there, (block, to) in zip(self.three, steps)
         ]
-        self.nears = [
-            net.copy(work.at[self.at_up, :, two], near.at[:, two], net.up),
-            net.copy(work.at[self.at_down, :, one], near.at[:, one], net.down),
-        ]
-
-    def relay(self):
-        net, far = self.net, self.far_in
-        steps = ((self.one, self.at_up, net.up), (self.two, self.at_down, net.down))
-        for k, (part, block, to) in enumerate(steps):
-            self.fars[k].wait_recv()
-            far[:, part] = add(far[:, part], self.work[block, :, part]).astype(BF16)
-            self.nears.append(net.copy(far.at[:, part], self.passed.at[:, part], to))
 
     def beside(self):
         net = self.net
         for made in self.nears:
             made.wait_recv()
-        self.kept[...] = add(self.work[net.y], self.near_in[...], self.passed[...]).astype(BF16)
+        three = [part[...] for part in self.three]
+        self.kept[...] = add(self.work[net.y], *three).astype(BF16)
         self.over = net.copy(self.kept, self.came, net.beside)
 
     def place(self, q, eighths=1):
@@ -296,20 +281,10 @@
                     at = i * D + t * size
                     out[own, at : at + size] = blocks[t][:, i * 128 : i * 128 + size]
         part = out.at[own]
-        self.shared = [net.copy(part, part, net.up), net.copy(part, part, net.down)]
-
-    def back_relay(self):
-        net, out = self.net, self.out
-        half = out.shape[1] // 2
-        self.lasts = []
-        steps = ((0, self.at_down, net.up), (half, self.at_up, net.down))
-        for k, (at, block, to) in enumerate(steps):
-            self.shared[k].wait_recv()
-            part = out.at[self.place(net.core * 4 + block), pl.ds(at, half)]
-            self.lasts.append(net.copy(part, part, to))
+        self.shared = [net.copy(part, part, to) for to in (net.up, net.down, net.facing)]
 
     def swap(self):
-        for made in self.lasts:
+        for made in self.shared:
             made.wait_recv()
         part = self.out.at[self.place(self.net.core * 4, 4)]
         self.ended = self.net.copy(part, part, self.net.twin)
@@ -436,7 +411,6 @@
     vec = [net.copy(vectors, all_vectors.at[s], to) for to in net.peers]
     all_vectors[s] = vectors[...]
     cot[s] = cotangent[...]
-    ag_cot = Gather(net, cot)
     qkv_in, up_in = [], []
     thirds = [
         lambda t, i=i: qkv_weight.at[sixteen, pl.ds(pl.multiple_of(i * D + t * 128, 128), 128)]
@@ -486,6 +460,7 @@
         [query_bias[...].astype(F32), jnp.zeros((1, 128), F32), value_bias[...].astype(F32)], axis=1
     )
     up_bias = up_bias[...].astype(F32)
+    up_bias = jnp.concatenate([up_bias[k : k + 1] for k in range(4)], axis=1)
     qkv_pass.wait_recv()
     ag.row()
 
@@ -497,11 +472,11 @@
         return carry
 
     each(project, 0, 5)
-    ag_cot.relay_one()
     ag.finish()
-    ag_cot.relay_two()
+    ag_cot = Gather(net, cot)
     each(project, 5, 8)
     qkv_low[...] = mixed[...].astype(BF16)
+    ag_cot.relay_one()
 
     def attend(image, carry):
         q, k, v = (qkv_low[image, :, i * 128 : (i + 1) * 128] for i in range(3))
@@ -536,6 +511,7 @@
     each_sent(rs, outward, 0)
     rs.over()
     rs.relay()
+    ag_cot.relay_two()
     resid = tokens[...].astype(F32) + (rs.finish() + bias_out)
     resid_ref[...] = resid
     unit2, inverse2 = norm_unit(resid)
@@ -628,7 +604,6 @@
     ag.relay_two()
     up_tile(1)
     ag.row()
-    down_all.relay()
     up_tile(2)
     up_tile(3)
     up_all.core()
@@ -677,9 +652,6 @@
     net.settle([rs_branch.hopped, *rs_branch.sides, *rs_branch.nears])
     rs = scatter(3)
     qkv_bias_grad = each_sent(rs, back_first, jnp.zeros((1, 384), F32))
-    up_all.relay()
-    rs_out.relay()
-    down_all.back_relay()
     small[4:5, :] = qkv_bias_grad[:, 0:128]
     small[5:6, :] = qkv_bias_grad[:, 256:384]
     small[6:7, :] = jnp.sum(branch[:, :, own].astype(F32).reshape(1152, 128), 0, keepdims=True)
@@ -697,30 +669,23 @@
 
     qkv_tile(0)
     qkv_tile(1)
-    up_all.beside()
     qkv_tile(2)
     qkv_tile(3)
     qkv_all.core()
+    rs_out.relay()
+    up_all.beside()
+    rs.over()
+    qkv_all.ring()
     value = dot_first(attended[...].reshape(1152, 128), branch[...].reshape(1152, D)).astype(BF16)
     for q in range(8):
         out_grad[q] = value[q * 16 : (q + 1) * 16]
     out_all.core()
-    rs.over()
-    qkv_all.ring()
+    rs.relay()
     up_all.cross()
+    down_all.swap()
+    qkv_all.beside()
     out_all.ring()
-    rs.relay()
-    down_all.swap()
-    qkv_all.relay()
-    out_all.relay()
     up_all.back()
-    qkv_all.beside()
-    out_all.beside()
-    block_out[...] = (resid_ref[...] + (rs_out.finish() + bias_down)).astype(BF16)
-    up_all.back_relay()
-    qkv_all.cross()
-    out_all.cross()
-    out_all.back()
     grad_first = rs.finish()
     unit1, inverse1 = norm_unit(tokens[...].astype(F32))
     gain1_grad = jnp.sum(grad_first * unit1, 0, keepdims=True)
@@ -732,12 +697,11 @@
         fours[t] = four[:, t * 128 : (t + 1) * 128]
     moved = [net.copy(fours.at[to["shard"]], fours_in.at[s], to) for to in net.peers]
     fours_in[s] = fours[s]
-    qkv_all.back()
+    qkv_all.cross()
+    out_all.beside()
     input_grad[...] = (
         grad_resid_ref[...] + norm_back(grad_first, unit1, inverse1, gain1)
     ).astype(BF16)
-    out_all.back_relay()
-    up_all.swap()
     for made in moved:
         made.wait_recv()
     total = jnp.sum(fours_in[...].astype(F32), 0)
@@ -745,12 +709,16 @@
     small_low[...] = small[...].astype(BF16)
     moved = [net.copy(small_low, small_ring.at[net.r], to) for to in net.replicas]
     small_ring[net.r] = small_low[...]
-    qkv_all.back_relay()
-    out_all.swap()
+    qkv_all.back()
+    out_all.cross()
+    out_all.back()
+    up_all.swap()
+    block_out[...] = (resid_ref[...] + (rs_out.finish() + bias_down)).astype(BF16)
     for made in moved:
         made.wait_recv()
     small_sum[...] = add(*(small_ring[k] for k in range(16)))
     qkv_all.swap()
+    out_all.swap()
     for every in (down_all, out_all, up_all, qkv_all):
         every.end()
     net.drain()
@@ -843,7 +811,7 @@
 
 
 def cast(down, out, up, qkv, small):
-    steps = 8
+    steps = 1
     block = lambda a: pl.BlockSpec((a.shape[0] // steps, a.shape[1]), lambda i: (i, 0))
     whole = lambda *sizes: pl.BlockSpec(sizes, lambda i: (0,) * len(sizes))
     shape = lambda *sizes: jax.ShapeDtypeStruct(sizes, F32)
@@ -885,7 +853,7 @@
     block_out, input_grad, *sums = layer(
         tokens.reshape(ROWS, D),
         cotangent.reshape(ROWS, D),
-        *(a.reshape(1, -1) for a in vectors),
+        *(a.reshape(-1, 128) for a in vectors),
         qkv_weight,
         up_weight,
         out_weight,

time: 208 us -> 197 us (0.947)
  Pallas kernels: 204 us -> 195 us
    pallas_call x1, Pallas kernels: 197 us -> 190 us  [layer(): pl.pallas_call(layer_kernel, out_shape=[shape(ROWS, D), shape(ROWS, D), s...]
    pallas_call x1, Pallas kernels: 7.08 us -> 4.7 us  [cast(): pl.pallas_call(cast_kernel, grid=(steps,), out_shape=[*(shape(*a.shape) f...]
where the time goes in v7:
time: 197 us
  Pallas kernels  195 us (99%)
    pallas_call x1, Pallas kernels, layer(): pl.pallas_call(layer_kernel, out_shape=[shape(ROWS, D), shape(ROWS, D), s...  190 us
    pallas_call x1, Pallas kernels, cast(): pl.pallas_call(cast_kernel, grid=(steps,), out_shape=[*(shape(*a.shape) f...  4.7 us

profile of v7, /device:TPU:1, one launch (start us, length us, event | category | flops | bytes accessed | tf_op | source)
XLA Modules:
  0.0 197.0 jit_solution(1039189876136058287)
XLA Ops:
  0.7 190.2 %layer.1 = (bf16[144,1024]{1,0:T(8,128)(2,1)}, bf16[144,1024]{1,0:T(8,128)(2,1)}, bf16[512,1024]{1,0:T(8,128)(2,1)}, bf16[128,1024]{1,0:T(8,128)(2,1)}, bf16[128...) custom-call(bf16[144,1024]{1,0:T(8,128)(2,1)} %bitcast.15, bf16[144,1024]{1,0:T(8,128)(2,1)} %bitcast.16, ...), custom_call_target="tpu_custom_call" | custom-call | flops 11000000512 | bytes 12000000 | tf_op jit(solution)/shard_map/layer/pallas_call | solution.py:732
  190.8 0.0 copy-start.1
  190.8 0.0 copy-start
  190.8 4.7 %cast.1 = (f32[512,1024]{1,0:T(8,128)}, f32[128,1024]{1,0:T(8,128)}, f32[128,4096]{1,0:T(8,128)}, f32[128,3072]{1,0:T(8,128)}, f32[128]{0:T(128)}, /*index=5*/f3...) custom-call(bf16[512,1024]{1,0:T(8,128)(2,1)} %get-tuple-element.37., ...), custom_call_target="tpu_custom_call" | custom-call | tf_op jit(solution)/shard_map/cast/pallas_call | solution.py:819
  195.5 0.0 copy-done.1
  195.5 0.7 copy.32
  196.3 0.0 copy-done
  196.3 0.7 copy.33
Async XLA Ops:
  190.8 4.7 %copy-start.1 = (bf16[144,1024]{1,0:T(8,128)(2,1)S(1)}, bf16[144,1024]{1,0:T(8,128)(2,1)}, u32[]{:S(2)}) copy-start(bf16[144,1024]{1,0:T(8,128)(2,1)} %get-tuple-element.35) | copy-start | bytes 884740
  190.8 5.4 %copy-start = (bf16[144,1024]{1,0:T(8,128)(2,1)S(1)}, bf16[144,1024]{1,0:T(8,128)(2,1)}, u32[]{:S(2)}) copy-start(bf16[144,1024]{1,0:T(8,128)(2,1)} %get-tuple-element.36) | copy-start | bytes 884740

commit v8 on v7

--- a/solution.py
+++ b/solution.py
@@ -306,8 +306,8 @@
     up_bias,
     qkv_weight,
     up_weight,
-    out_weight,
-    down_weight,
+    out_source,
+    down_source,
     block_out,
     input_grad,
     down_sum,
@@ -360,6 +360,9 @@
     qkv_pair,
     qkv_ring,
     qkv_turned,
+    out_weight,
+    down_weight,
+    load,
     send,
     recv,
 ):
@@ -393,7 +396,7 @@
 
         return lax.fori_loop(least, end, step, carry)
 
-    def each_sent(rs, work, carry):
+    def each_sent(rs, work, carry, beside=None):
         carry = each(work, 5, 6, carry)
         rs.hop()
         carry = each(work, 6, 8, carry)
@@ -401,8 +404,13 @@
         carry = each(work, 1, 3, carry)
         rs.near()
         carry = each(work, 3, 5, carry)
+        if beside is None:
+            rs.far()
+            return each(work, 0, 1, carry)
+        carry = each(work, 0, 1, carry)
+        beside()
         rs.far()
-        return each(work, 0, 1, carry)
+        return carry
 
     wide_vectors[...] = jnp.zeros_like(wide_vectors)
     for k, single in enumerate(singles):
@@ -424,9 +432,17 @@
     for to in net.peers:
         there = columns.at[s, sixteen, pl.ds(384, 512)]
         up_in.append(net.copy(quarter(to["shard"]), there, to))
-    for i in range(3):
-        columns[s, sixteen, i * 128 : (i + 1) * 128] = thirds[i](s)[...]
-    columns[s, sixteen, 384:896] = quarter(s)[...]
+    loads = [
+        (thirds[i](s), columns.at[s, sixteen, pl.ds(i * 128, 128)]) for i in range(3)
+    ]
+    loads += [
+        (quarter(s), columns.at[s, sixteen, pl.ds(384, 512)]),
+        (out_source, out_weight),
+        (down_source, down_weight),
+    ]
+    loads = [pltpu.make_async_copy(*pair, load.at[i]) for i, pair in enumerate(loads)]
+    for made in loads:
+        made.start()
 
     def share(arrived, at):
         for made in arrived:
@@ -451,6 +467,8 @@
     first[s] = (unit1 * gain1 + shift1).astype(BF16)
     ag = Gather(net, first)
     qkv_at, up_at = pl.ds(0, 384), pl.ds(384, 512)
+    for made in loads[:4]:
+        made.wait()
     qkv_in = share(qkv_in, qkv_at)
     ag.relay_one()
     up_in = share(up_in, up_at)
@@ -507,6 +525,8 @@
         parts[0, b] = dot(value, out_weight[...]).astype(BF16)
         return carry
 
+    for made in loads[4:]:
+        made.wait()
     rs = rs_branch = scatter(0)
     each_sent(rs, outward, 0)
     rs.over()
@@ -637,24 +657,16 @@
 
     lax.fori_loop(0, 1, attend_back, 0)
     up_all.ring()
+    lax.fori_loop(1, 2, attend_back, 0)
     rs_out.far()
     down_all.cross()
     down_all.back()
-    lax.fori_loop(1, 2, attend_back, 0)
-    rs_out.over()
 
     def back_first(b, total):
         value = by_device(mixed, b)
         grad_qkv[b] = value
         parts[0, b] = dot_last(value, columns[:, :, 0:384].reshape(D, 384)).astype(BF16)
         return total + jnp.sum(value.astype(F32), 0, keepdims=True)
-
-    net.settle([rs_branch.hopped, *rs_branch.sides, *rs_branch.nears])
-    rs = scatter(3)
-    qkv_bias_grad = each_sent(rs, back_first, jnp.zeros((1, 384), F32))
-    small[4:5, :] = qkv_bias_grad[:, 0:128]
-    small[5:6, :] = qkv_bias_grad[:, 256:384]
-    small[6:7, :] = jnp.sum(branch[:, :, own].astype(F32).reshape(1152, 128), 0, keepdims=True)
 
     def qkv_tile(i):
         value = dot_first(
@@ -667,12 +679,21 @@
                     j * 128 + q * 16 : j * 128 + (q + 1) * 16
                 ]
 
-    qkv_tile(0)
-    qkv_tile(1)
+    def two_tiles():
+        qkv_tile(0)
+        qkv_tile(1)
+
+    net.settle([rs_branch.hopped, *rs_branch.sides, *rs_branch.nears])
+    rs = scatter(3)
+    qkv_bias_grad = each_sent(rs, back_first, jnp.zeros((1, 384), F32), two_tiles)
+    small[4:5, :] = qkv_bias_grad[:, 0:128]
+    small[5:6, :] = qkv_bias_grad[:, 256:384]
+    small[6:7, :] = jnp.sum(branch[:, :, own].astype(F32).reshape(1152, 128), 0, keepdims=True)
+
     qkv_tile(2)
     qkv_tile(3)
     qkv_all.core()
-    rs_out.relay()
+    rs_out.over()
     up_all.beside()
     rs.over()
     qkv_all.ring()
@@ -680,6 +701,7 @@
     for q in range(8):
         out_grad[q] = value[q * 16 : (q + 1) * 16]
     out_all.core()
+    rs_out.relay()
     rs.relay()
     up_all.cross()
     down_all.swap()
@@ -740,7 +762,7 @@
             shape(128, 3 * D),
             jax.ShapeDtypeStruct((16, 128), F32),
         ],
-        in_specs=[space] * 15,
+        in_specs=[space] * 11 + [pl.BlockSpec(memory_space=pl.ANY)] * 4,
         out_specs=[space] * 7,
         scratch_shapes=[
             vmem(8, 64, D),
@@ -788,6 +810,9 @@
             vmem(2, 4, 128, 384),
             vmem(5, 128, 384),
             vmem(2, 8, 16, 384),
+            vmem(128, D),
+            vmem(512, D),
+            pltpu.SemaphoreType.DMA((6,)),
             pltpu.SemaphoreType.DMA((240,)),
             pltpu.SemaphoreType.DMA((240,)),
         ],
@@ -801,34 +826,33 @@
     )(*arguments)
 
 
-def cast_kernel(down, out, up, qkv, small, *outs):
-    for source, target in zip((down, out, up, qkv), outs[:4]):
+def cast_kernel(block, grad, down, out, up, qkv, small, *outs):
+    for source, target in zip((block, grad), outs[:2]):
+        target[...] = source[...].astype(F32).reshape(2, 72, D).astype(BF16)
+    for source, target in zip((down, out, up, qkv), outs[2:6]):
         target[...] = source[...].astype(F32)
-    for k, target in enumerate(outs[4:12]):
+    for k, target in enumerate(outs[6:14]):
         target[...] = small[k]
     for k in range(4):
-        outs[12][k * 128 : (k + 1) * 128] = small[8 + k]
-
-
-def cast(down, out, up, qkv, small):
-    steps = 1
-    block = lambda a: pl.BlockSpec((a.shape[0] // steps, a.shape[1]), lambda i: (i, 0))
-    whole = lambda *sizes: pl.BlockSpec(sizes, lambda i: (0,) * len(sizes))
+        outs[14][k * 128 : (k + 1) * 128] = small[8 + k]
+
+
+def cast(*arrays):
+    space = pl.BlockSpec(memory_space=pltpu.VMEM)
     shape = lambda *sizes: jax.ShapeDtypeStruct(sizes, F32)
-    large = (down, out, up, qkv)
     return pl.pallas_call(
         cast_kernel,
-        grid=(steps,),
         out_shape=[
-            *(shape(*a.shape) for a in large),
+            *(jax.ShapeDtypeStruct((2, 72, D), BF16) for _ in range(2)),
+            *(shape(*a.shape) for a in arrays[2:6]),
             *(shape(128) for _ in range(8)),
             shape(512),
         ],
-        in_specs=[*map(block, large), whole(16, 128)],
-        out_specs=[*map(block, large), *(whole(128) for _ in range(8)), whole(512)],
+        in_specs=[space] * 7,
+        out_specs=[space] * 15,
         name="cast",
         compiler_params=pltpu.CompilerParams(vmem_limit_bytes=62 << 20),
-    )(*large, small)
+    )(*arrays)
 
 
 def body(
@@ -850,7 +874,7 @@
 ):
     vectors = (attn_gain, attn_shift, mlp_gain, mlp_shift, out_bias, down_bias)
     vectors = (*vectors, query_bias, value_bias, up_bias)
-    block_out, input_grad, *sums = layer(
+    sums = layer(
         tokens.reshape(ROWS, D),
         cotangent.reshape(ROWS, D),
         *(a.reshape(-1, 128) for a in vectors),
@@ -859,10 +883,11 @@
         out_weight,
         down_weight,
     )
-    down_grad, out_grad, up_grad, qkv_grad, *small, up_bias_grad = cast(*sums)
+    block_out, input_grad, down_grad, out_grad, up_grad, qkv_grad, *small = cast(*sums)
+    up_bias_grad = small.pop()
     return (
-        block_out.reshape(2, 72, D),
-        input_grad.reshape(2, 72, D),
+        block_out,
+        input_grad,
         small[0],
         small[1],
         qkv_grad,

time: 197 us -> 189 us (0.959)
  Pallas kernels: 195 us -> 188 us
    pallas_call x1, Pallas kernels: 190 us -> 183 us  [layer(): pl.pallas_call(layer_kernel, out_shape=[shape(ROWS, D), shape(ROWS, D), s...]
where the time goes in v8:
time: 189 us
  Pallas kernels  188 us (99%)
    pallas_call x1, Pallas kernels, layer(): pl.pallas_call(layer_kernel, out_shape=[shape(ROWS, D), shape(ROWS, D), s...  183 us
    pallas_call x1, Pallas kernels, cast(): pl.pallas_call(cast_kernel, out_shape=[*(jax.ShapeDtypeStruct((2, 72, D),...  5.03 us

profile of v8, /device:TPU:1, one launch (start us, length us, event | category | flops | bytes accessed | tf_op | source)
XLA Modules:
  0.0 188.9 jit_solution(11802711715996420328)
XLA Ops:
  0.7 183.0 %layer.1 = (bf16[144,1024]{1,0:T(8,128)(2,1)}, bf16[144,1024]{1,0:T(8,128)(2,1)}, bf16[512,1024]{1,0:T(8,128)(2,1)}, bf16[128,1024]{1,0:T(8,128)(2,1)}, bf16[128...) custom-call(bf16[144,1024]{1,0:T(8,128)(2,1)} %bitcast.11, bf16[144,1024]{1,0:T(8,128)(2,1)} %bitcast.12, ...), custom_call_target="tpu_custom_call" | custom-call | flops 11000000512 | bytes 12000000 | tf_op jit(solution)/shard_map/layer/pallas_call | solution.py:754
  183.7 5.0 %cast.1 = (bf16[2,72,1024]{2,1,0:T(8,128)(2,1)}, bf16[2,72,1024]{2,1,0:T(8,128)(2,1)}, f32[512,1024]{1,0:T(8,128)}, f32[128,1024]{1,0:T(8,128)}, f32[128,4096]{1...) custom-call(bf16[144,1024]{1,0:T(8,128)(2,1)} %get-tuple-element.37., ...), custom_call_target="tpu_custom_call" | custom-call | tf_op jit(solution)/shard_map/cast/pallas_call | solution.py:843

commit v9 on v8

--- a/solution.py
+++ b/solution.py
@@ -412,6 +412,10 @@
         rs.far()
         return carry
 
+    parts[1, s] = tokens[...]
+    raw = parts.at[1]
+    ag_raw = Gather(net, raw)
+
     wide_vectors[...] = jnp.zeros_like(wide_vectors)
     for k, single in enumerate(singles):
         wide_vectors[k : k + 1, :] = single[...].astype(F32)
@@ -456,23 +460,19 @@
         part = columns.at[:, mine, at]
         return net.copy(part, part, net.twin)
 
-    x = tokens[...].astype(F32)
-    unit1, inverse1 = norm_unit(x)
+    qkv_at, up_at = pl.ds(0, 384), pl.ds(384, 512)
+    for made in loads[:4]:
+        made.wait()
+    ag_raw.relay_one()
+    qkv_in = share(qkv_in, qkv_at)
+    ag_raw.relay_two()
+    up_in = share(up_in, up_at)
     for made in vec:
         made.wait_recv()
     table = [all_vectors[j].astype(F32) for j in range(8)]
     gain1, shift1, gain2, shift2, bias_out, bias_down = (
         jnp.concatenate([t[i : i + 1] for t in table], axis=1) for i in range(6)
     )
-    first[s] = (unit1 * gain1 + shift1).astype(BF16)
-    ag = Gather(net, first)
-    qkv_at, up_at = pl.ds(0, 384), pl.ds(384, 512)
-    for made in loads[:4]:
-        made.wait()
-    qkv_in = share(qkv_in, qkv_at)
-    ag.relay_one()
-    up_in = share(up_in, up_at)
-    ag.relay_two()
     qkv_pass = share_twin(qkv_in, qkv_at)
     qkv_bias = jnp.concatenate(
         [query_bias[...].astype(F32), jnp.zeros((1, 128), F32), value_bias[...].astype(F32)], axis=1
@@ -480,9 +480,11 @@
     up_bias = up_bias[...].astype(F32)
     up_bias = jnp.concatenate([up_bias[k : k + 1] for k in range(4)], axis=1)
     qkv_pass.wait_recv()
-    ag.row()
+    ag_raw.row()
 
     def project(b, carry):
+        unit, _ = norm_unit(raw[b].astype(F32))
+        first[b] = (unit * gain1 + shift1).astype(BF16)
         value = dot(first[b], columns[:, :, 0:384].reshape(D, 384)) + qkv_bias
         at = pl.multiple_of(b * 72, 8)
         mixed[0, pl.ds(at, 72), :] = value[0:72]
@@ -490,7 +492,7 @@
         return carry
 
     each(project, 0, 5)
-    ag.finish()
+    ag_raw.finish()
     ag_cot = Gather(net, cot)
     each(project, 5, 8)
     qkv_low[...] = mixed[...].astype(BF16)
@@ -558,6 +560,7 @@
     ag.relay_one()
     ag_cot.row()
     ag_cot.finish()
+    net.settle([ag_raw.a, ag_raw.b, ag_raw.z, *ag_raw.more, ag_raw.c, ag_raw.d, *ag_raw.rest])
     up_bias_grad = each(feed, 0, 1, jnp.zeros((1, 512), F32))
     ag.relay_two()
     ag.row()
@@ -659,8 +662,6 @@
     up_all.ring()
     lax.fori_loop(1, 2, attend_back, 0)
     rs_out.far()
-    down_all.cross()
-    down_all.back()
 
     def back_first(b, total):
         value = by_device(mixed, b)
@@ -681,6 +682,8 @@
 
     def two_tiles():
         qkv_tile(0)
+        down_all.cross()
+        down_all.back()
         qkv_tile(1)
 
     net.settle([rs_branch.hopped, *rs_branch.sides, *rs_branch.nears])
@@ -826,33 +829,48 @@
     )(*arguments)
 
 
-def cast_kernel(block, grad, down, out, up, qkv, small, *outs):
-    for source, target in zip((block, grad), outs[:2]):
-        target[...] = source[...].astype(F32).reshape(2, 72, D).astype(BF16)
-    for source, target in zip((down, out, up, qkv), outs[2:6]):
-        target[...] = source[...].astype(F32)
-    for k, target in enumerate(outs[6:14]):
-        target[...] = small[k]
+def cast_kernel(*refs):
+    large, small, refs = refs[:6], refs[6], refs[7:]
+    outs, little, refs = refs[:6], refs[6:15], refs[15:]
+    held, wide, (load, store) = refs[:6], refs[6:12], refs[12:]
+    loads = [pltpu.make_async_copy(*pair, load.at[i]) for i, pair in enumerate(zip(large, held))]
+    stores = [pltpu.make_async_copy(*pair, store.at[i]) for i, pair in enumerate(zip(wide, outs))]
+    for made in loads:
+        made.start()
+    for i in range(6):
+        loads[i].wait()
+        value = held[i][...].astype(F32)
+        wide[i][...] = value if i < 4 else value.reshape(2, 72, D).astype(BF16)
+        stores[i].start()
+    for k in range(8):
+        little[k][...] = small[k]
     for k in range(4):
-        outs[14][k * 128 : (k + 1) * 128] = small[8 + k]
-
-
-def cast(*arrays):
+        little[8][k * 128 : (k + 1) * 128] = small[8 + k]
+    for made in stores:
+        made.wait()
+
+
+def cast(block, grad, *arrays):
     space = pl.BlockSpec(memory_space=pltpu.VMEM)
+    far = pl.BlockSpec(memory_space=pl.ANY)
     shape = lambda *sizes: jax.ShapeDtypeStruct(sizes, F32)
+    *grads, small = arrays
+    results = [shape(*a.shape) for a in grads] + [jax.ShapeDtypeStruct((2, 72, D), BF16)] * 2
+    large = (*grads, block, grad)
     return pl.pallas_call(
         cast_kernel,
-        out_shape=[
-            *(jax.ShapeDtypeStruct((2, 72, D), BF16) for _ in range(2)),
-            *(shape(*a.shape) for a in arrays[2:6]),
-            *(shape(128) for _ in range(8)),
-            shape(512),
+        out_shape=[*results, *(shape(128) for _ in range(8)), shape(512)],
+        in_specs=[far] * 6 + [space],
+        out_specs=[far] * 6 + [space] * 9,
+        scratch_shapes=[
+            *(pltpu.VMEM(a.shape, a.dtype) for a in large),
+            *(pltpu.VMEM(a.shape, a.dtype) for a in results),
+            pltpu.SemaphoreType.DMA((6,)),
+            pltpu.SemaphoreType.DMA((6,)),
         ],
-        in_specs=[space] * 7,
-        out_specs=[space] * 15,
         name="cast",
         compiler_params=pltpu.CompilerParams(vmem_limit_bytes=62 << 20),
-    )(*arrays)
+    )(*large, small)
 
 
 def body(
@@ -883,7 +901,7 @@
         out_weight,
         down_weight,
     )
-    block_out, input_grad, down_grad, out_grad, up_grad, qkv_grad, *small = cast(*sums)
+    down_grad, out_grad, up_grad, qkv_grad, block_out, input_grad, *small = cast(*sums)
     up_bias_grad = small.pop()
     return (
         block_out,

time: 189 us -> 194 us (1.026)
  Pallas kernels: 188 us -> 193 us
    pallas_call x1, Pallas kernels: 183 us -> 187 us  [layer(): pl.pallas_call(layer_kernel, out_shape=[shape(ROWS, D), shape(ROWS, D), s...]
where the time goes in v9:
time: 194 us; the launch traced here: 193 us
  Pallas kernels  193 us (99%)
    pallas_call x1, Pallas kernels, layer(): pl.pallas_call(layer_kernel, out_shape=[shape(ROWS, D), shape(ROWS, D), s...  187 us
    pallas_call x1, Pallas kernels, cast(): pl.pallas_call(cast_kernel, out_shape=[*results, *(shape(128) for _ in ra...  5.61 us

profile of v9, /device:TPU:1, one launch (start us, length us, event | category | flops | bytes accessed | tf_op | source)
XLA Modules:
  0.0 193.4 jit_solution(812047317909413320)
XLA Ops:
  0.7 186.9 %layer.1 = (bf16[144,1024]{1,0:T(8,128)(2,1)}, bf16[144,1024]{1,0:T(8,128)(2,1)}, bf16[512,1024]{1,0:T(8,128)(2,1)}, bf16[128,1024]{1,0:T(8,128)(2,1)}, bf16[128...) custom-call(bf16[144,1024]{1,0:T(8,128)(2,1)} %bitcast.11, bf16[144,1024]{1,0:T(8,128)(2,1)} %bitcast.12, ...), custom_call_target="tpu_custom_call" | custom-call | flops 11000000512 | bytes 12000000 | tf_op jit(solution)/shard_map/layer/pallas_call | solution.py:757
  187.6 5.6 %cast.1 = (f32[512,1024]{1,0:T(8,128)}, f32[128,1024]{1,0:T(8,128)}, f32[128,4096]{1,0:T(8,128)}, f32[128,3072]{1,0:T(8,128)}, bf16[2,72,1024]{2,1,0:T(8,128)(2,...) custom-call(bf16[512,1024]{1,0:T(8,128)(2,1)} %get-tuple-element.37., ...), custom_call_target="tpu_custom_call" | custom-call | tf_op jit(solution)/shard_map/cast/pallas_call | solution.py:860

commit v10 on v8

--- a/solution.py
+++ b/solution.py
@@ -337,6 +337,7 @@
     grad_qkv,
     resid_ref,
     grad_resid_ref,
+    unit_ref,
     small,
     fours,
     fours_in,
@@ -591,8 +592,10 @@
     down_tile(2)
     down_tile(3)
     down_all.core()
+    unit2, inverse2 = norm_unit(resid_ref[...])
+    unit_ref[...] = unit2
     grad_second = rs.finish()
-    unit2, inverse2 = norm_unit(resid_ref[...])
+    unit2 = unit_ref[...]
     grad_resid = cotangent[...].astype(F32) + norm_back(grad_second, unit2, inverse2, gain2)
     grad_resid_ref[...] = grad_resid
     branch[s] = grad_resid.astype(BF16)
@@ -659,8 +662,6 @@
     up_all.ring()
     lax.fori_loop(1, 2, attend_back, 0)
     rs_out.far()
-    down_all.cross()
-    down_all.back()
 
     def back_first(b, total):
         value = by_device(mixed, b)
@@ -681,6 +682,8 @@
 
     def two_tiles():
         qkv_tile(0)
+        down_all.cross()
+        down_all.back()
         qkv_tile(1)
 
     net.settle([rs_branch.hopped, *rs_branch.sides, *rs_branch.nears])
@@ -708,8 +711,10 @@
     qkv_all.beside()
     out_all.ring()
     up_all.back()
+    unit1, inverse1 = norm_unit(tokens[...].astype(F32))
+    unit_ref[...] = unit1
     grad_first = rs.finish()
-    unit1, inverse1 = norm_unit(tokens[...].astype(F32))
+    unit1 = unit_ref[...]
     gain1_grad = jnp.sum(grad_first * unit1, 0, keepdims=True)
     shift1_grad = jnp.sum(grad_first, 0, keepdims=True)
     four = jnp.concatenate(
@@ -785,6 +790,7 @@
             vmem(8, ROWS, 512),
             vmem(8, ROWS, 512),
             vmem(8, ROWS, 384),
+            wide(ROWS, D),
             wide(ROWS, D),
             wide(ROWS, D),
             wide(16, 128),

time: 189 us -> 189 us (level)
  no operation moved by 1% of the time
where the time goes in v10:
time: 189 us
  Pallas kernels  188 us (99%)
    pallas_call x1, Pallas kernels, layer(): pl.pallas_call(layer_kernel, out_shape=[shape(ROWS, D), shape(ROWS, D), s...  183 us
    pallas_call x1, Pallas kernels, cast(): pl.pallas_call(cast_kernel, out_shape=[*(jax.ShapeDtypeStruct((2, 72, D),...  5.03 us

profile of v10, /device:TPU:1, one launch (start us, length us, event | category | flops | bytes accessed | tf_op | source)
XLA Modules:
  0.0 188.6 jit_solution(8051107210923688975)
XLA Ops:
  0.7 182.7 %layer.1 = (bf16[144,1024]{1,0:T(8,128)(2,1)}, bf16[144,1024]{1,0:T(8,128)(2,1)}, bf16[512,1024]{1,0:T(8,128)(2,1)}, bf16[128,1024]{1,0:T(8,128)(2,1)}, bf16[128...) custom-call(bf16[144,1024]{1,0:T(8,128)(2,1)} %bitcast.11, bf16[144,1024]{1,0:T(8,128)(2,1)} %bitcast.12, ...), custom_call_target="tpu_custom_call" | custom-call | flops 11000000512 | bytes 12000000 | tf_op jit(solution)/shard_map/layer/pallas_call | solution.py:759
  183.4 5.0 %cast.1 = (bf16[2,72,1024]{2,1,0:T(8,128)(2,1)}, bf16[2,72,1024]{2,1,0:T(8,128)(2,1)}, f32[512,1024]{1,0:T(8,128)}, f32[128,1024]{1,0:T(8,128)}, f32[128,4096]{1...) custom-call(bf16[144,1024]{1,0:T(8,128)(2,1)} %get-tuple-element.37., ...), custom_call_target="tpu_custom_call" | custom-call | tf_op jit(solution)/shard_map/cast/pallas_call | solution.py:849

commit v11 on v10

--- a/solution.py
+++ b/solution.py
@@ -133,17 +133,17 @@
     def relay_two(self):
         net = self.net
         self.z.wait_recv()
-        part = self.whole.at[net.at(1 - net.h, net.x)]
+        part = self.whole.at[net.at(1 - net.h, net.x), :, pl.ds(128, D - 128)]
         self.rest = [net.copy(part, part, net.right), net.copy(part, part, net.left)]
+        for made, k in zip(self.more, (3, 1)):
+            made.wait_recv()
+            part = self.whole.at[net.at(net.h, net.x + k), :, pl.ds(0, 128)]
+            self.rest.append(net.copy(part, part, net.across))
         block = net.at(net.h, net.x + 2)
         self.c.wait_recv()
         self.rest.append(self.piece(block, 0, net.across))
         self.d.wait_recv()
         self.rest.append(self.piece(block, 1, net.across))
-
-    def row(self):
-        for made in self.more:
-            made.wait_recv()
 
     def finish(self):
         for made in self.rest:
@@ -481,7 +481,6 @@
     up_bias = up_bias[...].astype(F32)
     up_bias = jnp.concatenate([up_bias[k : k + 1] for k in range(4)], axis=1)
     qkv_pass.wait_recv()
-    ag.row()
 
     def project(b, carry):
         value = dot(first[b], columns[:, :, 0:384].reshape(D, 384)) + qkv_bias
@@ -557,11 +556,9 @@
         return total + jnp.sum(gu.astype(F32), 0, keepdims=True)
 
     ag.relay_one()
-    ag_cot.row()
     ag_cot.finish()
     up_bias_grad = each(feed, 0, 1, jnp.zeros((1, 512), F32))
     ag.relay_two()
-    ag.row()
     up_bias_grad = each(feed, 1, 5, up_bias_grad)
     ag.finish()
     rs = scatter(1)
@@ -626,7 +623,6 @@
     up_tile(0)
     ag.relay_two()
     up_tile(1)
-    ag.row()
     up_tile(2)
     up_tile(3)
     up_all.core()

time: 189 us -> 187 us (0.989)
  Pallas kernels: 188 us -> 186 us
where the time goes in v11:
time: 187 us
  Pallas kernels  186 us (99%)
    pallas_call x1, Pallas kernels, layer(): pl.pallas_call(layer_kernel, out_shape=[shape(ROWS, D), shape(ROWS, D), s...  181 us
    pallas_call x1, Pallas kernels, cast(): pl.pallas_call(cast_kernel, out_shape=[*(jax.ShapeDtypeStruct((2, 72, D),...  5.03 us

profile of v11, /device:TPU:1, one launch (start us, length us, event | category | flops | bytes accessed | tf_op | source)
XLA Modules:
  0.0 186.9 jit_solution(17884581676446543801)
XLA Ops:
  0.7 181.0 %layer.1 = (bf16[144,1024]{1,0:T(8,128)(2,1)}, bf16[144,1024]{1,0:T(8,128)(2,1)}, bf16[512,1024]{1,0:T(8,128)(2,1)}, bf16[128,1024]{1,0:T(8,128)(2,1)}, bf16[128...) custom-call(bf16[144,1024]{1,0:T(8,128)(2,1)} %bitcast.11, bf16[144,1024]{1,0:T(8,128)(2,1)} %bitcast.12, ...), custom_call_target="tpu_custom_call" | custom-call | flops 11000000512 | bytes 12000000 | tf_op jit(solution)/shard_map/layer/pallas_call | solution.py:755
  181.7 5.0 %cast.1 = (bf16[2,72,1024]{2,1,0:T(8,128)(2,1)}, bf16[2,72,1024]{2,1,0:T(8,128)(2,1)}, f32[512,1024]{1,0:T(8,128)}, f32[128,1024]{1,0:T(8,128)}, f32[128,4096]{1...) custom-call(bf16[144,1024]{1,0:T(8,128)(2,1)} %get-tuple-element.37., ...), custom_call_target="tpu_custom_call" | custom-call | tf_op jit(solution)/shard_map/cast/pallas_call | solution.py:845
